TPU v7x, 128 devices: a whole 4x4x4 slice. The times are simulated.
128 devices in a mesh: space: 8 (over y, core), mode: 16 (over x, z).
Axes of the slice: x: 4, y: 4, z: 4, core: 2. Of those that a mesh axis runs over, the one named last changes fastest.
Arguments:
- intensity: float32 [1024, 8, 128, 256], P('mode', None, 'space'), may hold values from 0.1 to 2
- dir_cos: float32 [3, 32], replicated, may hold values from -1 to 1, as said below
- velocity: float32 [32], replicated, may hold values from 0.2 to 1
- rate: float32 [32], replicated, may hold values from 0.05 to 2
- spectrum: float32 [32], replicated, may hold values from 0.2 to 2
- weight: float32 [32], replicated, may hold values from 0.25 to 1.75
- heat: float32 [128, 256], P('space'), may hold values from 0.5 to 4
- rough_cells: int32 [8192], P('space'), may hold values from 0 to 4095, as said below
- rough_count: int32 [8], P('space'), may hold values from 256 to 1024, as said below
- rough_map: int32 [8192, 16], P('space'), may hold values from 0 to 15
Outputs:
- intensity_new: float32 [1024, 8, 128, 256], P('mode', None, 'space')
- energy_new: float32 [8, 128, 256], P(None, 'space')
Inputs may be any that keep to these rules, and one draw needn't show every extreme that they name: `dir_cos`: even directions have a positive third cosine, and direction 2k+1 equals direction 2k with the third cosine negated; every direction has a third cosine of magnitude 0.3 or more. `rough_cells`: the entries of one index of space are distinct. `rough_count`: some index of space has all 1024 slots live.
All inputs are finite; a program needn't handle non-finite values.
Results may differ from a plain program's by a relative error of at most 0.0015.
Values sent between devices are 32-bit elements; how exact they have to be, the bound alone decides.
No kernel may reach another device: no remote copies, remote signals or barrier semaphores. Data moves between devices by JAX's collectives and lax.ppermute only.
A program may use at most 128 MiB of HBM per device.

v0:
```python
import jax
import jax.numpy as jnp
from jax import lax
from jax.sharding import PartitionSpec as P

PAIRS = 1024


def extended(block, sides, width):
    for axis, dim in sides:
        count = lax.axis_size(axis)
        forward = [(i, i + 1) for i in range(count - 1)]
        backward = [(target, source) for source, target in forward]
        low = lax.ppermute(
            lax.slice_in_dim(block, block.shape[dim] - width, None, axis=dim), axis, forward
        )
        high = lax.ppermute(lax.slice_in_dim(block, 0, width, axis=dim), axis, backward)
        block = jnp.concatenate([low, block, high], axis=dim)
    return block


def squash(energy):
    return energy / (1.0 + 0.3 * jnp.abs(energy))


def per_device(
    intensity, dir_cos, velocity, rate, spectrum, weight, heat, rough_cells, rough_count, rough_map
):
    pairs_local = intensity.shape[0]
    modes = velocity.shape[0]
    planes_count, rows, width = (intensity.shape[1], intensity.shape[2], intensity.shape[3])
    dirs_local = pairs_local // modes
    half = dirs_local // 2
    position = lax.axis_index("mode")
    cos_local = lax.dynamic_slice_in_dim(dir_cos, position * dirs_local, dirs_local, 1)
    weight_local = lax.dynamic_slice_in_dim(weight, position * dirs_local, dirs_local, 0)
    field = intensity.reshape(dirs_local, modes, planes_count, rows, width)
    partial_value = jnp.einsum("s,smzxy->zxy", weight_local, field)
    energy = lax.psum(partial_value, "mode") / PAIRS
    equil = squash(energy)
    padded = extended(field, (("space", 3),), 1)
    ox = cos_local[0][:, None, None, None, None]
    oy = cos_local[1][:, None, None, None, None]
    speed = velocity[None, :, None, None, None]
    pady = jnp.pad(field, ((0, 0), (0, 0), (0, 0), (0, 0), (1, 1)))
    along = jnp.maximum(ox, 0.0) * (field - padded[:, :, :, :-2]) + jnp.minimum(ox, 0.0) * (
        padded[:, :, :, 2:] - field
    )
    across = jnp.maximum(oy, 0.0) * (field - pady[..., :-2]) + jnp.minimum(oy, 0.0) * (
        pady[..., 2:] - field
    )
    source = (rate * spectrum)[:, None, None, None] * equil[None]
    rhs = field + source[None] - speed * (along + across)
    diag = 1.0 + rate
    couple = velocity[None, :] * jnp.abs(cos_local[2])[:, None]
    cdown = couple[1::2][:, :, None, None]
    adown = diag[None, :, None, None] + cdown
    down_rhs = rhs[1::2]
    carry = spectrum[None, :, None, None] * heat[None, None]
    planes = [None] * planes_count
    for level in reversed(range(planes_count)):
        carry = (down_rhs[:, :, level] + cdown * carry) / adown
        planes[level] = carry
    down_new = jnp.stack(planes, axis=2)
    bottom = down_new[:, :, 0].reshape(half, modes, rows * width)
    slots = rough_cells.shape[0]
    live = jnp.arange(slots, dtype=jnp.int32) < rough_count[0]
    everything = lax.all_gather(bottom, "mode", axis=0, tiled=True)
    values = everything[:, :, rough_cells]
    targets = lax.dynamic_slice_in_dim(rough_map, position * half, half, 1)
    picked = jnp.take_along_axis(values.transpose(2, 0, 1), targets[:, :, None], axis=1).transpose(
        1, 2, 0
    )
    current = bottom[:, :, rough_cells]
    inflow = 0.9 * bottom.at[:, :, rough_cells].set(jnp.where(live[None, None, :], picked, current))
    carry = inflow.reshape(half, modes, rows, width)
    cup = couple[0::2][:, :, None, None]
    aup = diag[None, :, None, None] + cup
    up_rhs = rhs[0::2]
    planes = []
    for level in range(planes_count):
        carry = (up_rhs[:, :, level] + cup * carry) / aup
        planes.append(carry)
    up_new = jnp.stack(planes, axis=2)
    fresh = jnp.stack([up_new, down_new], axis=1).reshape(
        dirs_local, modes, planes_count, rows, width
    )
    energy_new = lax.psum(jnp.einsum("s,smzxy->zxy", weight_local, fresh), "mode") / PAIRS
    return (fresh.reshape(pairs_local, planes_count, rows, width), energy_new)


def solution(mesh):
    in_specs = (
        P("mode", None, "space", None),
        P(),
        P(),
        P(),
        P(),
        P(),
        P("space", None),
        P("space"),
        P("space"),
        P("space", None),
    )
    out_specs = (P("mode", None, "space", None), P(None, "space", None))
    return jax.shard_map(
        per_device, mesh=mesh, in_specs=in_specs, out_specs=out_specs, check_vma=False
    )
```

profile of v0, /device:TPU:0, one launch (start us, length us, event | category | flops | bytes accessed | tf_op | source)
XLA Modules:
  0.0 387.9 jit_solution(15497214849482379465)
XLA Ops:
  7.2 4.4 %bitcast_reduce_fusion = bf16[2,8,16,256]{3,2,1,0:T(8,128)(2,1)S(1)} fusion(f32[64,8,16,256]{3,2,1,0:T(8,128)} %param.10), kind=kLoop, calls=%fused_computation.123 | loop fusion | flops 2031616 | bytes 8519680 | tf_op jit(solution)/shard_map/s,smzxy->zxy/reduce_sum | solution.py:38
  11.7 0.4 fusion.42
  12.0 0.7 copy.151
  12.8 4.5 %fusion.58 = (f32[2,32,8,1,256]{4,3,2,1,0:T(1,128)S(1)}, f32[2,32,8,1,256]{4,3,2,1,0:T(1,128)S(1)}) fusion(f32[2,32,8,16,256]{4,3,2,1,0:T(8,128)} %bitcast.132), kind=kLoop, calls=%fused_computation.128 | loop fusion | bytes 2097152 | tf_op jit(solution)/shard_map/slice | solution.py:15
  17.4 1.3 collective-permute-start
  18.7 1.5 collective-permute-start.1
  20.4 77.3 %all-reduce.4.cloned.1.call-done = f32[8,16,256]{2,1,0:T(8,128)} async-done(((f32[8,16,256]{2,1,0:T(8,128)}), f32[8,16,256]{2,1,0:T(8,128)}) %all-reduce.4.cloned.1.call-update) | async-done | bytes 131088 | tf_op jit(solution)/shard_map/psum | solution.py:39
  97.8 0.9 add_divide_fusion.7
  98.7 0.6 broadcast_multiply_fusion
  99.3 0.5 copy.112
  99.9 0.5 copy.114
  100.4 16.7 %fusion.5 = f32[2,32,8,16,256]{4,3,2,1,0:T(8,128)S(1)} fusion(f32[2,32,8,16,256]{4,3,2,1,0:T(8,128)} %bitcast.133, f32[2,32,8,1,256]{4,3,2,1,0:T(1,128)S(1)} %copy.114, f32[2,32,8,1,256]{4,3,2,1,0:T(1,128)S(1)} %copy.112, f32[2]{0:T(128)S(1)} %get-tuple-element.28, f32[2]{0:T(128)S(1)} %get-tuple-element.30, f32[2]{0:T(128)S(1)} %get-tuple-element.27, ...), kind=kLoop, calls=%fused_computation.11 | loop fusion | flops 33554432 | bytes 22020256 | tf_op jit(solution)/shard_map/sub | solution.py:53
  117.1 3.4 copy-done.2
  120.5 1.4 fusion.57
  121.9 3.0 copy.132
  124.9 3.0 copy.133
  127.9 2.0 copy.134
  129.9 2.0 copy.135
  132.0 2.0 copy.136
  133.9 2.1 copy.137
  136.0 2.0 copy.138
  138.0 2.0 copy.139
  140.0 6.8 %fusion.28 = f32[1,32,4096]{1,2,0:T(8,128)S(1)} fusion(f32[1,32,1,16,256]{1,4,3,2,0:T(8,128)} %copy.133, f32[1,32,1,16,256]{1,4,3,2,0:T(8,128)} %copy.132, f32[1,32,1,16,256]{1,4,3,2,0:T(8,128)} %copy.135, f32[1,32,1,16,256]{1,4,3,2,0:T(8,128)} %copy.134, f32[1,32,1,16,256]{1,4,3,2,0:T(8,128)} %copy.137, f32[1,32,1,16,256]{1,4,3,2,0:T(8,128)} %copy.136, ...), kind=kLoop, calls=%fused_computation.41 | loop fusion | flops 3276800 | bytes 4735360 | tf_op jit(solution)/shard_map/div | solution.py:62
  146.7 1.4 copy.123
  148.9 0.8 and_reduce_fusion
  149.7 0.8 compare_select_fusion
  150.5 68.0 %all-gather.2.cloned.1.call-done = f32[16,32,4096]{2,1,0:T(8,128)} async-done(((f32[1,32,4096]{2,1,0:T(8,128)}), f32[16,32,4096]{2,1,0:T(8,128)}) %all-gather.2.cloned.1.call-update) | async-done | bytes 8388624 | tf_op jit(solution)/shard_map/all_gather | solution.py:68
  218.5 23.2 %copy.124 = f32[16,32,4096]{1,0,2:T(8,128)} copy(f32[16,32,4096]{2,1,0:T(8,128)} %all-gather.2.cloned.1.call-done) | data formatting | bytes 16777216 | tf_op jit(solution)/shard_map/all_gather | solution.py:68
  241.7 20.0 %gather_fusion = f32[1024,16,32]{2,1,0:T(8,128)} fusion(f32[16,32,4096]{1,0,2:T(8,128)} %copy.124, s32[1024]{0:T(1024)S(1)} %get-tuple-element.24), kind=kCustom, calls=%fused_computation | custom fusion | bytes 4198400 | tf_op jit(solution)/shard_map/gather | solution.py:69
  261.7 13.3 %scatter_custom_fusion = f32[32,4096]{0,1:T(8,128)S(1)} fusion(f32[32,4096]{0,1:T(8,128)S(1)} %bitcast.134, s32[1024]{0:T(1024)S(1)} %get-tuple-element.25, f32[]{:T(128)} %constant.40.clone.1, pred[1024]{0:T(1024)(128)(4,1)S(1)} %and_reduce_fusion, pred[1024]{0:T(1024)(128)(4,1)S(1)} %iota_compare_fusion, f32[1024,16,32]{2,1,0:T(8,128)} %gather_fusion, ...), kind=kCustom, calls=%fused_computation.61 | custom fusion | flops 65536 | bytes 4728836 | tf_op jit(solution)/shard_map/scatter | solution.py:75
  275.0 1.5 broadcast_multiply_fusion.1
  276.6 2.3 copy.140
  278.8 1.2 constant_dynamic-update-slice_fusion.6
  280.1 1.4 constant_dynamic-update-slice_fusion.5
  281.5 1.2 constant_dynamic-update-slice_fusion.4
  282.7 1.6 constant_dynamic-update-slice_fusion.3
  284.3 1.2 constant_dynamic-update-slice_fusion.2
  285.5 1.4 constant_dynamic-update-slice_fusion.1
  286.9 1.4 constant_dynamic-update-slice_fusion
  288.3 3.2 divide_dynamic-update-slice_fusion
  291.9 0.3 constant_dynamic-update-slice_fusion.9
  292.2 0.2 constant_dynamic-update-slice_fusion.8
  292.4 0.2 constant_dynamic-update-slice_fusion.7
  292.6 4.1 %fusion.53 = (bf16[2,8,16,256]{3,2,1,0:T(8,128)(2,1)S(1)}, f32[1,2,32,8,16,256]{5,4,3,2,1,0:T(8,128)}) fusion(f32[1,1,32,8,16,256]{5,4,3,2,1,0:T(8,128)S(1)} %bitcast.137, f32[1,1,32,8,16,256]{5,4,3,2,1,0:T(8,128)S(1)} %bitcast.138), kind=kLoop, calls=%fused_computation.126 | loop fusion | flops 4128768 | bytes 16908288 | tf_op jit(solution)/shard_map/s,smzxy->zxy/reduce_sum | solution.py:88
  296.7 0.4 fusion.44
  297.0 0.7 copy.150
  297.7 82.1 %all-reduce.6.cloned.1.call-done = f32[8,16,256]{2,1,0:T(8,128)} async-done(((f32[8,16,256]{2,1,0:T(8,128)}), f32[8,16,256]{2,1,0:T(8,128)}) %all-reduce.6.cloned.1.call-update) | async-done | bytes 131088 | tf_op jit(solution)/shard_map/psum | solution.py:88
  379.8 1.6 broadcast_multiply_fusion.2
  (47 shorter events, 0.9 us)
Async XLA Ops:
  7.2 13.1 %copy-start = (f32[3,32]{1,0:T(4,128)S(1)}, f32[3,32]{1,0:T(4,128)}, u32[]{:S(2)}) copy-start(f32[3,32]{1,0:T(4,128)} %param.11) | copy-start | bytes 1156
  7.2 90.6 %all-reduce.4.cloned.1.call-start = ((), (), s32[]{:S(2)}) async-start(), calls=%async_computation | async-start | bytes 262144 | tf_op jit(solution)/shard_map/psum | solution.py:39
  7.2 4.4 %copy-start.8 = (f32[32]{0:T(128)S(1)}, f32[32]{0:T(128)}, u32[]{:S(2)}) copy-start(f32[32]{0:T(128)} %param.15) | copy-start | bytes 388
  11.6 8.7 %copy-start.3 = (f32[16,256]{1,0:T(8,128)S(1)}, f32[16,256]{1,0:T(8,128)}, u32[]{:S(2)}) copy-start(f32[16,256]{1,0:T(8,128)} %param.16) | copy-start | bytes 49156
  11.6 8.7 %copy-start.6 = (f32[32]{0:T(128)S(1)}, f32[32]{0:T(128)}, u32[]{:S(2)}) copy-start(f32[32]{0:T(128)} %param.12) | copy-start | bytes 388
  11.7 8.8 %copy-start.4 = (f32[32]{0:T(128)S(1)}, f32[32]{0:T(128)}, u32[]{:S(2)}) copy-start(f32[32]{0:T(128)} %param.14) | copy-start | bytes 388
  11.7 8.7 %copy-start.7 = (f32[32]{0:T(128)S(1)}, f32[32]{0:T(128)}, u32[]{:S(2)}) copy-start(f32[32]{0:T(128)} %param.13) | copy-start | bytes 388
  12.7 205.7 %all-gather.2.cloned.1.call-start = ((), (), s32[]{:S(2)}) async-start(), calls=%async_computation.1 | async-start | bytes 8912896 | tf_op jit(solution)/shard_map/all_gather | solution.py:68
  17.4 81.9 %collective-permute-start = (f32[2,32,8,1,256]{4,2,3,1,0:T(8,128)S(1)}, f32[2,32,8,1,256]{4,2,3,1,0:T(8,128)S(1)}, u32[]{:S(2)}, u32[]{:S(2)}) collective-permute-start(f32[2,32,8,1,256]{4,2,3,1,0:T(8,128)S(1)} %copy.111), channel_id=1, source_target_pairs={{0,16},{16,32},{32,48},{48,64},{64,80},{80,96},{96,112},{1,17},{17... | collective-permute-start | bytes 1572872 | tf_op jit(solution)/shard_map/ppermute | solution.py:14
  18.7 81.1 %collective-permute-start.1 = (f32[2,32,8,1,256]{4,2,3,1,0:T(8,128)S(1)}, f32[2,32,8,1,256]{4,2,3,1,0:T(8,128)S(1)}, u32[]{:S(2)}, u32[]{:S(2)}) collective-permute-start(f32[2,32,8,1,256]{4,2,3,1,0:T(8,128)S(1)} %copy.113), channel_id=1, source_target_pairs={{16,0},{32,16},{48,32},{64,48},{80,64},{96,80},{112,96},{17,1},{33... | collective-permute-start | bytes 1572872 | tf_op jit(solution)/shard_map/ppermute | solution.py:17
  117.1 3.4 copy-start.2
  140.0 10.5 %copy-start.5 = (s32[1024]{0:T(1024)S(1)}, s32[1024]{0:T(1024)}, u32[]{:S(2)}) copy-start(s32[1024]{0:T(1024)} %param.17) | copy-start | bytes 12292
  148.2 231.6 %all-reduce.6.cloned.1.call-start = ((), (), s32[]{:S(2)}) async-start(), calls=%async_computation.2 | async-start | bytes 262144 | tf_op jit(solution)/shard_map/psum | solution.py:88
  282.7 8.8 %slice-start = ((s8[8388608]{0:T(1024)(128)(4,1)}), s8[4194304]{0:T(1024)(128)(4,1)S(1)}, s32[]{:S(2)}) async-start(s8[8388608]{0:T(1024)(128)(4,1)} %bitcast.130), calls=%async_computation.3 | async-start | bytes 8388608
  286.9 4.6 %slice-start.1 = ((s8[8388608]{0:T(1024)(128)(4,1)}), s8[4194304]{0:T(1024)(128)(4,1)S(1)}, s32[]{:S(2)}) async-start(s8[8388608]{0:T(1024)(128)(4,1)} %bitcast.130), calls=%async_computation.4 | async-start | bytes 8388608
  292.6 88.8 %copy-start.1 = (f32[3,32]{1,0:T(4,128)S(1)}, f32[3,32]{1,0:T(4,128)}, u32[]{:S(2)}) copy-start(f32[3,32]{1,0:T(4,128)} %param.11) | copy-start | bytes 1156
Sparse Core Ops, SparseCore 0:
  12.9 84.8 all-reduce.3
  148.3 70.1 all-gather.1
  297.8 81.8 all-reduce.5
where the time goes:
time: 390 us; the launch traced here: 388 us
  waiting for transfers between devices  227 us (58%)
  local copies, waits for them, and re-layouts  77 us (20%)
  other arithmetic  65 us (17%)
  between operations  14.8 us (4%)
    psum x1, waiting for transfers between devices, per_device(): lax.psum(jnp.einsum('s,smzxy->zxy', weight_local, fresh), 'mode') / PAIRS  82.1 us
    psum x1, waiting for transfers between devices, per_device(): energy = lax.psum(partial_value, 'mode') / PAIRS  77.3 us
    all_gather x1, waiting for transfers between devices, per_device(): everything = lax.all_gather(bottom, 'mode', axis=0, tiled=True)  68 us
    all_gather x1, local copies, waits for them, and re-layouts, per_device(): everything = lax.all_gather(bottom, 'mode', axis=0, tiled=True)  23.2 us
    gather x1, local copies, waits for them, and re-layouts, per_device(): values = everything[:, :, rough_cells]  20 us
    squeeze x8, local copies, waits for them, and re-layouts, per_device(): carry = (down_rhs[:, :, level] + cdown * carry) / adown  18 us
    sub x1, other arithmetic, per_device(): rhs = field + source[None] - speed * (along + across)  16.7 us
    unnamed x13, other arithmetic  13.3 us
  transfers between devices with their start and end apart: 5, of which 3 were waited for; matrix products, arithmetic and copies ran while one was open for 2% of the time, Pallas kernels for 0%

commit v1 on v0

v1 whole, which is shorter than its diff:
```python
import jax
import jax.numpy as jnp
from jax import lax
from jax.experimental import pallas as pl
from jax.experimental.pallas import tpu as pltpu
from jax.sharding import PartitionSpec as P

PAIRS = 1024
DIRS = 32
MODES = 32
Z = 8
ROWS = 16
COLS = 256
GROUP = 16
PLANE = Z * ROWS
PACK = 48
F32 = jnp.float32


def column(row):
    r = lax.broadcasted_iota(jnp.int32, (MODES, MODES), 0)
    c = lax.broadcasted_iota(jnp.int32, (MODES, MODES), 1)
    return jnp.sum(jnp.where(r == c, jnp.broadcast_to(row, (MODES, MODES)), 0.0), axis=1, keepdims=True)


def edge_kernel(
    pos, dcs, wts, cnt, left, right, dcv, vel, rate, spec, wv, cells, rmap,
    e_ref, edge_ref, small_ref, jm_ref, k0_ref, kap, bet, acc,
):
    g = pl.program_id(0)
    k = pos[0]
    cx = dcs[0, 2 * k]
    cz = jnp.abs(dcs[2, 2 * k])
    row = jnp.where(cx > 0.0, ROWS - 1, 0)

    @pl.when(g == 0)
    def _():
        v, a = column(vel[...]), 1.0 + column(rate[...])
        inv = 1.0 / (a + v * cz)
        kap[...] = jnp.broadcast_to(v * cz * inv, (MODES, COLS))
        bet[...] = jnp.broadcast_to(v * jnp.abs(cx) * inv, (MODES, COLS))
        acc[...] = jnp.zeros_like(acc)
        e_ref[...] = jnp.zeros_like(e_ref)
        slot = lax.broadcasted_iota(jnp.int32, (1, cells.shape[1]), 1)
        local = jnp.where(slot < cnt[0], cells[...] - k * COLS, -1)
        q = lax.broadcasted_iota(jnp.int32, (COLS, cells.shape[1]), 0)
        hot = jnp.where(q == local, 1.0, 0.0).astype(jnp.bfloat16)
        idx = (rmap[...] + 1).astype(F32).astype(jnp.bfloat16)
        jm_ref[...] = lax.dot_general(idx, hot, (((1,), (1,)), ((), ())), preferred_element_type=F32)
        czr = jnp.abs(dcv[2:3, :])
        c_all = v * czr
        inv_all = 1.0 / (a + c_all)
        k_all = c_all * inv_all
        term = column(rate[...]) * column(spec[...]) * inv_all * wv[...]
        odd = lax.broadcasted_iota(jnp.int32, (MODES, DIRS), 1) % 2 == 1
        zr = lax.broadcasted_iota(jnp.int32, (Z, 128), 0)
        zc = lax.broadcasted_iota(jnp.int32, (Z, 128), 1)
        total = jnp.zeros((Z, 128), F32)
        for n in range(Z):
            down = jnp.sum(jnp.sum(jnp.where(odd, term, 0.0), axis=1, keepdims=True), axis=0, keepdims=True)
            up = jnp.sum(jnp.sum(jnp.where(odd, 0.0, term), axis=1, keepdims=True), axis=0, keepdims=True)
            total += jnp.where(zc - zr == n, down, 0.0) + jnp.where(zr - zc == n, up, 0.0)
            term = term * k_all
        k0_ref[...] = total

    w = wts[2 * k + g // 4]
    for h, x_ref in enumerate((left, right)):
        for t in range(PLANE // 8):
            part = x_ref[pl.ds(t * 8, 8), :]
            for p in range(1, 8):
                part += x_ref[pl.ds(p * PLANE + t * 8, 8), :]
            e_ref[h, pl.ds(t * 8, 8), :] += w * part
    m0 = pl.multiple_of(8 * (g % 4), 8)
    kp = kap[pl.ds(m0, 8), :]
    bt = bet[pl.ds(m0, 8), :]
    rows = []
    for z in range(Z):
        halves = [x_ref[pl.ds(z * ROWS + row, 8, stride=PLANE), :] for x_ref in (left, right)]
        for h in range(2):
            edge_ref[h, pl.ds(pl.multiple_of(z * 64 + 8 * g, 8), 8), :] = halves[h]
        rows.append(bt * jnp.concatenate(halves, axis=1))

    @pl.when(g < 4)
    def _():
        t = rows[0]
        acc[pl.ds(0, 8), :] += w * t
        for z in range(1, Z):
            t = kp * t + rows[z]
            acc[pl.ds(8 * z, 8), :] += w * t

    @pl.when(g >= 4)
    def _():
        t = rows[Z - 1]
        acc[pl.ds(8 * (Z - 1), 8), :] += w * t
        for z in reversed(range(Z - 1)):
            t = kp * t + rows[z]
            acc[pl.ds(8 * z, 8), :] += w * t
        small_ref[pl.ds(8 + m0, 8), :] = t

    @pl.when(g == 7)
    def _():
        for z in range(Z):
            small_ref[pl.ds(z, 1), :] = jnp.sum(acc[pl.ds(8 * z, 8), :], axis=0, keepdims=True)


def places(dcs, k):
    up_x, up_y = dcs[0, 2 * k] > 0.0, dcs[1, 2 * k] > 0.0
    first_row = jnp.where(up_x, 0, 8)
    first_col = jnp.where(up_y, 0, 128)
    rows = [pl.multiple_of(first_row, 8), pl.multiple_of(8 - first_row, 8)]
    cols = [pl.multiple_of(first_col, 128), pl.multiple_of(128 - first_col, 128)]
    sub = lax.broadcasted_iota(jnp.int32, (8, 128), 0) == jnp.where(up_x, 0, 7)
    lane = lax.broadcasted_iota(jnp.int32, (8, 128), 1) == jnp.where(up_y, 0, 127)
    return rows, cols, jnp.where(up_x, 1, 7), jnp.where(up_y, 1, 127), sub, lane


def sweep_kernel(
    pos, dcs, wts, x_ref, vel, rate, spec, heat, e_ref, l0_ref, pack_ref, tab, accd, accu, d0,
):
    m = pl.program_id(0)
    k = pos[0]
    cx, cy = jnp.abs(dcs[0, 2 * k]), jnp.abs(dcs[1, 2 * k])
    cz = jnp.abs(dcs[2, 2 * k])

    @pl.when(m == 0)
    def _():
        v, a = column(vel[...]), 1.0 + column(rate[...])
        inv = 1.0 / (a + v * cz)
        for i, c in enumerate(((1.0 - v * cx - v * cy) * inv, v * cx * inv, v * cy * inv, v * cz * inv, column(spec[...]))):
            tab[i] = jnp.broadcast_to(c, (MODES, 128))
        accd[...] = jnp.zeros_like(accd)
        accu[...] = jnp.zeros_like(accu)

    rows, cols, shift_x, shift_y, sub, lane = places(dcs, k)
    alpha, beta, gamma, kappa, share = [jnp.broadcast_to(tab[i, pl.ds(m, 1), :], (8, 128)) for i in range(5)]

    def rhs(d, z):
        i = [[x_ref[d, 0, pl.ds(z * ROWS + r, 8), pl.ds(c, 128)] for c in cols] for r in rows]
        rx = [[pltpu.roll(t, shift_x, 0) for t in ts] for ts in i]
        ry = [[pltpu.roll(t, shift_y, 1) for t in ts] for ts in i]
        out = []
        for r in range(2):
            for c in range(2):
                x = jnp.where(sub, 0.0 if r == 0 else rx[0][c], rx[r][c])
                y = jnp.where(lane, 0.0 if c == 0 else ry[r][0], ry[r][c])
                out.append(alpha * i[r][c] + beta * x + gamma * y)
        return out

    tiles = [(r, c) for r in rows for c in cols]
    down = [share * heat[pl.ds(r, 8), pl.ds(c, 128)] for r, c in tiles]
    for z in reversed(range(Z)):
        down = [f + kappa * t for f, t in zip(rhs(1, z), down)]
        for t, (r, c) in zip(down, tiles):
            at = pl.ds(z * ROWS + r, 8)
            l0_ref[1, 0, at, pl.ds(c, 128)] = t
            accd[c // 128, at, :] += t
    for t, (r, c) in zip(down, tiles):
        d0[c // 128, pl.ds(pl.multiple_of(m * ROWS, ROWS) + r, 8), :] = t
    up = None
    for z in range(Z):
        up = rhs(0, z) if up is None else [f + kappa * t for f, t in zip(rhs(0, z), up)]
        for t, (r, c) in zip(up, tiles):
            at = pl.ds(z * ROWS + r, 8)
            l0_ref[0, 0, at, pl.ds(c, 128)] = t
            accu[c // 128, at, :] += t

    @pl.when(m == MODES - 1)
    def _():
        accd[...] = wts[2 * k + 1] * accd[...] + wts[2 * k] * accu[...]
        for r in range(ROWS):
            for h in range(2):
                at = pl.ds(h * 128, 128)
                pack_ref[pl.ds(r * PACK, 8), at] = e_ref[h, pl.ds(r, 8, stride=ROWS), :]
                pack_ref[pl.ds(r * PACK + 8, 8), at] = accd[h, pl.ds(r, 8, stride=ROWS), :]
                for t in range(MODES // 8):
                    pack_ref[pl.ds(r * PACK + 16 + 8 * t, 8), at] = d0[h, pl.ds(t * PLANE + r, 8, stride=ROWS), :]


def middle_kernel(wts, got, dcv, vel, rate, spec, jm_ref, k0_ref, out, q_ref):
    energy = got[0, 0:8, :]
    rest = got[0, 8:16, :]
    for s in range(1, GROUP):
        energy += got[s, 0:8, :]
        rest += got[s, 8:16, :]
    energy = energy * (1.0 / PAIRS)
    equil = energy / (1.0 + 0.3 * jnp.abs(energy))
    eq = [jnp.broadcast_to(equil[z : z + 1, :], (8, COLS)) for z in range(Z)]
    v, a = column(vel[...]), 1.0 + column(rate[...])
    c_all = v * jnp.abs(dcv[2:3, :])
    inv_all = 1.0 / (a + c_all)
    k_all = c_all * inv_all
    n_all = column(rate[...]) * column(spec[...]) * inv_all
    for j in range(GROUP):
        for t in range(MODES // 8):
            at = slice(8 * t, 8 * t + 8)
            kp = jnp.broadcast_to(k_all[at, 2 * j + 1 : 2 * j + 2], (8, COLS))
            eta = jnp.broadcast_to(n_all[at, 2 * j + 1 : 2 * j + 2], (8, COLS))
            s = eq[Z - 1]
            for z in reversed(range(Z - 1)):
                s = kp * s + eq[z]
            q_ref[j, at, :] = 0.9 * (got[j, 16 + 8 * t : 24 + 8 * t, :] + eta * s)
    acc = [jnp.zeros((8, COLS), F32) for _ in range(Z)]
    for k in range(GROUP):
        jm = jnp.broadcast_to(jm_ref[k : k + 1, :], (8, COLS))
        jm = jnp.where(jm < 0.5, float(k + 1), jm)
        near = [jnp.abs(jm - float(j + 1)) < 0.5 for j in range(GROUP)]
        w = wts[2 * k]
        for t in range(MODES // 8):
            at = slice(8 * t, 8 * t + 8)
            pick = q_ref[0, at, :]
            for j in range(1, GROUP):
                pick = jnp.where(near[j], q_ref[j, at, :], pick)
            out[k, at, :] = pick
            kp = jnp.broadcast_to(k_all[at, 2 * k : 2 * k + 1], (8, COLS))
            pick = w * pick
            for z in range(Z):
                pick = kp * pick
                acc[z] += pick
    bounce = jnp.concatenate([jnp.sum(t, axis=0, keepdims=True) for t in acc], axis=0)
    fresh = rest + bounce
    for z in range(Z):
        fresh += jnp.broadcast_to(k0_ref[:, z : z + 1], (8, COLS)) * eq[z]
    fresh = fresh * (1.0 / PAIRS)
    for k in range(GROUP):
        out[k, 32:40, :] = equil
        out[k, 40:48, :] = fresh


def finish_kernel(
    pos, dcs, l0_ref, left, right, low, high, vel, rate, spec, out_ref, en_ref, tab, eq,
):
    m = pl.program_id(0)
    k = pos[0]
    cx, cz = dcs[0, 2 * k], jnp.abs(dcs[2, 2 * k])

    @pl.when(m == 0)
    def _():
        v, a = column(vel[...]), 1.0 + column(rate[...])
        inv = 1.0 / (a + v * cz)
        for i, c in enumerate((column(rate[...]) * column(spec[...]) * inv, v * jnp.abs(cx) * inv, v * cz * inv)):
            tab[i] = jnp.broadcast_to(c, (MODES, 128))
        for z in range(Z):
            for h, back in enumerate((left, right)):
                for b in range(2):
                    to = (pl.ds(z * ROWS + 8 * b, 8), pl.ds(h * 128, 128))
                    eq[to] = back[pl.ds(8 * b * PACK + 32 + z, 8, stride=PACK), :]
                    en_ref[to] = back[pl.ds(8 * b * PACK + 40 + z, 8, stride=PACK), :]

    rows, _, _, _, sub, _ = places(dcs, k)
    eta, beta, kappa = [jnp.broadcast_to(tab[i, pl.ds(m, 1), :], (8, 128)) for i in range(3)]
    tiles = [(i, r, 128 * h, back) for i, r in enumerate(rows) for h, back in enumerate((left, right))]

    def source(d, z, i, r, c):
        s = eta * eq[pl.ds(z * ROWS + r, 8), pl.ds(c, 128)]
        if i == 0:
            at = (c // 128, pl.ds(z * 64 + d * 32 + m, 1))
            e = jnp.where(cx > 0.0, low[at], high[at])
            s += jnp.where(sub, beta * e, 0.0)
        return s

    for i, r, c, back in tiles:
        at = [(pl.ds(z * ROWS + r, 8), pl.ds(c, 128)) for z in range(Z)]
        t = None
        for z in reversed(range(Z)):
            s = source(1, z, i, r, c)
            t = s if t is None else kappa * t + s
            out_ref[(1, 0) + at[z]] = l0_ref[(1, 0) + at[z]] + t
        t = back[pl.ds(r * PACK + m, 8, stride=PACK), :]
        for z in range(Z):
            t = kappa * t + source(0, z, i, r, c)
            out_ref[(0, 0) + at[z]] = l0_ref[(0, 0) + at[z]] + t


def per_device(
    intensity, dir_cos, velocity, rate, spectrum, weight, heat, rough_cells, rough_count, rough_map
):
    position = lax.axis_index("mode").astype(jnp.int32)
    pos = position.reshape(1)
    vel, rat, spe, wei = [t.reshape(1, -1) for t in (velocity, rate, spectrum, weight)]
    slots = rough_cells.shape[0]
    smem = pl.BlockSpec(memory_space=pltpu.SMEM)

    def whole(*shape):
        return pl.BlockSpec(shape, lambda i: (0,) * len(shape))

    rows_flat = intensity.reshape(64 * PLANE, COLS)
    params = pltpu.CompilerParams(vmem_limit_bytes=40 << 20)
    energy, edge, small, jm, k0 = pl.pallas_call(
        edge_kernel,
        grid=(8,),
        in_specs=[smem] * 4
        + [pl.BlockSpec((8 * PLANE, 128), lambda i: (i, 0)), pl.BlockSpec((8 * PLANE, 128), lambda i: (i, 1)), whole(3, DIRS)]
        + [whole(1, 32)] * 4
        + [whole(1, slots), whole(GROUP, slots)],
        out_specs=[whole(2, PLANE, 128), whole(2, 512, 128), whole(40, COLS), whole(GROUP, COLS), whole(Z, 128)],
        out_shape=[
            jax.ShapeDtypeStruct(s, F32)
            for s in ((2, PLANE, 128), (2, 512, 128), (40, COLS), (GROUP, COLS), (Z, 128))
        ],
        scratch_shapes=[pltpu.VMEM((MODES, COLS), F32)] * 2 + [pltpu.VMEM((64, COLS), F32)],
        compiler_params=params,
        cost_estimate=pl.CostEstimate(flops=4 << 20, bytes_accessed=8 << 20, transcendentals=0),
        name="edges",
    )(
        pos, dir_cos, weight, rough_count, rows_flat, rows_flat, dir_cos, vel, rat, spe, wei,
        rough_cells.reshape(1, slots), rough_map.T,
    )
    count = lax.axis_size("space")
    forward = [(i, i + 1) for i in range(count - 1)]
    backward = [(t, s) for s, t in forward]
    small_low = lax.ppermute(small, "space", forward)
    small_high = lax.ppermute(small, "space", backward)
    edge_low = lax.ppermute(edge, "space", forward)
    edge_high = lax.ppermute(edge, "space", backward)

    field = intensity.reshape(2, MODES, PLANE, COLS)
    block = pl.BlockSpec((2, 1, PLANE, COLS), lambda i: (0, i, 0, 0))
    base, pack = pl.pallas_call(
        sweep_kernel,
        grid=(MODES,),
        in_specs=[smem] * 3 + [block] + [whole(1, 32)] * 3 + [whole(ROWS, COLS), whole(2, PLANE, 128)],
        out_specs=[block, whole(ROWS * PACK, COLS)],
        out_shape=[
            jax.ShapeDtypeStruct(field.shape, F32),
            jax.ShapeDtypeStruct((ROWS * PACK, COLS), F32),
        ],
        scratch_shapes=[
            pltpu.VMEM((5, MODES, 128), F32),
            pltpu.VMEM((2, PLANE, 128), F32),
            pltpu.VMEM((2, PLANE, 128), F32),
            pltpu.VMEM((2, MODES * ROWS, 128), F32),
        ],
        compiler_params=params,
        cost_estimate=pl.CostEstimate(flops=30 << 20, bytes_accessed=16 << 20, transcendentals=0),
        name="sweep",
    )(pos, dir_cos, weight, field, vel, rat, spe, heat, energy)

    up_x = lax.dynamic_slice(dir_cos, (0, 2 * position), (1, 1))[0, 0] > 0.0
    delta = jnp.where(up_x, small_low, small_high)
    start = jnp.where(up_x, 0, (ROWS - 1) * PACK) + 8
    pack = lax.dynamic_update_slice(pack, lax.dynamic_slice(pack, (start, 0), (40, COLS)) + delta, (start, 0))
    got = lax.all_to_all(pack.reshape(GROUP, PACK, COLS), "mode", 0, 0, tiled=True)

    reply = pl.pallas_call(
        middle_kernel,
        in_specs=[smem] + [pl.BlockSpec(memory_space=pltpu.VMEM)] * 7,
        out_specs=pl.BlockSpec(memory_space=pltpu.VMEM),
        out_shape=jax.ShapeDtypeStruct((GROUP, PACK, COLS), F32),
        scratch_shapes=[pltpu.VMEM((GROUP, MODES, COLS), F32)],
        compiler_params=params,
        name="middle",
    )(weight, got, dir_cos, vel, rat, spe, jm, k0)
    back = lax.all_to_all(reply, "mode", 0, 0, tiled=True).reshape(GROUP * PACK, COLS)

    fresh, energy_new = pl.pallas_call(
        finish_kernel,
        grid=(MODES,),
        in_specs=[smem] * 2
        + [block] + [pl.BlockSpec((GROUP * PACK, 128), lambda i, h=h: (0, h)) for h in range(2)]
        + [whole(2, 512, 128), whole(2, 512, 128)]
        + [whole(1, 32)] * 3,
        out_specs=[block, whole(PLANE, COLS)],
        out_shape=[
            jax.ShapeDtypeStruct(field.shape, F32),
            jax.ShapeDtypeStruct((PLANE, COLS), F32),
        ],
        scratch_shapes=[pltpu.VMEM((3, MODES, 128), F32), pltpu.VMEM((PLANE, COLS), F32)],
        compiler_params=params,
        name="finish",
    )(pos, dir_cos, base, back, back, edge_low, edge_high, vel, rat, spe)
    return fresh.reshape(intensity.shape), energy_new.reshape(Z, ROWS, COLS)


def solution(mesh):
    in_specs = (
        P("mode", None, "space", None),
        P(),
        P(),
        P(),
        P(),
        P(),
        P("space", None),
        P("space"),
        P("space"),
        P("space", None),
    )
    out_specs = (P("mode", None, "space", None), P(None, "space", None))
    return jax.shard_map(
        per_device, mesh=mesh, in_specs=in_specs, out_specs=out_specs, check_vma=False
    )
```

time: 390 us -> 106 us (0.27)
  waiting for transfers between devices: 227 us -> 10.4 us
  other arithmetic: 65 us -> 1.25 us
  local copies, waits for them, and re-layouts: 77 us -> 15 us
  Pallas kernels: 0 us -> 40.4 us
  blocking collectives: 0 us -> 23.2 us
  between operations: 14.8 us -> 2.11 us
  starting transfers between devices: 2.92 us -> 12.5 us
    psum x2 -> x0, waiting for transfers between devices: 159 us -> none  [the longest x1 82.1 us: per_device(): lax.psum(jnp.einsum('s,smzxy->zxy', weight_local, fresh), 'mode') / PAIRS]
    all_gather x1 -> x0, waiting for transfers between devices: 68 us -> none  [per_device(): everything = lax.all_gather(bottom, 'mode', axis=0, tiled=True)]
    pallas_call x0 -> x4, Pallas kernels: none -> 40.4 us  [the longest x1 20.6 us: per_device(): pl.pallas_call(sweep_kernel, grid=(MODES,), in_specs=[smem] * 3 + [block]...]
    all_gather x1 -> x0, local copies, waits for them, and re-layouts: 23.2 us -> none  [per_device(): everything = lax.all_gather(bottom, 'mode', axis=0, tiled=True)]
    all_to_all x0 -> x1, blocking collectives: none -> 23.2 us  [per_device(): lax.all_to_all(pack.reshape(GROUP, PACK, COLS), 'mode', 0, 0, tiled=True)]
    gather x1 -> x0, local copies, waits for them, and re-layouts: 20 us -> none  [per_device(): values = everything[:, :, rough_cells]]
    squeeze x8 -> x0, local copies, waits for them, and re-layouts: 18 us -> none  [per_device(): carry = (down_rhs[:, :, level] + cdown * carry) / adown]
    sub x1 -> x0, other arithmetic: 16.7 us -> none  [per_device(): rhs = field + source[None] - speed * (along + across)]
  transfers between devices with their start and end apart: 5 -> 5, of which waited for: 3 -> 2; matrix products, arithmetic and copies ran while one was open for 2% -> 1% of each run, Pallas kernels for 0% -> 20%
where the time goes in v1:
time: 106 us; the launch traced here: 105 us
  Pallas kernels  40.4 us (38%)
  blocking collectives  23.2 us (22%)
  local copies, waits for them, and re-layouts  15 us (14%)
  starting transfers between devices  12.5 us (12%)
  waiting for transfers between devices  10.4 us (10%)
  between operations  2.11 us (2%)
  other arithmetic  1.25 us (1%)
    all_to_all x1, blocking collectives, per_device(): lax.all_to_all(pack.reshape(GROUP, PACK, COLS), 'mode', 0, 0, tiled=True)  23.2 us
    pallas_call x1, Pallas kernels, per_device(): pl.pallas_call(sweep_kernel, grid=(MODES,), in_specs=[smem] * 3 + [block]...  20.6 us
    unnamed x32, local copies, waits for them, and re-layouts  15 us
    pallas_call x1, Pallas kernels, per_device(): pl.pallas_call(finish_kernel, grid=(MODES,), in_specs=[smem] * 2 + [block...  14 us
    all_to_all x1, waiting for transfers between devices, per_device(): lax.all_to_all(reply, 'mode', 0, 0, tiled=True).reshape(GROUP * PACK, COLS)  8.87 us
    all_to_all x1, starting transfers between devices, per_device(): lax.all_to_all(reply, 'mode', 0, 0, tiled=True).reshape(GROUP * PACK, COLS)  3.8 us
    pallas_call x1, Pallas kernels, per_device(): pl.pallas_call(middle_kernel, in_specs=[smem] + [pl.BlockSpec(memory_spac...  3.09 us
    ppermute x1, starting transfers between devices, per_device(): edge_low = lax.ppermute(edge, 'space', forward)  3.06 us
  transfers between devices with their start and end apart: 5, of which 2 were waited for; matrix products, arithmetic and copies ran while one was open for 1% of the time, Pallas kernels for 20%

profile of v1, /device:TPU:0, one launch (start us, length us, event | category | flops | bytes accessed | tf_op | source)
XLA Modules:
  0.0 104.8 jit_solution(6750782633086450645)
XLA Ops:
  1.3 0.0 copy-start
  1.3 3.4 %copy-done = f32[64,8,16,256]{3,2,1,0:T(8,128)S(1)} copy-done((f32[64,8,16,256]{3,2,1,0:T(8,128)S(1)}, f32[64,8,16,256]{3,2,1,0:T(8,128)}, u32[]{:S(2)}) %copy-start) | copy-done | bytes 8388632
  4.7 0.0 copy-start.3
  4.7 0.8 copy-done.3
  5.5 0.0 copy-start.4
  5.5 0.7 copy-done.4
  6.2 0.0 copy-start.7
  6.2 0.7 copy-done.7
  6.8 0.0 copy-start.9
  6.8 0.7 copy-done.9
  7.5 0.0 copy-start.11
  7.5 0.7 copy-done.11
  8.2 0.0 copy-start.13
  8.2 0.7 copy-done.13
  8.8 0.0 copy-start.15
  8.8 0.7 copy-done.15
  9.5 0.0 copy-start.5
  9.5 0.0 copy-start.6
  9.5 0.0 copy-start.8
  9.5 0.0 copy-start.10
  9.5 0.0 copy-start.12
  9.5 0.0 copy-start.14
  9.5 2.7 %edges.1 = (f32[2,128,128]{2,1,0:T(8,128)S(1)}, f32[2,512,128]{2,1,0:T(8,128)S(1)}, f32[40,256]{1,0:T(8,128)S(1)}, f32[16,256]{1,0:T(8,128)S(1)}, f32[8,128]{1,0:T(8,128)S(1)}) custom-call(s32[1]{0:T(128)} %bitcast.pos, f32[3,32]{1,0:T(4,128)S(1)} %copy-done.4, f32[32]{0:T(128)S(1)} %copy-done.7, s32[1]{0:T(128)S(6)} %copy.13.cnt, f32[8192,256]{1,0:T(8,128)S(1)} %bitcast.15, ...), custom_call_target="tpu_custom_call" | custom-call | flops 4194304 | bytes 8388608 | tf_op jit(solution)/shard_map/edges/pallas_call | solution.py:288
  12.2 1.3 %collective-permute-start.1 = (f32[40,256]{1,0:T(8,128)S(1)}, f32[40,256]{1,0:T(8,128)S(1)}, u32[]{:S(2)}, u32[]{:S(2)}) collective-permute-start(f32[40,256]{1,0:T(8,128)S(1)} %get-tuple-element.14), channel_id=1, source_target_pairs={{16,0},{32,16},{48,32},{64,48},{80,64},{96,80},{112,96},{17,1},{33... | collective-permute-start | bytes 122888 | tf_op jit(solution)/shard_map/ppermute | solution.py:312
  13.5 3.0 %collective-permute-start = (f32[40,256]{1,0:T(8,128)S(1)}, f32[40,256]{1,0:T(8,128)S(1)}, u32[]{:S(2)}, u32[]{:S(2)}) collective-permute-start(f32[40,256]{1,0:T(8,128)S(1)} %get-tuple-element.14), channel_id=1, source_target_pairs={{0,16},{16,32},{32,48},{48,64},{64,80},{80,96},{96,112},{1,17},{17... | collective-permute-start | bytes 122888 | tf_op jit(solution)/shard_map/ppermute | solution.py:311
  16.6 0.0 copy-done.5
  16.6 0.6 fusion
  17.8 0.0 copy-done.6
  17.8 0.0 copy-done.8
  17.8 0.0 copy-done.10
  17.8 0.0 copy-done.12
  17.9 0.0 copy-done.14
  17.9 20.6 %sweep.1 = (f32[2,32,128,256]{3,2,1,0:T(8,128)S(1)}, f32[768,256]{1,0:T(8,128)S(1)}) custom-call(s32[1]{0:T(128)} %bitcast.pos, f32[3,32]{1,0:T(4,128)S(1)} %copy-done.5, f32[32]{0:T(128)S(1)} %copy-done.8, f32[2,32,128,256]{3,2,1,0:T(8,128)} %bitcast.14, f32[1,32]{1,0:T(1,128)S(1)} %bitcast.23, f32[1,32]{1,0:T(1,128)S(1)} %bitcast.27, ...), custom_call_target="tpu_custom_call" | custom-call | flops 31457280 | bytes 16777216 | tf_op jit(solution)/shard_map/sweep/pallas_call | solution.py:318
  38.5 0.0 copy-start.1
  38.5 3.4 %copy-done.1 = f32[2,32,128,256]{3,2,1,0:T(8,128)} copy-done((f32[2,32,128,256]{3,2,1,0:T(8,128)}, f32[2,32,128,256]{3,2,1,0:T(8,128)S(1)}, u32[]{:S(2)}) %copy-start.1) | copy-done | bytes 8388632
  41.9 0.0 collective-permute-done.1
  41.9 0.0 collective-permute-done
  41.9 0.7 add_dynamic-update-slice_fusion
  42.5 23.2 %all_to_all.10.got = f32[16,48,256]{2,1,0:T(8,128)S(1)} all-to-all(f32[16,48,256]{2,1,0:T(8,128)S(1)} %bitcast.19), channel_id=1, replica_groups=mesh['space'=8,'mode'=16] {'mode'}, dimensions={0} | all-to-all | bytes 1572864 | tf_op jit(solution)/shard_map/all_to_all | solution.py:342
  65.7 3.1 %middle.1 = f32[16,48,256]{2,1,0:T(8,128)} custom-call(f32[32]{0:T(128)S(1)} %copy-done.8, f32[16,48,256]{2,1,0:T(8,128)S(1)} %all_to_all.10.got, f32[3,32]{1,0:T(4,128)S(1)} %copy-done.5, f32[1,32]{1,0:T(1,128)S(1)} %bitcast.24, f32[1,32]{1,0:T(1,128)S(1)} %bitcast.28, f32[1,32]{1,0:T(1,128)S(1)} %bitcast.32, f32[16,256]{1,0:T(8,128)S(1)} %get-tuple-element.15.jm_ref, ...), custom_call_target="tpu_custom_call" | custom-call | tf_op jit(solution)/shard_map/middle/pallas_call | solution.py:344
  68.8 3.8 %all-to-all-start.1 = ((f32[16,48,256]{2,1,0:T(8,128)}), f32[16,48,256]{2,1,0:T(8,128)S(1)}, u32[]{:S(2)}, u32[]{:S(2)}) async-start(f32[16,48,256]{2,1,0:T(8,128)} %middle.1), calls=%async_computation.1 | async-start | bytes 1572864 | tf_op jit(solution)/shard_map/all_to_all | solution.py:353
  72.6 1.3 %collective-permute-start.3 = (f32[2,512,128]{2,1,0:T(8,128)S(1)}, f32[2,512,128]{2,1,0:T(8,128)S(1)}, u32[]{:S(2)}, u32[]{:S(2)}) collective-permute-start(f32[2,512,128]{2,1,0:T(8,128)S(1)} %get-tuple-element.17), channel_id=1, source_target_pairs={{16,0},{32,16},{48,32},{64,48},{80,64},{96,80},{112,96},{17,1},{33... | collective-permute-start | bytes 1572872 | tf_op jit(solution)/shard_map/ppermute | solution.py:314
  73.9 3.1 %collective-permute-start.2 = (f32[2,512,128]{2,1,0:T(8,128)S(1)}, f32[2,512,128]{2,1,0:T(8,128)S(1)}, u32[]{:S(2)}, u32[]{:S(2)}) collective-permute-start(f32[2,512,128]{2,1,0:T(8,128)S(1)} %get-tuple-element.17), channel_id=1, source_target_pairs={{0,16},{16,32},{32,48},{48,64},{64,80},{80,96},{96,112},{1,17},{17... | collective-permute-start | bytes 1572872 | tf_op jit(solution)/shard_map/ppermute | solution.py:313
  77.0 0.0 collective-permute-done.3.high
  77.0 1.5 %collective-permute-done.2.low = f32[2,512,128]{2,1,0:T(8,128)S(1)} collective-permute-done((f32[2,512,128]{2,1,0:T(8,128)S(1)}, f32[2,512,128]{2,1,0:T(8,128)S(1)}, u32[]{:S(2)}, u32[]{:S(2)}) %collective-permute-start.2) | collective-permute-done | bytes 524320 | tf_op jit(solution)/shard_map/ppermute | solution.py:313
  78.5 8.9 %all-to-all-done.1 = f32[16,48,256]{2,1,0:T(8,128)S(1)} async-done(((f32[16,48,256]{2,1,0:T(8,128)}), f32[16,48,256]{2,1,0:T(8,128)S(1)}, u32[]{:S(2)}, u32[]{:S(2)}) %all-to-all-start.1) | async-done | bytes 786464 | tf_op jit(solution)/shard_map/all_to_all | solution.py:353
  87.3 3.4 %copy-done.2 = f32[2,32,128,256]{3,2,1,0:T(8,128)S(1)} copy-done((f32[2,32,128,256]{3,2,1,0:T(8,128)S(1)}, f32[2,32,128,256]{3,2,1,0:T(8,128)}, u32[]{:S(2)}) %copy-start.2) | copy-done | bytes 8388632
  90.7 14.0 %finish.1 = (f32[2,32,128,256]{3,2,1,0:T(8,128)}, f32[128,256]{1,0:T(8,128)}) custom-call(s32[1]{0:T(128)} %bitcast.pos, f32[3,32]{1,0:T(4,128)S(1)} %copy-done.5, f32[2,32,128,256]{3,2,1,0:T(8,128)S(1)} %copy-done.2, f32[768,256]{1,0:T(8,128)S(1)} %bitcast.17, f32[768,256]{1,0:T(8,128)S(1)} %bitcast.18, f32[2,512,128]{2,1,0:T(8,128)S(1)} %collective-permute-done.2.low, ...), custom_call_target="tpu_custom_call" | custom-call | tf_op jit(solution)/shard_map/finish/pallas_call | solution.py:355
  (1 shorter events, 0.0 us)
Async XLA Ops:
  1.3 3.4 %copy-start = (f32[64,8,16,256]{3,2,1,0:T(8,128)S(1)}, f32[64,8,16,256]{3,2,1,0:T(8,128)}, u32[]{:S(2)}) copy-start(f32[64,8,16,256]{3,2,1,0:T(8,128)} %param.10) | copy-start | bytes 25165828
  4.7 0.8 copy-start.3
  5.5 0.7 copy-start.4
  6.2 0.7 copy-start.7
  6.8 0.7 copy-start.9
  7.5 0.7 copy-start.11
  8.2 0.7 copy-start.13
  8.8 0.7 copy-start.15
  9.5 7.1 %copy-start.5 = (f32[3,32]{1,0:T(4,128)S(1)}, f32[3,32]{1,0:T(4,128)}, u32[]{:S(2)}) copy-start(f32[3,32]{1,0:T(4,128)} %dcs.5) | copy-start | bytes 1156
  9.5 8.3 %copy-start.6 = (f32[16,256]{1,0:T(8,128)S(1)}, f32[16,256]{1,0:T(8,128)}, u32[]{:S(2)}) copy-start(f32[16,256]{1,0:T(8,128)} %heat.1) | copy-start | bytes 49156
  9.5 8.3 %copy-start.8 = (f32[32]{0:T(128)S(1)}, f32[32]{0:T(128)}, u32[]{:S(2)}) copy-start(f32[32]{0:T(128)} %wts.5) | copy-start | bytes 388
  9.5 8.3 %copy-start.10 = (f32[32]{0:T(128)S(1)}, f32[32]{0:T(128)}, u32[]{:S(2)}) copy-start(f32[32]{0:T(128)} %param.12) | copy-start | bytes 388
  9.5 8.3 %copy-start.12 = (f32[32]{0:T(128)S(1)}, f32[32]{0:T(128)}, u32[]{:S(2)}) copy-start(f32[32]{0:T(128)} %param.13) | copy-start | bytes 388
  9.5 8.3 %copy-start.14 = (f32[32]{0:T(128)S(1)}, f32[32]{0:T(128)}, u32[]{:S(2)}) copy-start(f32[32]{0:T(128)} %param.14) | copy-start | bytes 388
  12.2 29.6 %collective-permute-start.1 = (f32[40,256]{1,0:T(8,128)S(1)}, f32[40,256]{1,0:T(8,128)S(1)}, u32[]{:S(2)}, u32[]{:S(2)}) collective-permute-start(f32[40,256]{1,0:T(8,128)S(1)} %get-tuple-element.14), channel_id=1, source_target_pairs={{16,0},{32,16},{48,32},{64,48},{80,64},{96,80},{112,96},{17,1},{33... | collective-permute-start | bytes 122888 | tf_op jit(solution)/shard_map/ppermute | solution.py:312
  13.5 28.4 %collective-permute-start = (f32[40,256]{1,0:T(8,128)S(1)}, f32[40,256]{1,0:T(8,128)S(1)}, u32[]{:S(2)}, u32[]{:S(2)}) collective-permute-start(f32[40,256]{1,0:T(8,128)S(1)} %get-tuple-element.14), channel_id=1, source_target_pairs={{0,16},{16,32},{32,48},{48,64},{64,80},{80,96},{96,112},{1,17},{17... | collective-permute-start | bytes 122888 | tf_op jit(solution)/shard_map/ppermute | solution.py:311
  38.5 3.4 %copy-start.1 = (f32[2,32,128,256]{3,2,1,0:T(8,128)}, f32[2,32,128,256]{3,2,1,0:T(8,128)S(1)}, u32[]{:S(2)}) copy-start(f32[2,32,128,256]{3,2,1,0:T(8,128)S(1)} %get-tuple-element.12.l0_ref) | copy-start | bytes 25165828
  68.8 18.5 %all-to-all-start.1 = ((f32[16,48,256]{2,1,0:T(8,128)}), f32[16,48,256]{2,1,0:T(8,128)S(1)}, u32[]{:S(2)}, u32[]{:S(2)}) async-start(f32[16,48,256]{2,1,0:T(8,128)} %middle.1), calls=%async_computation.1 | async-start | bytes 1572864 | tf_op jit(solution)/shard_map/all_to_all | solution.py:353
  72.6 4.4 %collective-permute-start.3 = (f32[2,512,128]{2,1,0:T(8,128)S(1)}, f32[2,512,128]{2,1,0:T(8,128)S(1)}, u32[]{:S(2)}, u32[]{:S(2)}) collective-permute-start(f32[2,512,128]{2,1,0:T(8,128)S(1)} %get-tuple-element.17), channel_id=1, source_target_pairs={{16,0},{32,16},{48,32},{64,48},{80,64},{96,80},{112,96},{17,1},{33... | collective-permute-start | bytes 1572872 | tf_op jit(solution)/shard_map/ppermute | solution.py:314
  73.9 4.6 %collective-permute-start.2 = (f32[2,512,128]{2,1,0:T(8,128)S(1)}, f32[2,512,128]{2,1,0:T(8,128)S(1)}, u32[]{:S(2)}, u32[]{:S(2)}) collective-permute-start(f32[2,512,128]{2,1,0:T(8,128)S(1)} %get-tuple-element.17), channel_id=1, source_target_pairs={{0,16},{16,32},{32,48},{48,64},{64,80},{80,96},{96,112},{1,17},{17... | collective-permute-start | bytes 1572872 | tf_op jit(solution)/shard_map/ppermute | solution.py:313
  87.3 3.4 %copy-start.2 = (f32[2,32,128,256]{3,2,1,0:T(8,128)S(1)}, f32[2,32,128,256]{3,2,1,0:T(8,128)}, u32[]{:S(2)}) copy-start(f32[2,32,128,256]{3,2,1,0:T(8,128)} %copy-done.1) | copy-start | bytes 25165828

commit v2 on v0

v2 whole, which is shorter than its diff:
```python
import jax
import jax.numpy as jnp
from jax import lax
from jax.experimental import pallas as pl
from jax.experimental.pallas import tpu as pltpu
from jax.sharding import PartitionSpec as P

PAIRS = 1024
DIRS = 32
MODES = 32
Z = 8
ROWS = 16
COLS = 256
GROUP = 16
PLANE = Z * ROWS
PACK = 48
STEP = 4
F32 = jnp.float32


def column(row):
    r = lax.broadcasted_iota(jnp.int32, (MODES, MODES), 0)
    c = lax.broadcasted_iota(jnp.int32, (MODES, MODES), 1)
    return jnp.sum(jnp.where(r == c, jnp.broadcast_to(row, (MODES, MODES)), 0.0), axis=1, keepdims=True)


ALPHA, BETA, GAMMA, KAPPA, SHARE, ETA = range(6)
CHUNK = 8 * PLANE
SMALL = 512


def edge_kernel(
    pos, cnt, x_hbm, dc_h, v_h, r_h, s_h, w_h, c_h, m_h,
    x_ref, e_ref, edge_ref, tab, par, jm_ref, k0_ref, flags,
    dcv, vel, rate, spec, wv, cells, rmap, acc, sems, xsems,
):
    k = pos[0]

    def chunk(c, h):
        rows = pl.ds(pl.multiple_of(c * CHUNK, CHUNK), CHUNK)
        return pltpu.make_async_copy(x_hbm.at[rows, pl.ds(h * 128, 128)], x_ref.at[h, rows, :], xsems.at[h, c])

    few = list(zip((dc_h, v_h, r_h, s_h, w_h, c_h, m_h), (dcv, vel, rate, spec, wv, cells, rmap)))
    few = [pltpu.make_async_copy(a, b, sems.at[n]) for n, (a, b) in enumerate(few)]
    for copy in few:
        copy.start()
    for c in range(8):
        for h in range(2):
            chunk(c, h).start()
    for copy in few:
        copy.wait()

    lane = lax.broadcasted_iota(jnp.int32, (1, DIRS), 1)

    def pick(row, at):
        return jnp.sum(jnp.where(lane == at, row, 0.0))

    cx, cy, cz = [pick(dcv[n : n + 1, :], 2 * k) for n in range(3)]
    cz = jnp.abs(cz)
    flags[0] = cx
    flags[1] = cy
    flags[2] = pick(wv[...], 2 * k)
    flags[3] = pick(wv[...], 2 * k + 1)
    v, a = column(vel[...]), 1.0 + column(rate[...])
    share, eta = column(spec[...]), column(rate[...]) * column(spec[...])
    inv = 1.0 / (a + v * cz)
    table = {
        ALPHA: (1.0 - v * jnp.abs(cx) - v * jnp.abs(cy)) * inv,
        BETA: v * jnp.abs(cx) * inv,
        GAMMA: v * jnp.abs(cy) * inv,
        KAPPA: v * cz * inv,
        SHARE: share,
        ETA: eta * inv,
    }
    for n, col in table.items():
        tab[n] = jnp.broadcast_to(col, (MODES, 128))
    acc[...] = jnp.zeros_like(acc)
    e_ref[...] = jnp.zeros_like(e_ref)

    slot = lax.broadcasted_iota(jnp.int32, (1, cells.shape[1]), 1)
    local = jnp.where(slot < cnt[0], cells[...] - k * COLS, -1)
    q = lax.broadcasted_iota(jnp.int32, (COLS, cells.shape[1]), 0)
    hot = jnp.where(q == local, 1.0, 0.0).astype(jnp.bfloat16)
    idx = (rmap[...] + 1).astype(F32).astype(jnp.bfloat16)
    jm_ref[...] = lax.dot_general(idx, hot, (((1,), (1,)), ((), ())), preferred_element_type=F32)

    c_all = v * jnp.abs(dcv[2:3, :])
    inv_all = 1.0 / (a + c_all)
    k_all = c_all * inv_all
    for n, block in enumerate((k_all, eta * inv_all, jnp.broadcast_to(wv[...], (MODES, DIRS)))):
        par[n, :, pl.ds(0, DIRS)] = block
    term = eta * inv_all * wv[...]
    odd = lax.broadcasted_iota(jnp.int32, (MODES, DIRS), 1) % 2 == 1
    zr = lax.broadcasted_iota(jnp.int32, (Z, 128), 0)
    zc = lax.broadcasted_iota(jnp.int32, (Z, 128), 1)
    total = jnp.zeros((Z, 128), F32)
    for n in range(Z):
        down = jnp.sum(jnp.sum(jnp.where(odd, term, 0.0), axis=1, keepdims=True), axis=0, keepdims=True)
        up = jnp.sum(jnp.sum(jnp.where(odd, 0.0, term), axis=1, keepdims=True), axis=0, keepdims=True)
        total += jnp.where(zc - zr == n, down, 0.0) + jnp.where(zr - zc == n, up, 0.0)
        term = term * k_all
    k0_ref[...] = total

    row = jnp.where(cx > 0.0, ROWS - 1, 0)

    def one(c, carry):
        w = flags[2 + c // 4]
        base = pl.multiple_of(c * CHUNK, CHUNK)
        m0 = pl.multiple_of(8 * (c % 4), 8)
        for h in range(2):
            chunk(c, h).wait()
            for t in range(PLANE // 8):
                part = x_ref[h, pl.ds(base + t * 8, 8), :]
                for p in range(1, 8):
                    part += x_ref[h, pl.ds(base + p * PLANE + t * 8, 8), :]
                e_ref[h, pl.ds(t * 8, 8), :] += w * part
            kp, bt = [tab[n, pl.ds(m0, 8), :] for n in (KAPPA, BETA)]
            rows = []
            for z in range(Z):
                e = x_ref[h, pl.ds(base + z * ROWS + row, 8, stride=PLANE), :]
                edge_ref[h, pl.ds(pl.multiple_of(z * 64 + 8 * c, 8), 8), :] = e
                rows.append(bt * e)

            @pl.when(c < 4)
            def _():
                t = rows[0]
                acc[h, pl.ds(0, 8), :] += w * t
                for z in range(1, Z):
                    t = kp * t + rows[z]
                    acc[h, pl.ds(8 * z, 8), :] += w * t

            @pl.when(c >= 4)
            def _():
                t = rows[Z - 1]
                acc[h, pl.ds(8 * (Z - 1), 8), :] += w * t
                for z in reversed(range(Z - 1)):
                    t = kp * t + rows[z]
                    acc[h, pl.ds(8 * z, 8), :] += w * t
                edge_ref[h, pl.ds(SMALL + 8 + m0, 8), :] = t

        return carry

    lax.fori_loop(0, 8, one, 0)
    for h in range(2):
        for z in range(Z):
            edge_ref[h, pl.ds(SMALL + z, 1), :] = jnp.sum(acc[h, pl.ds(8 * z, 8), :], axis=0, keepdims=True)


def sweep_kernel(
    flags, tab, x_ref, heat, l0_ref, e0_ref, d0, accd, accu,
):
    up_x, up_y = flags[0] > 0.0, flags[1] > 0.0
    accd[...] = jnp.zeros_like(accd)
    accu[...] = jnp.zeros_like(accu)

    def run(pos_x, pos_y):
        rows = (0, 8) if pos_x else (8, 0)
        cols = (0, 1) if pos_y else (1, 0)
        tiles = [(r, c) for r in rows for c in cols]
        sub = lax.broadcasted_iota(jnp.int32, (8, 128), 0) == (0 if pos_x else 7)
        lane = lax.broadcasted_iota(jnp.int32, (8, 128), 1) == (0 if pos_y else 127)

        def pair(i, carry):
            modes = [2 * i, 2 * i + 1]
            coef = [[jnp.broadcast_to(tab[n, pl.ds(m, 1), :], (8, 128)) for n in range(4)] for m in modes]

            def rhs(d, t, z):
                alpha, beta, gamma, _ = coef[t]
                at = pl.multiple_of((d * MODES + modes[t]) * PLANE, PLANE) + z * ROWS
                f = [[x_ref[c, pl.ds(at + r, 8), :] for c in cols] for r in rows]
                rx = [[pltpu.roll(v, 1 if pos_x else 7, 0) for v in vs] for vs in f]
                ry = [[pltpu.roll(v, 1 if pos_y else 127, 1) for v in vs] for vs in f]
                out = []
                for r in range(2):
                    for c in range(2):
                        x = jnp.where(sub, 0.0 if r == 0 else rx[0][c], rx[r][c])
                        y = jnp.where(lane, 0.0 if c == 0 else ry[r][0], ry[r][c])
                        out.append(alpha * f[r][c] + beta * x + gamma * y)
                return out

            for d, acc, order in ((1, accd, range(Z - 1, -1, -1)), (0, accu, range(Z))):
                if d == 1:
                    state = [
                        [jnp.broadcast_to(tab[4, pl.ds(m, 1), :], (8, 128)) * heat[pl.ds(r, 8), pl.ds(c * 128, 128)] for r, c in tiles]
                        for m in modes
                    ]
                else:
                    state = [None, None]
                for z in order:
                    for t in range(2):
                        f = rhs(d, t, z)
                        state[t] = f if state[t] is None else [a + coef[t][3] * b for a, b in zip(f, state[t])]
                        for v, (r, c) in zip(state[t], tiles):
                            l0_ref[d, modes[t], pl.ds(z * ROWS + r, 8), pl.ds(c * 128, 128)] = v
                    for n, (r, c) in enumerate(tiles):
                        acc[c, pl.ds(z * ROWS + r, 8), :] += state[0][n] + state[1][n]
                if d == 1:
                    for t in range(2):
                        for v, (r, c) in zip(state[t], tiles):
                            d0[c, pl.ds(pl.multiple_of(modes[t] * ROWS, ROWS) + r, 8), :] = v
            return carry

        lax.fori_loop(0, MODES // 2, pair, 0)

    for pos_x in (True, False):
        for pos_y in (True, False):
            pl.when((up_x == pos_x) & (up_y == pos_y))(lambda px=pos_x, py=pos_y: run(px, py))

    e0_ref[...] = flags[3] * accd[...] + flags[2] * accu[...]


def pack_kernel(flags, e_ref, e0_ref, d0, low, high, out):
    up_x = flags[0] > 0.0
    for h in range(2):
        at = pl.ds(h * 128, 128)
        for r in range(ROWS):
            more = None
            if r == 0:
                more = jnp.where(up_x, low[h, pl.ds(SMALL, 40), :], 0.0)
            if r == ROWS - 1:
                more = jnp.where(up_x, 0.0, high[h, pl.ds(SMALL, 40), :])
            out[pl.ds(r * PACK, 8), at] = e_ref[h, pl.ds(r, 8, stride=ROWS), :]
            for t in range(5):
                if t == 0:
                    part = e0_ref[h, pl.ds(r, 8, stride=ROWS), :]
                else:
                    part = d0[h, pl.ds((t - 1) * PLANE + r, 8, stride=ROWS), :]
                if more is not None:
                    part += more[8 * t : 8 * t + 8, :]
                out[pl.ds(r * PACK + 8 + 8 * t, 8), at] = part


def middle_kernel(got, par, jm_ref, k0_ref, out, q_ref):
    energy = got[0, 0:8, :]
    rest = got[0, 8:16, :]
    for s in range(1, GROUP):
        energy += got[s, 0:8, :]
        rest += got[s, 8:16, :]
    energy = energy * (1.0 / PAIRS)
    equil = energy / (1.0 + 0.3 * jnp.abs(energy))
    eq = [jnp.broadcast_to(equil[z : z + 1, :], (8, COLS)) for z in range(Z)]
    k_all, n_all, w_all = par[0], par[1], par[2]
    for j in range(GROUP):
        for t in range(MODES // 8):
            at = slice(8 * t, 8 * t + 8)
            kp = jnp.broadcast_to(k_all[at, 2 * j + 1 : 2 * j + 2], (8, COLS))
            eta = jnp.broadcast_to(n_all[at, 2 * j + 1 : 2 * j + 2], (8, COLS))
            s = eq[Z - 1]
            for z in reversed(range(Z - 1)):
                s = kp * s + eq[z]
            q_ref[j, at, :] = 0.9 * (got[j, 16 + 8 * t : 24 + 8 * t, :] + eta * s)
    acc = [jnp.zeros((8, COLS), F32) for _ in range(Z)]
    for k in range(GROUP):
        jm = jnp.broadcast_to(jm_ref[k : k + 1, :], (8, COLS))
        jm = jnp.where(jm < 0.5, float(k + 1), jm)
        near = [jnp.abs(jm - float(j + 1)) < 0.5 for j in range(GROUP)]
        w = jnp.broadcast_to(w_all[0:8, 2 * k : 2 * k + 1], (8, COLS))
        for t in range(MODES // 8):
            at = slice(8 * t, 8 * t + 8)
            pick = q_ref[0, at, :]
            for j in range(1, GROUP):
                pick = jnp.where(near[j], q_ref[j, at, :], pick)
            out[k, at, :] = pick
            kp = jnp.broadcast_to(k_all[at, 2 * k : 2 * k + 1], (8, COLS))
            pick = w * pick
            for z in range(Z):
                pick = kp * pick
                acc[z] += pick
    bounce = jnp.concatenate([jnp.sum(t, axis=0, keepdims=True) for t in acc], axis=0)
    fresh = rest + bounce
    for z in range(Z):
        fresh += jnp.broadcast_to(k0_ref[:, z : z + 1], (8, COLS)) * eq[z]
    fresh = fresh * (1.0 / PAIRS)
    for k in range(GROUP):
        out[k, 32:40, :] = equil
        out[k, 40:48, :] = fresh


def finish_kernel(
    flags, tab, l0_ref, left, right, low, high, out_hbm, en_ref, eq, res, sems,
):
    up_x = flags[0] > 0.0
    for z in range(Z):
        for h, back in enumerate((left, right)):
            for b in range(2):
                to = (pl.ds(z * ROWS + 8 * b, 8), pl.ds(h * 128, 128))
                eq[to] = back[pl.ds(8 * b * PACK + 32 + z, 8, stride=PACK), :]
                en_ref[to] = back[pl.ds(8 * b * PACK + 40 + z, 8, stride=PACK), :]

    def leave(g, d):
        part = pl.ds(g * STEP, STEP)
        return pltpu.make_async_copy(res.at[d, part], out_hbm.at[d, part], sems.at[d, g])

    def run(pos_x):
        edge = low if pos_x else high
        first = 0 if pos_x else 8
        sub = lax.broadcasted_iota(jnp.int32, (8, 128), 0) == (0 if pos_x else 7)

        def one(m, carry):
            eta, beta, kappa = [jnp.broadcast_to(tab[n, pl.ds(m, 1), :], (8, 128)) for n in (ETA, BETA, KAPPA)]
            for r in (0, 8):
                for h, back in enumerate((left, right)):
                    at = [(pl.ds(z * ROWS + r, 8), pl.ds(h * 128, 128)) for z in range(Z)]
                    src = [eta * eq[at[z]] for z in range(Z)]

                    def source(d, z):
                        if r != first:
                            return src[z]
                        e = jnp.broadcast_to(edge[h, pl.ds(z * 64 + d * 32 + m, 1), :], (8, 128))
                        return src[z] + jnp.where(sub, beta * e, 0.0)

                    t = None
                    for z in reversed(range(Z)):
                        t = source(1, z) if t is None else kappa * t + source(1, z)
                        res[(1, m) + at[z]] = l0_ref[(1, m) + at[z]] + t
                    t = back[pl.ds(r * PACK + m, 8, stride=PACK), :]
                    for z in range(Z):
                        t = kappa * t + source(0, z)
                        res[(0, m) + at[z]] = l0_ref[(0, m) + at[z]] + t
            return carry

        def some(g, carry):
            lax.fori_loop(g * STEP, g * STEP + STEP, one, 0)
            for d in range(2):
                leave(g, d).start()
            return carry

        lax.fori_loop(0, MODES // STEP, some, 0)

    pl.when(up_x)(lambda: run(True))
    pl.when(jnp.logical_not(up_x))(lambda: run(False))
    for g in range(MODES // STEP):
        for d in range(2):
            leave(g, d).wait()


def per_device(
    intensity, dir_cos, velocity, rate, spectrum, weight, heat, rough_cells, rough_count, rough_map
):
    pos = lax.axis_index("mode").astype(jnp.int32).reshape(1)
    slots = rough_cells.shape[0]
    smem = pl.BlockSpec(memory_space=pltpu.SMEM)
    vmem = pl.BlockSpec(memory_space=pltpu.VMEM)

    def hbm(x):
        return pltpu.with_memory_space_constraint(x, pltpu.HBM)

    anywhere = pl.BlockSpec(memory_space=pltpu.HBM)
    field = (2, MODES, PLANE, COLS)
    ones = [t.reshape(1, -1) for t in (velocity, rate, spectrum, weight, rough_cells)]
    x, energy, edge, tab, par, jm, k0, flags = pl.pallas_call(
        edge_kernel,
        in_specs=[smem] * 2 + [anywhere] * 8,
        out_specs=[vmem] * 7 + [smem],
        out_shape=[
            pltpu.VMEM(s, F32)
            for s in (
                (2, 64 * PLANE, 128), (2, PLANE, 128), (2, SMALL + 40, 128), (6, MODES, 128), (3, MODES, 128),
                (GROUP, COLS), (Z, 128),
            )
        ]
        + [pltpu.SMEM((4,), F32)],
        scratch_shapes=[
            pltpu.VMEM((3, DIRS), F32),
            pltpu.VMEM((1, MODES), F32),
            pltpu.VMEM((1, MODES), F32),
            pltpu.VMEM((1, MODES), F32),
            pltpu.VMEM((1, DIRS), F32),
            pltpu.VMEM((1, slots), jnp.int32),
            pltpu.VMEM((GROUP, slots), jnp.int32),
            pltpu.VMEM((2, 64, 128), F32),
            pltpu.SemaphoreType.DMA((7,)),
            pltpu.SemaphoreType.DMA((2, 8)),
        ],
        compiler_params=pltpu.CompilerParams(vmem_limit_bytes=8 << 20),
        cost_estimate=pl.CostEstimate(flops=4 << 20, bytes_accessed=8 << 20, transcendentals=0),
        name="edges",
    )(
        pos, rough_count, hbm(intensity.reshape(64 * PLANE, COLS)), hbm(dir_cos), *[hbm(t) for t in ones], hbm(rough_map.T),
    )
    count = lax.axis_size("space")
    forward = [(i, i + 1) for i in range(count - 1)]
    backward = [(t, s) for s, t in forward]
    low = lax.ppermute(edge, "space", forward)
    high = lax.ppermute(edge, "space", backward)

    base, e0, d0 = pl.pallas_call(
        sweep_kernel,
        in_specs=[smem] + [vmem] * 3,
        out_specs=[vmem] * 3,
        out_shape=[pltpu.VMEM(s, F32) for s in (field, (2, PLANE, 128), (2, MODES * ROWS, 128))],
        scratch_shapes=[pltpu.VMEM((2, PLANE, 128), F32), pltpu.VMEM((2, PLANE, 128), F32)],
        compiler_params=pltpu.CompilerParams(vmem_limit_bytes=8 << 20),
        cost_estimate=pl.CostEstimate(flops=30 << 20, bytes_accessed=16 << 20, transcendentals=0),
        name="sweep",
    )(flags, tab, x, heat)

    pack = pl.pallas_call(
        pack_kernel,
        in_specs=[smem] + [vmem] * 5,
        out_specs=vmem,
        out_shape=pltpu.VMEM((ROWS * PACK, COLS), F32),
        compiler_params=pltpu.CompilerParams(vmem_limit_bytes=8 << 20),
        name="pack",
    )(flags, energy, e0, d0, low, high)
    got = lax.all_to_all(pack.reshape(GROUP, PACK, COLS), "mode", 0, 0, tiled=True)

    reply = pl.pallas_call(
        middle_kernel,
        in_specs=[vmem] * 4,
        out_specs=vmem,
        out_shape=pltpu.VMEM((GROUP, PACK, COLS), F32),
        scratch_shapes=[pltpu.VMEM((GROUP, MODES, COLS), F32)],
        compiler_params=pltpu.CompilerParams(vmem_limit_bytes=8 << 20),
        name="middle",
    )(got, par, jm, k0)
    back = lax.all_to_all(reply, "mode", 0, 0, tiled=True).reshape(GROUP * PACK, COLS)

    fresh, energy_new = pl.pallas_call(
        finish_kernel,
        grid=(1,),
        in_specs=[smem, vmem, vmem]
        + [pl.BlockSpec((GROUP * PACK, 128), lambda i, h=h: (0, h)) for h in range(2)]
        + [vmem] * 2,
        out_specs=[anywhere, vmem],
        out_shape=[pltpu.HBM(field, F32), jax.ShapeDtypeStruct((PLANE, COLS), F32)],
        scratch_shapes=[
            pltpu.VMEM((PLANE, COLS), F32),
            pltpu.VMEM(field, F32),
            pltpu.SemaphoreType.DMA((2, MODES // STEP)),
        ],
        compiler_params=pltpu.CompilerParams(vmem_limit_bytes=20 << 20),
        name="finish",
    )(flags, tab, base, back, back, low, high)
    return fresh.reshape(intensity.shape), energy_new.reshape(Z, ROWS, COLS)


def solution(mesh):
    in_specs = (
        P("mode", None, "space", None),
        P(),
        P(),
        P(),
        P(),
        P(),
        P("space", None),
        P("space"),
        P("space"),
        P("space", None),
    )
    out_specs = (P("mode", None, "space", None), P(None, "space", None))
    return jax.shard_map(
        per_device, mesh=mesh, in_specs=in_specs, out_specs=out_specs, check_vma=False
    )
```

time: 390 us -> 62.4 us (0.16)
  the two profiles are of different devices: /device:TPU:0 before, /device:TPU:8 now
where the time goes in v2:
time: 62.4 us; the launch traced here: 62.2 us
  blocking collectives  36.9 us (59%)
  Pallas kernels  14.6 us (23%)
  waiting for transfers between devices  4.97 us (8%)
  starting transfers between devices  4.33 us (7%)
  between operations  1.35 us (2%)
    all_to_all x1, blocking collectives, per_device(): lax.all_to_all(pack.reshape(GROUP, PACK, COLS), 'mode', 0, 0, tiled=True)  21.2 us
    all_to_all x1, blocking collectives, per_device(): lax.all_to_all(reply, 'mode', 0, 0, tiled=True).reshape(GROUP * PACK, COLS)  15.7 us
    pallas_call x1, Pallas kernels, per_device(): pl.pallas_call(edge_kernel, in_specs=[smem] * 2 + [anywhere] * 8, out_spe...  4.84 us
    pallas_call x1, Pallas kernels, per_device(): pl.pallas_call(finish_kernel, grid=(1,), in_specs=[smem, vmem, vmem] + [p...  4.44 us
    ppermute x1, waiting for transfers between devices, per_device(): low = lax.ppermute(edge, 'space', forward)  3.82 us
    pallas_call x1, Pallas kernels, per_device(): pl.pallas_call(sweep_kernel, in_specs=[smem] + [vmem] * 3, out_specs=[vme...  3.54 us
    ppermute x1, starting transfers between devices, per_device(): low = lax.ppermute(edge, 'space', forward)  2.41 us
    ppermute x1, starting transfers between devices, per_device(): high = lax.ppermute(edge, 'space', backward)  1.92 us
  transfers between devices with their start and end apart: 2, of which 2 were waited for; matrix products, arithmetic and copies ran while one was open for 0% of the time, Pallas kernels for 6%

profile of v2, /device:TPU:8, one launch (start us, length us, event | category | flops | bytes accessed | tf_op | source)
XLA Modules:
  0.0 62.2 jit_solution(18369833298569009900)
XLA Ops:
  0.6 0.0 copy-start
  1.3 4.8 %edges.1 = (f32[2,8192,128]{2,1,0:T(8,128)S(1)}, f32[2,128,128]{2,1,0:T(8,128)S(1)}, f32[2,552,128]{2,1,0:T(8,128)S(1)}, f32[6,32,128]{2,1,0:T(8,128)S(1)}, f32[...) custom-call(s32[1]{0:T(128)} %bitcast.pos, s32[1]{0:T(128)S(6)} %copy.12.cnt, ...), custom_call_target="tpu_custom_call" | custom-call | flops 4194304 | bytes 8388608 | tf_op jit(solution)/shard_map/edges/pallas_call | solution.py:351
  6.2 1.9 %collective-permute-start.1 = (f32[2,552,128]{2,1,0:T(8,128)S(1)}, f32[2,552,128]{2,1,0:T(8,128)S(1)}, u32[]{:S(2)}, u32[]{:S(2)}) collective-permute-start(f32[2,552,128]{2,1,0:T(8,128)S(1)} %get-tuple-element.22), channel_id=1, source_target_pairs={{16,0},{32,16},{48,32},{64,48},{80,64},{96,80},{112,96},{17,1},{33... | collective-permute-start | bytes 1695752 | tf_op jit(solution)/shard_map/ppermute | solution.py:385
  8.1 2.4 %collective-permute-start = (f32[2,552,128]{2,1,0:T(8,128)S(1)}, f32[2,552,128]{2,1,0:T(8,128)S(1)}, u32[]{:S(2)}, u32[]{:S(2)}) collective-permute-start(f32[2,552,128]{2,1,0:T(8,128)S(1)} %get-tuple-element.22), channel_id=1, source_target_pairs={{0,16},{16,32},{32,48},{48,64},{64,80},{80,96},{96,112},{1,17},{17... | collective-permute-start | bytes 1695752 | tf_op jit(solution)/shard_map/ppermute | solution.py:384
  10.5 0.0 copy-done
  10.5 3.5 %sweep.1 = (f32[2,32,128,256]{3,2,1,0:T(8,128)S(1)}, f32[2,128,128]{2,1,0:T(8,128)S(1)}, f32[2,512,128]{2,1,0:T(8,128)S(1)}) custom-call(f32[4]{0:T(128)S(4)} %get-tuple-element.15.flags, f32[6,32,128]{2,1,0:T(8,128)S(1)} %get-tuple-element.16.tab, f32[2,8192,128]{2,1,0:T(8,128)S(1)} %get-tuple-element.17.x_ref, f32[16,256]{1,0:T(8,128)S(1)} %copy-done), custom_call_target="tpu_custom_call" | custom-call | flops 31457280 | bytes 16777216 | tf_op jit(solution)/shard_map/sweep/pallas_call | solution.py:387
  14.1 1.1 %collective-permute-done.1.high = f32[2,552,128]{2,1,0:T(8,128)S(1)} collective-permute-done((f32[2,552,128]{2,1,0:T(8,128)S(1)}, f32[2,552,128]{2,1,0:T(8,128)S(1)}, u32[]{:S(2)}, u32[]{:S(2)}) %collective-permute-start.1) | collective-permute-done | bytes 565280 | tf_op jit(solution)/shard_map/ppermute | solution.py:385
  15.2 3.8 %collective-permute-done.low = f32[2,552,128]{2,1,0:T(8,128)S(1)} collective-permute-done((f32[2,552,128]{2,1,0:T(8,128)S(1)}, f32[2,552,128]{2,1,0:T(8,128)S(1)}, u32[]{:S(2)}, u32[]{:S(2)}) %collective-permute-start) | collective-permute-done | bytes 565280 | tf_op jit(solution)/shard_map/ppermute | solution.py:384
  19.0 0.3 pack.1
  19.3 21.2 %all_to_all.10.got = f32[16,48,256]{2,1,0:T(8,128)S(1)} all-to-all(f32[16,48,256]{2,1,0:T(8,128)S(1)} %bitcast.14), channel_id=1, replica_groups=mesh['space'=8,'mode'=16] {'mode'}, dimensions={0} | all-to-all | bytes 1572864 | tf_op jit(solution)/shard_map/all_to_all | solution.py:406
  40.4 1.5 %middle.1 = f32[16,48,256]{2,1,0:T(8,128)S(1)} custom-call(f32[16,48,256]{2,1,0:T(8,128)S(1)} %all_to_all.10.got, f32[3,32,128]{2,1,0:T(8,128)S(1)} %get-tuple-element.23.par, f32[16,256]{1,0:T(8,128)S(1)} %get-tuple-element.24.jm_ref, f32[8,128]{1,0:T(8,128)S(1)} %get-tuple-element.25.k0_ref), custom_call_target="tpu_custom_call" | custom-call | tf_op jit(solution)/shard_map/middle/pallas_call | solution.py:408
  42.0 15.7 %all_to_all.11 = f32[16,48,256]{2,1,0:T(8,128)S(1)} all-to-all(f32[16,48,256]{2,1,0:T(8,128)S(1)} %middle.1), channel_id=1, replica_groups=mesh['space'=8,'mode'=16] {'mode'}, dimensions={0} | all-to-all | bytes 1572864 | tf_op jit(solution)/shard_map/all_to_all | solution.py:417
  57.7 4.4 %finish.1 = (f32[2,32,128,256]{3,2,1,0:T(8,128)}, f32[128,256]{1,0:T(8,128)}) custom-call(f32[4]{0:T(128)S(4)} %get-tuple-element.15.flags, f32[6,32,128]{2,1,0:T(8,128)S(1)} %get-tuple-element.16.tab, f32[2,32,128,256]{3,2,1,0:T(8,128)S(1)} %get-tuple-element.18.l0_ref, f32[768,256]{1,0:T(8,128)S(1)} %bitcast.12, f32[768,256]{1,0:T(8,128)S(1)} %bitcast.13, ...), custom_call_target="tpu_custom_call" | custom-call | tf_op jit(solution)/shard_map/finish/pallas_call | solution.py:419
Async XLA Ops:
  0.6 9.9 %copy-start = (f32[16,256]{1,0:T(8,128)S(1)}, f32[16,256]{1,0:T(8,128)}, u32[]{:S(2)}) copy-start(f32[16,256]{1,0:T(8,128)} %heat.1) | copy-start | bytes 49156
  6.2 9.0 %collective-permute-start.1 = (f32[2,552,128]{2,1,0:T(8,128)S(1)}, f32[2,552,128]{2,1,0:T(8,128)S(1)}, u32[]{:S(2)}, u32[]{:S(2)}) collective-permute-start(f32[2,552,128]{2,1,0:T(8,128)S(1)} %get-tuple-element.22), channel_id=1, source_target_pairs={{16,0},{32,16},{48,32},{64,48},{80,64},{96,80},{112,96},{17,1},{33... | collective-permute-start | bytes 1695752 | tf_op jit(solution)/shard_map/ppermute | solution.py:385
  8.1 10.9 %collective-permute-start = (f32[2,552,128]{2,1,0:T(8,128)S(1)}, f32[2,552,128]{2,1,0:T(8,128)S(1)}, u32[]{:S(2)}, u32[]{:S(2)}) collective-permute-start(f32[2,552,128]{2,1,0:T(8,128)S(1)} %get-tuple-element.22), channel_id=1, source_target_pairs={{0,16},{16,32},{32,48},{48,64},{64,80},{80,96},{96,112},{1,17},{17... | collective-permute-start | bytes 1695752 | tf_op jit(solution)/shard_map/ppermute | solution.py:384

commit v3 on v2

--- a/solution.py
+++ b/solution.py
@@ -13,7 +13,9 @@
 COLS = 256
 GROUP = 16
 PLANE = Z * ROWS
-PACK = 48
+SEND = 24
+BACK = 32
+SLOTS = 1024
 STEP = 4
 F32 = jnp.float32
 
@@ -26,21 +28,22 @@
 
 ALPHA, BETA, GAMMA, KAPPA, SHARE, ETA = range(6)
 CHUNK = 8 * PLANE
-SMALL = 512
+EDGE = 512
 
 
 def edge_kernel(
-    pos, cnt, x_hbm, dc_h, v_h, r_h, s_h, w_h, c_h, m_h,
-    x_ref, e_ref, edge_ref, tab, par, jm_ref, k0_ref, flags,
-    dcv, vel, rate, spec, wv, cells, rmap, acc, sems, xsems,
+    x_hbm, dc_h, v_h, r_h, s_h, w_h,
+    x_ref, e_ref, edge_ref, tab, flags,
+    dcv, vel, rate, spec, wv, acc, sems, xsems,
 ):
-    k = pos[0]
+    k = lax.axis_index("mode")
+    odd_row = lax.axis_index("space") % 2 == 1
 
     def chunk(c, h):
         rows = pl.ds(pl.multiple_of(c * CHUNK, CHUNK), CHUNK)
         return pltpu.make_async_copy(x_hbm.at[rows, pl.ds(h * 128, 128)], x_ref.at[h, rows, :], xsems.at[h, c])
 
-    few = list(zip((dc_h, v_h, r_h, s_h, w_h, c_h, m_h), (dcv, vel, rate, spec, wv, cells, rmap)))
+    few = list(zip((dc_h, v_h, r_h, s_h, w_h), (dcv, vel, rate, spec, wv)))
     few = [pltpu.make_async_copy(a, b, sems.at[n]) for n, (a, b) in enumerate(few)]
     for copy in few:
         copy.start()
@@ -61,6 +64,7 @@
     flags[1] = cy
     flags[2] = pick(wv[...], 2 * k)
     flags[3] = pick(wv[...], 2 * k + 1)
+    flags[4] = jnp.where((cx > 0.0) == odd_row, 1.0, 0.0)
     v, a = column(vel[...]), 1.0 + column(rate[...])
     share, eta = column(spec[...]), column(rate[...]) * column(spec[...])
     inv = 1.0 / (a + v * cz)
@@ -76,30 +80,6 @@
         tab[n] = jnp.broadcast_to(col, (MODES, 128))
     acc[...] = jnp.zeros_like(acc)
     e_ref[...] = jnp.zeros_like(e_ref)
-
-    slot = lax.broadcasted_iota(jnp.int32, (1, cells.shape[1]), 1)
-    local = jnp.where(slot < cnt[0], cells[...] - k * COLS, -1)
-    q = lax.broadcasted_iota(jnp.int32, (COLS, cells.shape[1]), 0)
-    hot = jnp.where(q == local, 1.0, 0.0).astype(jnp.bfloat16)
-    idx = (rmap[...] + 1).astype(F32).astype(jnp.bfloat16)
-    jm_ref[...] = lax.dot_general(idx, hot, (((1,), (1,)), ((), ())), preferred_element_type=F32)
-
-    c_all = v * jnp.abs(dcv[2:3, :])
-    inv_all = 1.0 / (a + c_all)
-    k_all = c_all * inv_all
-    for n, block in enumerate((k_all, eta * inv_all, jnp.broadcast_to(wv[...], (MODES, DIRS)))):
-        par[n, :, pl.ds(0, DIRS)] = block
-    term = eta * inv_all * wv[...]
-    odd = lax.broadcasted_iota(jnp.int32, (MODES, DIRS), 1) % 2 == 1
-    zr = lax.broadcasted_iota(jnp.int32, (Z, 128), 0)
-    zc = lax.broadcasted_iota(jnp.int32, (Z, 128), 1)
-    total = jnp.zeros((Z, 128), F32)
-    for n in range(Z):
-        down = jnp.sum(jnp.sum(jnp.where(odd, term, 0.0), axis=1, keepdims=True), axis=0, keepdims=True)
-        up = jnp.sum(jnp.sum(jnp.where(odd, 0.0, term), axis=1, keepdims=True), axis=0, keepdims=True)
-        total += jnp.where(zc - zr == n, down, 0.0) + jnp.where(zr - zc == n, up, 0.0)
-        term = term * k_all
-    k0_ref[...] = total
 
     row = jnp.where(cx > 0.0, ROWS - 1, 0)
 
@@ -136,14 +116,14 @@
                 for z in reversed(range(Z - 1)):
                     t = kp * t + rows[z]
                     acc[h, pl.ds(8 * z, 8), :] += w * t
-                edge_ref[h, pl.ds(SMALL + 8 + m0, 8), :] = t
+                edge_ref[h, pl.ds(EDGE + 8 + m0, 8), :] = t
 
         return carry
 
     lax.fori_loop(0, 8, one, 0)
     for h in range(2):
         for z in range(Z):
-            edge_ref[h, pl.ds(SMALL + z, 1), :] = jnp.sum(acc[h, pl.ds(8 * z, 8), :], axis=0, keepdims=True)
+            edge_ref[h, pl.ds(EDGE + z, 1), :] = jnp.sum(acc[h, pl.ds(8 * z, 8), :], axis=0, keepdims=True)
 
 
 def sweep_kernel(
@@ -209,28 +189,137 @@
     e0_ref[...] = flags[3] * accd[...] + flags[2] * accu[...]
 
 
-def pack_kernel(flags, e_ref, e0_ref, d0, low, high, out):
+def split(x):
+    high = x.astype(jnp.bfloat16)
+    return high, (x - high.astype(F32)).astype(jnp.bfloat16)
+
+
+def spread(x, hot):
+    high, low = split(x)
+    dims = (((1,), (1,)), ((), ()))
+    return lax.dot_general(high, hot, dims, preferred_element_type=F32) + lax.dot_general(
+        low, hot, dims, preferred_element_type=F32
+    )
+
+
+def slot_kernel(
+    cnt, flags, dcv, vel, rate, spec, wv, cells, rmap, tab, d0, e0_in,
+    hot_ref, rm_ref, par, jm_ref, k0_ref, mt_ref, cz_ref, ksel, nsel, slot_ref, e0_ref, parts,
+):
+    k = lax.axis_index("mode")
+    live = lax.broadcasted_iota(jnp.int32, (1, SLOTS), 1) < cnt[0]
+    q = lax.broadcasted_iota(jnp.int32, (COLS, SLOTS), 0)
+    hot_ref[...] = jnp.where(q == jnp.where(live, cells[...] & (COLS - 1), -1), 1.0, 0.0).astype(jnp.bfloat16)
+    hot = hot_ref[...]
+    cell_row = jnp.where(live, cells[...] >> 8, -1)
+    rows = lax.broadcasted_iota(jnp.int32, (ROWS, SLOTS), 0)
+    rm = jnp.where(rows == cell_row, 1.0, 0.0)
+    rm_ref[...] = rm
+    idx = jnp.where(cell_row == k, (rmap[...] + 1).astype(F32), 0.0).astype(jnp.bfloat16)
+    jm_ref[...] = lax.dot_general(idx, hot, (((1,), (1,)), ((), ())), preferred_element_type=F32)
+    mt_ref[...] = rmap[:, pl.ds(pl.multiple_of(128 * (k % 8), 128), 128)].astype(F32)
+    mine = jnp.sum(jnp.where(rows == k, rmap[...], 0), axis=0, keepdims=True)
+    czr = jnp.zeros((1, SLOTS), F32)
+    for j in range(GROUP):
+        czr = jnp.where(mine == j, jnp.abs(dcv[2:3, 2 * j : 2 * j + 1]), czr)
+    cz_ref[...] = spread(rm * czr, hot)
+
+    v, a = column(vel[...]), 1.0 + column(rate[...])
+    eta = column(rate[...]) * column(spec[...])
+    c_all = v * jnp.abs(dcv[2:3, :])
+    inv_all = 1.0 / (a + c_all)
+    k_all = c_all * inv_all
+    for n, block in enumerate((k_all, eta * inv_all, jnp.broadcast_to(wv[...], (MODES, DIRS)))):
+        par[n, :, pl.ds(0, DIRS)] = block
+    term = eta * inv_all * wv[...]
+    odd = lax.broadcasted_iota(jnp.int32, (MODES, DIRS), 1) % 2 == 1
+    zr = lax.broadcasted_iota(jnp.int32, (Z, 128), 0)
+    zc = lax.broadcasted_iota(jnp.int32, (Z, 128), 1)
+    total = jnp.zeros((Z, 128), F32)
+    for n in range(Z):
+        down = jnp.sum(jnp.sum(jnp.where(odd, term, 0.0), axis=1, keepdims=True), axis=0, keepdims=True)
+        up = jnp.sum(jnp.sum(jnp.where(odd, 0.0, term), axis=1, keepdims=True), axis=0, keepdims=True)
+        total += jnp.where(zc - zr == n, down, 0.0) + jnp.where(zr - zc == n, up, 0.0)
+        term = term * k_all
+    k0_ref[...] = total
+
+    vb, ab, nb = [jnp.broadcast_to(t, (MODES, 128)) for t in (v, a, 0.9 * eta)]
+    for h in range(2):
+        for r in (0, 8):
+            cz = cz_ref[pl.ds(r, 8), pl.ds(h * 128, 128)]
+            gain = jnp.where(cz < 0.1, 0.9 * flags[2], 0.0)
+            acc = [jnp.zeros((8, 128), F32) for _ in range(Z)]
+            for m in range(MODES):
+                at = pl.ds(m * ROWS + r, 8)
+                c = vb[m : m + 1, :] * cz
+                inv = 1.0 / (ab[m : m + 1, :] + c)
+                ksel[h, at, :] = c * inv
+                nsel[h, at, :] = nb[m : m + 1, :] * inv
+                f = gain * d0[h, at, :]
+                kp = jnp.broadcast_to(tab[KAPPA, pl.ds(m, 1), :], (8, 128))
+                for z in range(Z):
+                    f = kp * f
+                    acc[z] += f
+            for z in range(Z):
+                at = pl.ds(z * ROWS + r, 8)
+                e0_ref[h, at, :] = e0_in[h, at, :] + acc[z]
+
+    for r in range(ROWS):
+        for t in range(2):
+            x = jnp.concatenate(
+                [
+                    jnp.concatenate([d0[h, pl.ds((2 * t + u) * PLANE + r, 8, stride=ROWS), :] for h in range(2)], axis=1)
+                    for u in range(2)
+                ],
+                axis=0,
+            )
+            high, low = split(x)
+            parts[0, pl.ds(r * MODES + 16 * t, 16), :] = high
+            parts[1, pl.ds(r * MODES + 16 * t, 16), :] = low
+    for n in range(SLOTS // 256):
+        at = pl.ds(n * 256, 256)
+        got = jnp.dot(parts[0], hot_ref[:, at], preferred_element_type=F32)
+        got += jnp.dot(parts[1], hot_ref[:, at], preferred_element_type=F32)
+        total = rm[0:1, n * 256 : n * 256 + 256] * got[0:MODES]
+        for r in range(1, ROWS):
+            total += rm[r : r + 1, n * 256 : n * 256 + 256] * got[r * MODES : (r + 1) * MODES]
+        slot_ref[:, at] = total
+
+
+def pack_kernel(flags, tab, e_ref, e0_ref, slot_ref, hot, rm, cz_ref, chip, next_chip, out):
     up_x = flags[0] > 0.0
+    delta = [jnp.where(flags[4] > 0.5, chip[h, pl.ds(EDGE, 40), :], next_chip[h, pl.ds(EDGE, 40), :]) for h in range(2)]
+    extra = []
     for h in range(2):
-        at = pl.ds(h * 128, 128)
-        for r in range(ROWS):
-            more = None
+        at = slice(h * 128, h * 128 + 128)
+        cz = jnp.where(up_x, cz_ref[0:1, at], cz_ref[ROWS - 1 : ROWS, at])
+        gain = jnp.broadcast_to(jnp.where(cz < 0.1, 0.9 * flags[2], 0.0), (8, 128))
+        acc = [jnp.zeros((8, 128), F32) for _ in range(Z)]
+        for t in range(MODES // 8):
+            f = gain * delta[h][8 + 8 * t : 16 + 8 * t, :]
+            for z in range(Z):
+                f = tab[KAPPA, pl.ds(8 * t, 8), :] * f
+                acc[z] += f
+        extra.append(delta[h][0:8, :] + jnp.concatenate([jnp.sum(t, axis=0, keepdims=True) for t in acc], axis=0))
+    high, low = split(jnp.concatenate([d[8:40, :] for d in delta], axis=1))
+    more = jnp.dot(jnp.concatenate([high, low], axis=0), hot[...], preferred_element_type=F32)
+    mask = jnp.where(up_x, rm[0:1, :], rm[ROWS - 1 : ROWS, :])
+    slots = slot_ref[...] + mask * (more[0:MODES, :] + more[MODES : 2 * MODES, :])
+    for r in range(ROWS):
+        tile, low_mode = (r % 8) * 128, 16 * (r // 8)
+        for h in range(2):
+            at = pl.ds(h * 128, 128)
+            part = e0_ref[h, pl.ds(r, 8, stride=ROWS), :]
             if r == 0:
-                more = jnp.where(up_x, low[h, pl.ds(SMALL, 40), :], 0.0)
+                part += jnp.where(up_x, extra[h], 0.0)
             if r == ROWS - 1:
-                more = jnp.where(up_x, 0.0, high[h, pl.ds(SMALL, 40), :])
-            out[pl.ds(r * PACK, 8), at] = e_ref[h, pl.ds(r, 8, stride=ROWS), :]
-            for t in range(5):
-                if t == 0:
-                    part = e0_ref[h, pl.ds(r, 8, stride=ROWS), :]
-                else:
-                    part = d0[h, pl.ds((t - 1) * PLANE + r, 8, stride=ROWS), :]
-                if more is not None:
-                    part += more[8 * t : 8 * t + 8, :]
-                out[pl.ds(r * PACK + 8 + 8 * t, 8), at] = part
-
-
-def middle_kernel(got, par, jm_ref, k0_ref, out, q_ref):
+                part += jnp.where(up_x, 0.0, extra[h])
+            out[pl.ds(r * SEND, 8), at] = e_ref[h, pl.ds(r, 8, stride=ROWS), :]
+            out[pl.ds(r * SEND + 8, 8), at] = part
+            out[pl.ds(r * SEND + 16, 8), at] = slots[low_mode + 8 * h : low_mode + 8 * h + 8, tile : tile + 128]
+
+
+def middle_kernel(got, par, jm_ref, k0_ref, mt_ref, out, q_ref):
     energy = got[0, 0:8, :]
     rest = got[0, 8:16, :]
     for s in range(1, GROUP):
@@ -248,7 +337,7 @@
             s = eq[Z - 1]
             for z in reversed(range(Z - 1)):
                 s = kp * s + eq[z]
-            q_ref[j, at, :] = 0.9 * (got[j, 16 + 8 * t : 24 + 8 * t, :] + eta * s)
+            q_ref[j, at, :] = (0.9 * eta) * s
     acc = [jnp.zeros((8, COLS), F32) for _ in range(Z)]
     for k in range(GROUP):
         jm = jnp.broadcast_to(jm_ref[k : k + 1, :], (8, COLS))
@@ -260,47 +349,91 @@
             pick = q_ref[0, at, :]
             for j in range(1, GROUP):
                 pick = jnp.where(near[j], q_ref[j, at, :], pick)
-            out[k, at, :] = pick
             kp = jnp.broadcast_to(k_all[at, 2 * k : 2 * k + 1], (8, COLS))
             pick = w * pick
             for z in range(Z):
                 pick = kp * pick
                 acc[z] += pick
     bounce = jnp.concatenate([jnp.sum(t, axis=0, keepdims=True) for t in acc], axis=0)
+    first = pl.multiple_of(16 * (lax.axis_index("mode") // 8), 16)
+    acc = [jnp.zeros((8, COLS), F32) for _ in range(Z)]
+    for k in range(GROUP):
+        index = jnp.concatenate([jnp.broadcast_to(mt_ref[k : k + 1, :], (8, 128))] * 2, axis=1)
+        pick = got[0, 16:24, :]
+        for j in range(1, GROUP):
+            pick = jnp.where(index > j - 0.5, got[j, 16:24, :], pick)
+        pick = 0.9 * pick
+        out[k, 0:8, :] = pick
+        kp = jnp.concatenate(
+            [jnp.broadcast_to(par[0, pl.ds(first + 8 * u, 8), pl.ds(0, 128)][:, 2 * k : 2 * k + 1], (8, 128)) for u in range(2)],
+            axis=1,
+        )
+        pick = jnp.broadcast_to(w_all[0:8, 2 * k : 2 * k + 1], (8, COLS)) * pick
+        for z in range(Z):
+            pick = kp * pick
+            acc[z] += pick
+    sums = [jnp.sum(t, axis=0, keepdims=True) for t in acc]
+    at_slots = jnp.concatenate([t[:, 0:128] + t[:, 128:256] for t in sums], axis=0) * (1.0 / PAIRS)
+    at_slots = jnp.concatenate([at_slots, jnp.zeros((Z, 128), F32)], axis=1)
     fresh = rest + bounce
     for z in range(Z):
         fresh += jnp.broadcast_to(k0_ref[:, z : z + 1], (8, COLS)) * eq[z]
     fresh = fresh * (1.0 / PAIRS)
     for k in range(GROUP):
-        out[k, 32:40, :] = equil
-        out[k, 40:48, :] = fresh
+        out[k, 8:16, :] = equil
+        out[k, 16:24, :] = fresh
+        out[k, 24:32, :] = at_slots
 
 
 def finish_kernel(
-    flags, tab, l0_ref, left, right, low, high, out_hbm, en_ref, eq, res, sems,
+    flags, tab, l0_ref, left, right, hot_ref, rm_ref, cz_ref, ksel, nsel, chip, next_chip,
+    out_hbm, en_ref, eq, res, cell, grid_en, sems,
 ):
     up_x = flags[0] > 0.0
+    hot = hot_ref[...]
+    picked = [
+        jnp.concatenate([back[pl.ds((8 * half + t) * BACK, 8), :] for t in range(8)], axis=1)
+        for half in range(2) for back in (left, right)
+    ]
+    heard = jnp.concatenate(
+        [left[pl.ds(t * BACK + 24, 8), :] + left[pl.ds((8 + t) * BACK + 24, 8), :] for t in range(8)], axis=1
+    )
+    for part in range(4):
+        lhs = []
+        for r in range(4 * part, 4 * part + 4):
+            lhs += [rm_ref[r : r + 1, :] * t for t in picked + [heard]]
+        got = spread(jnp.concatenate(lhs, axis=0), hot)
+        for n, r in enumerate(range(4 * part, 4 * part + 4)):
+            for h, back in enumerate((left, right)):
+                cell[h, pl.ds(r * MODES, MODES), :] = got[40 * n : 40 * n + 32, h * 128 : h * 128 + 128]
+                grid_en[h, pl.ds(r * 8, 8), :] = got[40 * n + 32 : 40 * n + 40, h * 128 : h * 128 + 128] + back[pl.ds(r * BACK + 16, 8), :]
     for z in range(Z):
         for h, back in enumerate((left, right)):
             for b in range(2):
                 to = (pl.ds(z * ROWS + 8 * b, 8), pl.ds(h * 128, 128))
-                eq[to] = back[pl.ds(8 * b * PACK + 32 + z, 8, stride=PACK), :]
-                en_ref[to] = back[pl.ds(8 * b * PACK + 40 + z, 8, stride=PACK), :]
+                eq[to] = back[pl.ds(8 * b * BACK + 8 + z, 8, stride=BACK), :]
+                en_ref[to] = grid_en[h, pl.ds(8 * b * 8 + z, 8, stride=8), :]
 
     def leave(g, d):
         part = pl.ds(g * STEP, STEP)
         return pltpu.make_async_copy(res.at[d, part], out_hbm.at[d, part], sems.at[d, g])
 
-    def run(pos_x):
-        edge = low if pos_x else high
+    def run(pos_x, edge):
         first = 0 if pos_x else 8
         sub = lax.broadcasted_iota(jnp.int32, (8, 128), 0) == (0 if pos_x else 7)
 
         def one(m, carry):
             eta, beta, kappa = [jnp.broadcast_to(tab[n, pl.ds(m, 1), :], (8, 128)) for n in (ETA, BETA, KAPPA)]
             for r in (0, 8):
-                for h, back in enumerate((left, right)):
+                for h in range(2):
                     at = [(pl.ds(z * ROWS + r, 8), pl.ds(h * 128, 128)) for z in range(Z)]
+                    here = pl.ds(pl.multiple_of(m * ROWS, ROWS) + r, 8)
+                    kp = ksel[h, here, :]
+                    far = eq[at[Z - 1]]
+                    for z in reversed(range(Z - 1)):
+                        far = kp * far + eq[at[z]]
+                    far = nsel[h, here, :] * far + cell[h, pl.ds(r * MODES + m, 8, stride=MODES), :]
+                    rough = cz_ref[pl.ds(r, 8), pl.ds(h * 128, 128)] > 0.1
                     src = [eta * eq[at[z]] for z in range(Z)]
 
                     def source(d, z):
@@ -312,8 +445,9 @@
                     t = None
                     for z in reversed(range(Z)):
                         t = source(1, z) if t is None else kappa * t + source(1, z)
-                        res[(1, m) + at[z]] = l0_ref[(1, m) + at[z]] + t
-                    t = back[pl.ds(r * PACK + m, 8, stride=PACK), :]
+                        bottom = l0_ref[(1, m) + at[z]] + t
+                        res[(1, m) + at[z]] = bottom
+                    t = jnp.where(rough, far, 0.9 * bottom)
                     for z in range(Z):
                         t = kappa * t + source(0, z)
                         res[(0, m) + at[z]] = l0_ref[(0, m) + at[z]] + t
@@ -327,8 +461,10 @@
 
         lax.fori_loop(0, MODES // STEP, some, 0)
 
-    pl.when(up_x)(lambda: run(True))
-    pl.when(jnp.logical_not(up_x))(lambda: run(False))
+    on_chip = flags[4] > 0.5
+    for pos_x in (True, False):
+        for here, edge in ((True, chip), (False, next_chip)):
+            pl.when((up_x == pos_x) & (on_chip == here))(lambda p=pos_x, e=edge: run(p, e))
     for g in range(MODES // STEP):
         for d in range(2):
             leave(g, d).wait()
@@ -337,8 +473,6 @@
 def per_device(
     intensity, dir_cos, velocity, rate, spectrum, weight, heat, rough_cells, rough_count, rough_map
 ):
-    pos = lax.axis_index("mode").astype(jnp.int32).reshape(1)
-    slots = rough_cells.shape[0]
     smem = pl.BlockSpec(memory_space=pltpu.SMEM)
     vmem = pl.BlockSpec(memory_space=pltpu.VMEM)
 
@@ -348,41 +482,33 @@
     anywhere = pl.BlockSpec(memory_space=pltpu.HBM)
     field = (2, MODES, PLANE, COLS)
     ones = [t.reshape(1, -1) for t in (velocity, rate, spectrum, weight, rough_cells)]
-    x, energy, edge, tab, par, jm, k0, flags = pl.pallas_call(
+    x, energy, edge, tab, flags = pl.pallas_call(
         edge_kernel,
-        in_specs=[smem] * 2 + [anywhere] * 8,
-        out_specs=[vmem] * 7 + [smem],
+        in_specs=[anywhere] * 6,
+        out_specs=[vmem] * 4 + [smem],
         out_shape=[
             pltpu.VMEM(s, F32)
-            for s in (
-                (2, 64 * PLANE, 128), (2, PLANE, 128), (2, SMALL + 40, 128), (6, MODES, 128), (3, MODES, 128),
-                (GROUP, COLS), (Z, 128),
-            )
+            for s in ((2, 64 * PLANE, 128), (2, PLANE, 128), (2, EDGE + 40, 128), (6, MODES, 128))
         ]
-        + [pltpu.SMEM((4,), F32)],
+        + [pltpu.SMEM((5,), F32)],
         scratch_shapes=[
             pltpu.VMEM((3, DIRS), F32),
             pltpu.VMEM((1, MODES), F32),
             pltpu.VMEM((1, MODES), F32),
             pltpu.VMEM((1, MODES), F32),
             pltpu.VMEM((1, DIRS), F32),
-            pltpu.VMEM((1, slots), jnp.int32),
-            pltpu.VMEM((GROUP, slots), jnp.int32),
             pltpu.VMEM((2, 64, 128), F32),
-            pltpu.SemaphoreType.DMA((7,)),
+            pltpu.SemaphoreType.DMA((5,)),
             pltpu.SemaphoreType.DMA((2, 8)),
         ],
         compiler_params=pltpu.CompilerParams(vmem_limit_bytes=8 << 20),
         cost_estimate=pl.CostEstimate(flops=4 << 20, bytes_accessed=8 << 20, transcendentals=0),
         name="edges",
-    )(
-        pos, rough_count, hbm(intensity.reshape(64 * PLANE, COLS)), hbm(dir_cos), *[hbm(t) for t in ones], hbm(rough_map.T),
-    )
+    )(hbm(intensity.reshape(64 * PLANE, COLS)), hbm(dir_cos), *[hbm(t) for t in ones[:4]])
     count = lax.axis_size("space")
-    forward = [(i, i + 1) for i in range(count - 1)]
-    backward = [(t, s) for s, t in forward]
-    low = lax.ppermute(edge, "space", forward)
-    high = lax.ppermute(edge, "space", backward)
+    on_chip = [(i, i ^ 1) for i in range(count)]
+    across = [(i, i + 1 if i % 2 else i - 1) for i in range(1, count - 1)]
+    edge_chip, edge_next = [lax.ppermute(edge, "space", p) for p in (on_chip, across)]
 
     base, e0, d0 = pl.pallas_call(
         sweep_kernel,
@@ -395,43 +521,61 @@
         name="sweep",
     )(flags, tab, x, heat)
 
+    tables = [
+        ((COLS, SLOTS), jnp.bfloat16), ((ROWS, SLOTS), F32), ((3, MODES, 128), F32), ((GROUP, COLS), F32),
+        ((Z, 128), F32), ((GROUP, 128), F32), ((ROWS, COLS), F32), ((2, MODES * ROWS, 128), F32),
+        ((2, MODES * ROWS, 128), F32), ((MODES, SLOTS), F32), ((2, PLANE, 128), F32),
+    ]
+    hot, rm, par, jm, k0, mt, cz, ksel, nsel, at_slots, e0 = pl.pallas_call(
+        slot_kernel,
+        in_specs=[smem] * 2 + [vmem] * 10,
+        out_specs=[vmem] * len(tables),
+        out_shape=[pltpu.VMEM(*t) for t in tables],
+        scratch_shapes=[pltpu.VMEM((2, MODES * ROWS, COLS), jnp.bfloat16)],
+        compiler_params=pltpu.CompilerParams(vmem_limit_bytes=12 << 20),
+        cost_estimate=pl.CostEstimate(flops=30 << 20, bytes_accessed=8 << 20, transcendentals=0),
+        name="slots",
+    )(rough_count, flags, dir_cos, *ones, rough_map.T, tab, d0, e0)
+
     pack = pl.pallas_call(
         pack_kernel,
-        in_specs=[smem] + [vmem] * 5,
+        in_specs=[smem] + [vmem] * 9,
         out_specs=vmem,
-        out_shape=pltpu.VMEM((ROWS * PACK, COLS), F32),
+        out_shape=pltpu.VMEM((ROWS * SEND, COLS), F32),
         compiler_params=pltpu.CompilerParams(vmem_limit_bytes=8 << 20),
         name="pack",
-    )(flags, energy, e0, d0, low, high)
-    got = lax.all_to_all(pack.reshape(GROUP, PACK, COLS), "mode", 0, 0, tiled=True)
+    )(flags, tab, energy, e0, at_slots, hot, rm, cz, edge_chip, edge_next)
+    got = lax.all_to_all(pack.reshape(GROUP, SEND, COLS), "mode", 0, 0, tiled=True)
 
     reply = pl.pallas_call(
         middle_kernel,
-        in_specs=[vmem] * 4,
+        in_specs=[vmem] * 5,
         out_specs=vmem,
-        out_shape=pltpu.VMEM((GROUP, PACK, COLS), F32),
+        out_shape=pltpu.VMEM((GROUP, BACK, COLS), F32),
         scratch_shapes=[pltpu.VMEM((GROUP, MODES, COLS), F32)],
         compiler_params=pltpu.CompilerParams(vmem_limit_bytes=8 << 20),
         name="middle",
-    )(got, par, jm, k0)
-    back = lax.all_to_all(reply, "mode", 0, 0, tiled=True).reshape(GROUP * PACK, COLS)
+    )(got, par, jm, k0, mt)
+    back = lax.all_to_all(reply, "mode", 0, 0, tiled=True).reshape(GROUP * BACK, COLS)
 
     fresh, energy_new = pl.pallas_call(
         finish_kernel,
         grid=(1,),
         in_specs=[smem, vmem, vmem]
-        + [pl.BlockSpec((GROUP * PACK, 128), lambda i, h=h: (0, h)) for h in range(2)]
-        + [vmem] * 2,
+        + [pl.BlockSpec((GROUP * BACK, 128), lambda i, h=h: (0, h)) for h in range(2)]
+        + [vmem] * 7,
         out_specs=[anywhere, vmem],
         out_shape=[pltpu.HBM(field, F32), jax.ShapeDtypeStruct((PLANE, COLS), F32)],
         scratch_shapes=[
             pltpu.VMEM((PLANE, COLS), F32),
             pltpu.VMEM(field, F32),
+            pltpu.VMEM((2, MODES * ROWS, 128), F32),
+            pltpu.VMEM((2, PLANE, 128), F32),
             pltpu.SemaphoreType.DMA((2, MODES // STEP)),
         ],
-        compiler_params=pltpu.CompilerParams(vmem_limit_bytes=20 << 20),
+        compiler_params=pltpu.CompilerParams(vmem_limit_bytes=24 << 20),
         name="finish",
-    )(flags, tab, base, back, back, low, high)
+    )(flags, tab, base, back, back, hot, rm, cz, ksel, nsel, edge_chip, edge_next)
     return fresh.reshape(intensity.shape), energy_new.reshape(Z, ROWS, COLS)
 
 

time: 62.4 us -> 57.2 us (0.917)
  the two profiles are of different devices: /device:TPU:8 before, /device:TPU:0 now
where the time goes in v3:
time: 57.2 us; the launch traced here: 57 us
  blocking collectives  34.1 us (60%)
  Pallas kernels  17.7 us (31%)
  starting transfers between devices  3.76 us (7%)
  between operations  1.47 us (3%)
    all_to_all x1, blocking collectives, per_device(): lax.all_to_all(pack.reshape(GROUP, SEND, COLS), 'mode', 0, 0, tiled=True)  19.1 us
    all_to_all x1, blocking collectives, per_device(): lax.all_to_all(reply, 'mode', 0, 0, tiled=True).reshape(GROUP * BACK, COLS)  15 us
    pallas_call x1, Pallas kernels, per_device(): pl.pallas_call(finish_kernel, grid=(1,), in_specs=[smem, vmem, vmem] + [p...  6.07 us
    pallas_call x1, Pallas kernels, per_device(): pl.pallas_call(edge_kernel, in_specs=[anywhere] * 6, out_specs=[vmem] * 4...  4.56 us
    ppermute x2, starting transfers between devices, per_device(): lax.ppermute(edge, 'space', p)  3.76 us
    pallas_call x1, Pallas kernels, per_device(): pl.pallas_call(sweep_kernel, in_specs=[smem] + [vmem] * 3, out_specs=[vme...  3.55 us
    pallas_call x1, Pallas kernels, per_device(): pl.pallas_call(slot_kernel, in_specs=[smem] * 2 + [vmem] * 10, out_specs=...  1.72 us
    pallas_call x1, Pallas kernels, per_device(): pl.pallas_call(middle_kernel, in_specs=[vmem] * 5, out_specs=vmem, out_sh...  1.53 us
  transfers between devices with their start and end apart: 2, of which 0 were waited for; matrix products, arithmetic and copies ran while one was open for 0% of the time, Pallas kernels for 9%

profile of v3, /device:TPU:0, one launch (start us, length us, event | category | flops | bytes accessed | tf_op | source)
XLA Modules:
  0.0 57.0 jit_solution(8235461361665303723)
XLA Ops:
  0.6 0.0 copy-start.1
  0.6 0.0 copy-start
  0.7 0.0 copy-start.2
  0.7 0.0 copy-start.3
  0.7 0.0 copy-start.4
  0.7 0.0 copy-start.5
  0.7 0.0 copy-start.6
  0.7 0.0 copy-start.7
  0.7 4.6 %edges.1 = (f32[2,8192,128]{2,1,0:T(8,128)S(1)}, f32[2,128,128]{2,1,0:T(8,128)S(1)}, f32[2,552,128]{2,1,0:T(8,128)S(1)}, f32[6,32,128]{2,1,0:T(8,128)S(1)}, f32[5]{0:T(128)S(4)}) custom-call(f32[8192,256]{1,0:T(8,128)} %bitcast.24, f32[3,32]{1,0:T(4,128)} %dcv.1, f32[1,32]{1,0:T(1,128)} %bitcast.16, f32[1,32]{1,0:T(1,128)} %bitcast.18, f32[1,32]{1,0:T(1,128)} %bitcast.20, ...), custom_call_target="tpu_custom_call" | custom-call | flops 4194304 | bytes 8388608 | tf_op jit(solution)/shard_map/edges/pallas_call | solution.py:485
  5.3 0.7 %collective-permute-start.1 = (f32[2,552,128]{2,1,0:T(8,128)S(1)}, f32[2,552,128]{2,1,0:T(8,128)S(1)}, u32[]{:S(2)}, u32[]{:S(2)}) collective-permute-start(f32[2,552,128]{2,1,0:T(8,128)S(1)} %get-tuple-element.35), channel_id=1, source_target_pairs={{16,32},{32,16},{48,64},{64,48},{80,96},{96,80},{17,33},{33,17},{4... | collective-permute-start | bytes 1695752 | tf_op jit(solution)/shard_map/ppermute | solution.py:511
  6.0 3.1 %collective-permute-start = (f32[2,552,128]{2,1,0:T(8,128)S(1)}, f32[2,552,128]{2,1,0:T(8,128)S(1)}, u32[]{:S(2)}, u32[]{:S(2)}) collective-permute-start(f32[2,552,128]{2,1,0:T(8,128)S(1)} %get-tuple-element.35), channel_id=1, source_target_pairs={{0,16},{16,0},{32,48},{48,32},{64,80},{80,64},{96,112},{112,96},{1... | collective-permute-start | bytes 1695752 | tf_op jit(solution)/shard_map/ppermute | solution.py:511
  9.7 0.0 copy-done.1
  9.7 3.5 %sweep.1 = (f32[2,32,128,256]{3,2,1,0:T(8,128)S(1)}, f32[2,128,128]{2,1,0:T(8,128)S(1)}, f32[2,512,128]{2,1,0:T(8,128)S(1)}) custom-call(f32[5]{0:T(128)S(4)} %get-tuple-element.23.flags, f32[6,32,128]{2,1,0:T(8,128)S(1)} %get-tuple-element.24.tab, f32[2,8192,128]{2,1,0:T(8,128)S(1)} %get-tuple-element.25.x_ref, f32[16,256]{1,0:T(8,128)S(1)} %copy-done.1), custom_call_target="tpu_custom_call" | custom-call | flops 31457280 | bytes 16777216 | tf_op jit(solution)/shard_map/sweep/pallas_call | solution.py:513
  13.3 0.0 copy-done
  13.3 0.0 copy-done.2
  13.3 0.0 copy-done.3
  13.3 0.0 copy-done.4
  13.3 0.0 copy-done.5
  13.3 0.0 copy-done.6
  13.3 0.0 copy-done.7
  13.3 1.7 %slots.1 = (bf16[256,1024]{1,0:T(8,128)(2,1)S(1)}, f32[16,1024]{1,0:T(8,128)S(1)}, f32[3,32,128]{2,1,0:T(8,128)S(1)}, f32[16,256]{1,0:T(8,128)S(1)}, f32[8,128]{...) custom-call(s32[1]{0:T(128)S(6)} %copy.12.cnt, ...), custom_call_target="tpu_custom_call" | custom-call | flops 31457280 | bytes 8388608 | tf_op jit(solution)/shard_map/slots/pallas_call | solution.py:529
  15.1 0.0 collective-permute-done.1.next_chip
  15.1 0.0 collective-permute-done.chip
  15.1 0.3 pack.1
  15.4 19.1 %all_to_all.10.got = f32[16,24,256]{2,1,0:T(8,128)S(1)} all-to-all(f32[16,24,256]{2,1,0:T(8,128)S(1)} %bitcast.13), channel_id=1, replica_groups=mesh['space'=8,'mode'=16] {'mode'}, dimensions={0} | all-to-all | bytes 786432 | tf_op jit(solution)/shard_map/all_to_all | solution.py:548
  34.4 1.5 %middle.1 = f32[16,32,256]{2,1,0:T(8,128)S(1)} custom-call(f32[16,24,256]{2,1,0:T(8,128)S(1)} %all_to_all.10.got, f32[3,32,128]{2,1,0:T(8,128)S(1)} %get-tuple-element.36.par, f32[16,256]{1,0:T(8,128)S(1)} %get-tuple-element.37.jm_ref, f32[8,128]{1,0:T(8,128)S(1)} %get-tuple-element.38.k0_ref, f32[16,128]{1,0:T(8,128)S(1)} %get-tuple-element.39.mt_ref), custom_call_target="tpu_custom_call" | custom-call | tf_op jit(solution)/shard_map/middle/pallas_call | solution.py:550
  36.0 15.0 %all_to_all.11 = f32[16,32,256]{2,1,0:T(8,128)S(1)} all-to-all(f32[16,32,256]{2,1,0:T(8,128)S(1)} %middle.1), channel_id=1, replica_groups=mesh['space'=8,'mode'=16] {'mode'}, dimensions={0} | all-to-all | bytes 1048576 | tf_op jit(solution)/shard_map/all_to_all | solution.py:559
  51.0 6.1 %finish.1 = (f32[2,32,128,256]{3,2,1,0:T(8,128)}, f32[128,256]{1,0:T(8,128)}) custom-call(f32[5]{0:T(128)S(4)} %get-tuple-element.23.flags, f32[6,32,128]{2,1,0:T(8,128)S(1)} %get-tuple-element.24.tab, f32[2,32,128,256]{3,2,1,0:T(8,128)S(1)} %get-tuple-element.26.l0_ref, f32[512,256]{1,0:T(8,128)S(1)} %bitcast.11, f32[512,256]{1,0:T(8,128)S(1)} %bitcast.12, ...), custom_call_target="tpu_custom_call" | custom-call | tf_op jit(solution)/shard_map/finish/pallas_call | solution.py:561
Async XLA Ops:
  0.6 9.1 %copy-start.1 = (f32[16,256]{1,0:T(8,128)S(1)}, f32[16,256]{1,0:T(8,128)}, u32[]{:S(2)}) copy-start(f32[16,256]{1,0:T(8,128)} %heat.1) | copy-start | bytes 49156
  0.6 12.6 %copy-start = (s32[1024,16]{0,1:T(8,128)S(1)}, s32[1024,16]{0,1:T(8,128)}, u32[]{:S(2)}) copy-start(s32[1024,16]{0,1:T(8,128)} %param.19) | copy-start | bytes 196612
  0.7 12.6 %copy-start.2 = (f32[3,32]{1,0:T(4,128)S(1)}, f32[3,32]{1,0:T(4,128)}, u32[]{:S(2)}) copy-start(f32[3,32]{1,0:T(4,128)} %dcv.1) | copy-start | bytes 1156
  0.7 12.6 %copy-start.3 = (s32[1024]{0:T(1024)S(1)}, s32[1024]{0:T(1024)}, u32[]{:S(2)}) copy-start(s32[1024]{0:T(1024)} %param.17) | copy-start | bytes 12292
  0.7 12.6 %copy-start.4 = (f32[32]{0:T(128)S(1)}, f32[32]{0:T(128)}, u32[]{:S(2)}) copy-start(f32[32]{0:T(128)} %param.12) | copy-start | bytes 388
  0.7 12.6 %copy-start.5 = (f32[32]{0:T(128)S(1)}, f32[32]{0:T(128)}, u32[]{:S(2)}) copy-start(f32[32]{0:T(128)} %param.13) | copy-start | bytes 388
  0.7 12.6 %copy-start.6 = (f32[32]{0:T(128)S(1)}, f32[32]{0:T(128)}, u32[]{:S(2)}) copy-start(f32[32]{0:T(128)} %param.14) | copy-start | bytes 388
  0.7 12.6 %copy-start.7 = (f32[32]{0:T(128)S(1)}, f32[32]{0:T(128)}, u32[]{:S(2)}) copy-start(f32[32]{0:T(128)} %param.15) | copy-start | bytes 388
  5.3 9.8 %collective-permute-start.1 = (f32[2,552,128]{2,1,0:T(8,128)S(1)}, f32[2,552,128]{2,1,0:T(8,128)S(1)}, u32[]{:S(2)}, u32[]{:S(2)}) collective-permute-start(f32[2,552,128]{2,1,0:T(8,128)S(1)} %get-tuple-element.35), channel_id=1, source_target_pairs={{16,32},{32,16},{48,64},{64,48},{80,96},{96,80},{17,33},{33,17},{4... | collective-permute-start | bytes 1695752 | tf_op jit(solution)/shard_map/ppermute | solution.py:511
  6.0 9.1 %collective-permute-start = (f32[2,552,128]{2,1,0:T(8,128)S(1)}, f32[2,552,128]{2,1,0:T(8,128)S(1)}, u32[]{:S(2)}, u32[]{:S(2)}) collective-permute-start(f32[2,552,128]{2,1,0:T(8,128)S(1)} %get-tuple-element.35), channel_id=1, source_target_pairs={{0,16},{16,0},{32,48},{48,32},{64,80},{80,64},{96,112},{112,96},{1... | collective-permute-start | bytes 1695752 | tf_op jit(solution)/shard_map/ppermute | solution.py:511

commit v4 on v3

--- a/solution.py
+++ b/solution.py
@@ -27,38 +27,39 @@
 
 
 ALPHA, BETA, GAMMA, KAPPA, SHARE, ETA = range(6)
-CHUNK = 8 * PLANE
+CHUNK = 8 * Z
 EDGE = 512
+
+
+def half_tiles(x_hbm, dst, sems, half, c, h):
+    src = x_hbm.at[pl.ds(c * CHUNK, CHUNK), half, :, pl.ds(h * 128, 128)]
+    return pltpu.make_async_copy(src, dst.at[h, pl.ds(c * CHUNK, CHUNK)], sems.at[h, c])
 
 
 def edge_kernel(
     x_hbm, dc_h, v_h, r_h, s_h, w_h,
-    x_ref, e_ref, edge_ref, tab, flags,
+    x_ref, edge_ref, tab, flags,
     dcv, vel, rate, spec, wv, acc, sems, xsems,
 ):
     k = lax.axis_index("mode")
     odd_row = lax.axis_index("space") % 2 == 1
-
-    def chunk(c, h):
-        rows = pl.ds(pl.multiple_of(c * CHUNK, CHUNK), CHUNK)
-        return pltpu.make_async_copy(x_hbm.at[rows, pl.ds(h * 128, 128)], x_ref.at[h, rows, :], xsems.at[h, c])
-
     few = list(zip((dc_h, v_h, r_h, s_h, w_h), (dcv, vel, rate, spec, wv)))
     few = [pltpu.make_async_copy(a, b, sems.at[n]) for n, (a, b) in enumerate(few)]
     for copy in few:
         copy.start()
+    few[0].wait()
+    lane = lax.broadcasted_iota(jnp.int32, (1, DIRS), 1)
+
+    def pick(row, at):
+        return jnp.sum(jnp.where(lane == at, row, 0.0))
+
+    cx, cy, cz = [pick(dcv[n : n + 1, :], 2 * k) for n in range(3)]
+    half = jnp.where(cx > 0.0, 1, 0)
     for c in range(8):
         for h in range(2):
-            chunk(c, h).start()
-    for copy in few:
+            half_tiles(x_hbm, x_ref, xsems, half, c, h).start()
+    for copy in few[1:]:
         copy.wait()
-
-    lane = lax.broadcasted_iota(jnp.int32, (1, DIRS), 1)
-
-    def pick(row, at):
-        return jnp.sum(jnp.where(lane == at, row, 0.0))
-
-    cx, cy, cz = [pick(dcv[n : n + 1, :], 2 * k) for n in range(3)]
     cz = jnp.abs(cz)
     flags[0] = cx
     flags[1] = cy
@@ -79,25 +80,20 @@
     for n, col in table.items():
         tab[n] = jnp.broadcast_to(col, (MODES, 128))
     acc[...] = jnp.zeros_like(acc)
-    e_ref[...] = jnp.zeros_like(e_ref)
-
-    row = jnp.where(cx > 0.0, ROWS - 1, 0)
+
+    row = jnp.where(cx > 0.0, 7, 0)
+    flat = x_ref.reshape(2, 512 * 8, 128)
 
     def one(c, carry):
         w = flags[2 + c // 4]
-        base = pl.multiple_of(c * CHUNK, CHUNK)
+        base = pl.multiple_of(c * CHUNK * 8, CHUNK * 8)
         m0 = pl.multiple_of(8 * (c % 4), 8)
         for h in range(2):
-            chunk(c, h).wait()
-            for t in range(PLANE // 8):
-                part = x_ref[h, pl.ds(base + t * 8, 8), :]
-                for p in range(1, 8):
-                    part += x_ref[h, pl.ds(base + p * PLANE + t * 8, 8), :]
-                e_ref[h, pl.ds(t * 8, 8), :] += w * part
+            half_tiles(x_hbm, x_ref, xsems, half, c, h).wait()
             kp, bt = [tab[n, pl.ds(m0, 8), :] for n in (KAPPA, BETA)]
             rows = []
             for z in range(Z):
-                e = x_ref[h, pl.ds(base + z * ROWS + row, 8, stride=PLANE), :]
+                e = flat[h, pl.ds(base + z * 8 + row, 8, stride=8 * Z), :]
                 edge_ref[h, pl.ds(pl.multiple_of(z * 64 + 8 * c, 8), 8), :] = e
                 rows.append(bt * e)
 
@@ -127,11 +123,17 @@
 
 
 def sweep_kernel(
-    flags, tab, x_ref, heat, l0_ref, e0_ref, d0, accd, accu,
+    flags, tab, x_hbm, far_ref, heat, l0_ref, e_ref, e0_ref, d0, near_ref, accd, accu, xsems,
 ):
     up_x, up_y = flags[0] > 0.0, flags[1] > 0.0
+    half = jnp.where(up_x, 0, 1)
+    for g in range(4):
+        for c in (4 + g, g):
+            for h in range(2):
+                half_tiles(x_hbm, near_ref, xsems, half, c, h).start()
     accd[...] = jnp.zeros_like(accd)
     accu[...] = jnp.zeros_like(accu)
+    e_ref[...] = jnp.zeros_like(e_ref)
 
     def run(pos_x, pos_y):
         rows = (0, 8) if pos_x else (8, 0)
@@ -146,8 +148,8 @@
 
             def rhs(d, t, z):
                 alpha, beta, gamma, _ = coef[t]
-                at = pl.multiple_of((d * MODES + modes[t]) * PLANE, PLANE) + z * ROWS
-                f = [[x_ref[c, pl.ds(at + r, 8), :] for c in cols] for r in rows]
+                at = (d * MODES + modes[t]) * Z + z
+                f = [[ref[c, at] for c in cols] for ref in (near_ref, far_ref)]
                 rx = [[pltpu.roll(v, 1 if pos_x else 7, 0) for v in vs] for vs in f]
                 ry = [[pltpu.roll(v, 1 if pos_y else 127, 1) for v in vs] for vs in f]
                 out = []
@@ -156,7 +158,7 @@
                         x = jnp.where(sub, 0.0 if r == 0 else rx[0][c], rx[r][c])
                         y = jnp.where(lane, 0.0 if c == 0 else ry[r][0], ry[r][c])
                         out.append(alpha * f[r][c] + beta * x + gamma * y)
-                return out
+                return out, f[0] + f[1]
 
             for d, acc, order in ((1, accd, range(Z - 1, -1, -1)), (0, accu, range(Z))):
                 if d == 1:
@@ -166,21 +168,31 @@
                     ]
                 else:
                     state = [None, None]
+                weight = flags[2 + d]
                 for z in order:
+                    sums = []
                     for t in range(2):
-                        f = rhs(d, t, z)
+                        f, raw = rhs(d, t, z)
+                        sums.append(raw)
                         state[t] = f if state[t] is None else [a + coef[t][3] * b for a, b in zip(f, state[t])]
                         for v, (r, c) in zip(state[t], tiles):
                             l0_ref[d, modes[t], pl.ds(z * ROWS + r, 8), pl.ds(c * 128, 128)] = v
                     for n, (r, c) in enumerate(tiles):
                         acc[c, pl.ds(z * ROWS + r, 8), :] += state[0][n] + state[1][n]
+                        e_ref[c, pl.ds(z * ROWS + r, 8), :] += weight * (sums[0][n] + sums[1][n])
                 if d == 1:
                     for t in range(2):
                         for v, (r, c) in zip(state[t], tiles):
                             d0[c, pl.ds(pl.multiple_of(modes[t] * ROWS, ROWS) + r, 8), :] = v
             return carry
 
-        lax.fori_loop(0, MODES // 2, pair, 0)
+        def eight(g, carry):
+            for c in (4 + g, g):
+                for h in range(2):
+                    half_tiles(x_hbm, near_ref, xsems, half, c, h).wait()
+            return lax.fori_loop(4 * g, 4 * g + 4, pair, carry)
+
+        lax.fori_loop(0, 4, eight, 0)
 
     for pos_x in (True, False):
         for pos_y in (True, False):
@@ -342,13 +354,12 @@
     for k in range(GROUP):
         jm = jnp.broadcast_to(jm_ref[k : k + 1, :], (8, COLS))
         jm = jnp.where(jm < 0.5, float(k + 1), jm)
-        near = [jnp.abs(jm - float(j + 1)) < 0.5 for j in range(GROUP)]
         w = jnp.broadcast_to(w_all[0:8, 2 * k : 2 * k + 1], (8, COLS))
         for t in range(MODES // 8):
             at = slice(8 * t, 8 * t + 8)
             pick = q_ref[0, at, :]
             for j in range(1, GROUP):
-                pick = jnp.where(near[j], q_ref[j, at, :], pick)
+                pick = jnp.where(jm > j + 0.5, q_ref[j, at, :], pick)
             kp = jnp.broadcast_to(k_all[at, 2 * k : 2 * k + 1], (8, COLS))
             pick = w * pick
             for z in range(Z):
@@ -389,7 +400,67 @@
     flags, tab, l0_ref, left, right, hot_ref, rm_ref, cz_ref, ksel, nsel, chip, next_chip,
     out_hbm, en_ref, eq, res, cell, grid_en, sems,
 ):
-    up_x = flags[0] > 0.0
+    up_x, on_chip = flags[0] > 0.0, flags[4] > 0.5
+    for z in range(Z):
+        for h, back in enumerate((left, right)):
+            for b in range(2):
+                eq[pl.ds(z * ROWS + 8 * b, 8), pl.ds(h * 128, 128)] = back[pl.ds(8 * b * BACK + 8 + z, 8, stride=BACK), :]
+
+    def leave(g, d):
+        part = pl.ds(g * STEP, STEP)
+        return pltpu.make_async_copy(res.at[d, part], out_hbm.at[d, part], sems.at[d, g])
+
+    def run(d, pos_x, edge):
+        first = 0 if pos_x else 8
+        sub = lax.broadcasted_iota(jnp.int32, (8, 128), 0) == (0 if pos_x else 7)
+
+        def pair(i, carry):
+            modes = [2 * i, 2 * i + 1]
+            eta, beta, kappa = [
+                [jnp.broadcast_to(tab[n, pl.ds(m, 1), :], (8, 128)) for m in modes] for n in (ETA, BETA, KAPPA)
+            ]
+            for r in (0, 8):
+                for h in range(2):
+                    at = [(pl.ds(z * ROWS + r, 8), pl.ds(h * 128, 128)) for z in range(Z)]
+                    e = [eq[to] for to in at]
+
+                    def source(n, z):
+                        s = eta[n] * e[z]
+                        if r == first:
+                            row = edge[h, pl.ds(z * 64 + d * 32 + modes[n], 1), :]
+                            s += jnp.where(sub, beta[n] * jnp.broadcast_to(row, (8, 128)), 0.0)
+                        return s
+
+                    t = [None, None]
+                    if d == 0:
+                        rough = cz_ref[pl.ds(r, 8), pl.ds(h * 128, 128)] > 0.1
+                        here = [pl.ds(pl.multiple_of(m * ROWS, ROWS) + r, 8) for m in modes]
+                        kp = [ksel[h, to, :] for to in here]
+                        far = [e[Z - 1]] * 2
+                        for z in reversed(range(Z - 1)):
+                            far = [a * b + e[z] for a, b in zip(kp, far)]
+                        for n, m in enumerate(modes):
+                            far[n] = nsel[h, here[n], :] * far[n] + cell[h, pl.ds(r * MODES + m, 8, stride=MODES), :]
+                            t[n] = jnp.where(rough, far[n], 0.9 * res[(1, m) + at[0]])
+                    for z in range(Z) if d == 0 else range(Z - 1, -1, -1):
+                        for n, m in enumerate(modes):
+                            t[n] = source(n, z) if t[n] is None else kappa[n] * t[n] + source(n, z)
+                            res[(d, m) + at[z]] = l0_ref[(d, m) + at[z]] + t[n]
+            return carry
+
+        def some(g, carry):
+            lax.fori_loop(g * STEP // 2, g * STEP // 2 + STEP // 2, pair, 0)
+            leave(g, d).start()
+            return carry
+
+        lax.fori_loop(0, MODES // STEP, some, 0)
+
+    def all_modes(d):
+        for pos_x in (True, False):
+            for here, edge in ((True, chip), (False, next_chip)):
+                pl.when((up_x == pos_x) & (on_chip == here))(lambda p=pos_x, e=edge: run(d, p, e))
+
+    all_modes(1)
     hot = hot_ref[...]
     picked = [
         jnp.concatenate([back[pl.ds((8 * half + t) * BACK, 8), :] for t in range(8)], axis=1)
@@ -407,64 +478,11 @@
             for h, back in enumerate((left, right)):
                 cell[h, pl.ds(r * MODES, MODES), :] = got[40 * n : 40 * n + 32, h * 128 : h * 128 + 128]
                 grid_en[h, pl.ds(r * 8, 8), :] = got[40 * n + 32 : 40 * n + 40, h * 128 : h * 128 + 128] + back[pl.ds(r * BACK + 16, 8), :]
+    all_modes(0)
     for z in range(Z):
-        for h, back in enumerate((left, right)):
+        for h in range(2):
             for b in range(2):
-                to = (pl.ds(z * ROWS + 8 * b, 8), pl.ds(h * 128, 128))
-                eq[to] = back[pl.ds(8 * b * BACK + 8 + z, 8, stride=BACK), :]
-                en_ref[to] = grid_en[h, pl.ds(8 * b * 8 + z, 8, stride=8), :]
-
-    def leave(g, d):
-        part = pl.ds(g * STEP, STEP)
-        return pltpu.make_async_copy(res.at[d, part], out_hbm.at[d, part], sems.at[d, g])
-
-    def run(pos_x, edge):
-        first = 0 if pos_x else 8
-        sub = lax.broadcasted_iota(jnp.int32, (8, 128), 0) == (0 if pos_x else 7)
-
-        def one(m, carry):
-            eta, beta, kappa = [jnp.broadcast_to(tab[n, pl.ds(m, 1), :], (8, 128)) for n in (ETA, BETA, KAPPA)]
-            for r in (0, 8):
-                for h in range(2):
-                    at = [(pl.ds(z * ROWS + r, 8), pl.ds(h * 128, 128)) for z in range(Z)]
-                    here = pl.ds(pl.multiple_of(m * ROWS, ROWS) + r, 8)
-                    kp = ksel[h, here, :]
-                    far = eq[at[Z - 1]]
-                    for z in reversed(range(Z - 1)):
-                        far = kp * far + eq[at[z]]
-                    far = nsel[h, here, :] * far + cell[h, pl.ds(r * MODES + m, 8, stride=MODES), :]
-                    rough = cz_ref[pl.ds(r, 8), pl.ds(h * 128, 128)] > 0.1
-                    src = [eta * eq[at[z]] for z in range(Z)]
-
-                    def source(d, z):
-                        if r != first:
-                            return src[z]
-                        e = jnp.broadcast_to(edge[h, pl.ds(z * 64 + d * 32 + m, 1), :], (8, 128))
-                        return src[z] + jnp.where(sub, beta * e, 0.0)
-
-                    t = None
-                    for z in reversed(range(Z)):
-                        t = source(1, z) if t is None else kappa * t + source(1, z)
-                        bottom = l0_ref[(1, m) + at[z]] + t
-                        res[(1, m) + at[z]] = bottom
-                    t = jnp.where(rough, far, 0.9 * bottom)
-                    for z in range(Z):
-                        t = kappa * t + source(0, z)
-                        res[(0, m) + at[z]] = l0_ref[(0, m) + at[z]] + t
-            return carry
-
-        def some(g, carry):
-            lax.fori_loop(g * STEP, g * STEP + STEP, one, 0)
-            for d in range(2):
-                leave(g, d).start()
-            return carry
-
-        lax.fori_loop(0, MODES // STEP, some, 0)
-
-    on_chip = flags[4] > 0.5
-    for pos_x in (True, False):
-        for here, edge in ((True, chip), (False, next_chip)):
-            pl.when((up_x == pos_x) & (on_chip == here))(lambda p=pos_x, e=edge: run(p, e))
+                en_ref[pl.ds(z * ROWS + 8 * b, 8), pl.ds(h * 128, 128)] = grid_en[h, pl.ds(8 * b * 8 + z, 8, stride=8), :]
     for g in range(MODES // STEP):
         for d in range(2):
             leave(g, d).wait()
@@ -482,13 +500,14 @@
     anywhere = pl.BlockSpec(memory_space=pltpu.HBM)
     field = (2, MODES, PLANE, COLS)
     ones = [t.reshape(1, -1) for t in (velocity, rate, spectrum, weight, rough_cells)]
-    x, energy, edge, tab, flags = pl.pallas_call(
+    tiles = hbm(intensity.reshape(512, 2, 8, COLS))
+    x, edge, tab, flags = pl.pallas_call(
         edge_kernel,
         in_specs=[anywhere] * 6,
-        out_specs=[vmem] * 4 + [smem],
+        out_specs=[vmem] * 3 + [smem],
         out_shape=[
             pltpu.VMEM(s, F32)
-            for s in ((2, 64 * PLANE, 128), (2, PLANE, 128), (2, EDGE + 40, 128), (6, MODES, 128))
+            for s in ((2, 512, 8, 128), (2, EDGE + 40, 128), (6, MODES, 128))
         ]
         + [pltpu.SMEM((5,), F32)],
         scratch_shapes=[
@@ -504,22 +523,27 @@
         compiler_params=pltpu.CompilerParams(vmem_limit_bytes=8 << 20),
         cost_estimate=pl.CostEstimate(flops=4 << 20, bytes_accessed=8 << 20, transcendentals=0),
         name="edges",
-    )(hbm(intensity.reshape(64 * PLANE, COLS)), hbm(dir_cos), *[hbm(t) for t in ones[:4]])
+    )(tiles, hbm(dir_cos), *[hbm(t) for t in ones[:4]])
     count = lax.axis_size("space")
     on_chip = [(i, i ^ 1) for i in range(count)]
     across = [(i, i + 1 if i % 2 else i - 1) for i in range(1, count - 1)]
     edge_chip, edge_next = [lax.ppermute(edge, "space", p) for p in (on_chip, across)]
 
-    base, e0, d0 = pl.pallas_call(
+    base, energy, e0, d0 = pl.pallas_call(
         sweep_kernel,
-        in_specs=[smem] + [vmem] * 3,
-        out_specs=[vmem] * 3,
-        out_shape=[pltpu.VMEM(s, F32) for s in (field, (2, PLANE, 128), (2, MODES * ROWS, 128))],
-        scratch_shapes=[pltpu.VMEM((2, PLANE, 128), F32), pltpu.VMEM((2, PLANE, 128), F32)],
-        compiler_params=pltpu.CompilerParams(vmem_limit_bytes=8 << 20),
+        in_specs=[smem, vmem, anywhere, vmem, vmem],
+        out_specs=[vmem] * 4,
+        out_shape=[pltpu.VMEM(s, F32) for s in (field, (2, PLANE, 128), (2, PLANE, 128), (2, MODES * ROWS, 128))],
+        scratch_shapes=[
+            pltpu.VMEM((2, 512, 8, 128), F32),
+            pltpu.VMEM((2, PLANE, 128), F32),
+            pltpu.VMEM((2, PLANE, 128), F32),
+            pltpu.SemaphoreType.DMA((2, 8)),
+        ],
+        compiler_params=pltpu.CompilerParams(vmem_limit_bytes=12 << 20),
         cost_estimate=pl.CostEstimate(flops=30 << 20, bytes_accessed=16 << 20, transcendentals=0),
         name="sweep",
-    )(flags, tab, x, heat)
+    )(flags, tab, tiles, x, heat)
 
     tables = [
         ((COLS, SLOTS), jnp.bfloat16), ((ROWS, SLOTS), F32), ((3, MODES, 128), F32), ((GROUP, COLS), F32),

time: 57.2 us -> 55.1 us (0.963)
  blocking collectives: 34.1 us -> 31.7 us
    all_to_all x1, blocking collectives: 19.1 us -> 17.7 us  [per_device(): lax.all_to_all(pack.reshape(GROUP, SEND, COLS), 'mode', 0, 0, tiled=True)]
    all_to_all x1, blocking collectives: 15 us -> 14 us  [per_device(): lax.all_to_all(reply, 'mode', 0, 0, tiled=True).reshape(GROUP * BACK, COLS)]
  transfers between devices with their start and end apart: 2 -> 2, of which waited for: 0 -> 0; matrix products, arithmetic and copies ran while one was open for 0% -> 0% of each run, Pallas kernels for 9% -> 13%
where the time goes in v4:
time: 55.1 us; the launch traced here: 54.8 us
  blocking collectives  31.7 us (58%)
  Pallas kernels  17.7 us (32%)
  starting transfers between devices  3.89 us (7%)
  between operations  1.46 us (3%)
    all_to_all x1, blocking collectives, per_device(): lax.all_to_all(pack.reshape(GROUP, SEND, COLS), 'mode', 0, 0, tiled=True)  17.7 us
    all_to_all x1, blocking collectives, per_device(): lax.all_to_all(reply, 'mode', 0, 0, tiled=True).reshape(GROUP * BACK, COLS)  14 us
    pallas_call x1, Pallas kernels, per_device(): pl.pallas_call(finish_kernel, grid=(1,), in_specs=[smem, vmem, vmem] + [p...  5.9 us
    pallas_call x1, Pallas kernels, per_device(): pl.pallas_call(sweep_kernel, in_specs=[smem, vmem, anywhere, vmem, vmem],...  5.24 us
    ppermute x2, starting transfers between devices, per_device(): lax.ppermute(edge, 'space', p)  3.89 us
    pallas_call x1, Pallas kernels, per_device(): pl.pallas_call(edge_kernel, in_specs=[anywhere] * 6, out_specs=[vmem] * 3...  3.24 us
    pallas_call x1, Pallas kernels, per_device(): pl.pallas_call(slot_kernel, in_specs=[smem] * 2 + [vmem] * 10, out_specs=...  1.73 us
    pallas_call x1, Pallas kernels, per_device(): pl.pallas_call(middle_kernel, in_specs=[vmem] * 5, out_specs=vmem, out_sh...  1.34 us
  transfers between devices with their start and end apart: 2, of which 0 were waited for; matrix products, arithmetic and copies ran while one was open for 0% of the time, Pallas kernels for 13%

profile of v4, /device:TPU:0, one launch (start us, length us, event | category | flops | bytes accessed | tf_op | source)
XLA Modules:
  0.0 54.8 jit_solution(9526072208432279718)
XLA Ops:
  0.6 0.0 copy-start.1
  0.6 3.2 %edges.1 = (f32[2,512,8,128]{3,2,1,0:T(8,128)S(1)}, f32[2,552,128]{2,1,0:T(8,128)S(1)}, f32[6,32,128]{2,1,0:T(8,128)S(1)}, f32[5]{0:T(128)S(4)}) custom-call(f32[512,2,8,256]{3,2,1,0:T(8,128)} %bitcast.24, f32[3,32]{1,0:T(4,128)} %dcv.1, f32[1,32]{1,0:T(1,128)} %bitcast.16, f32[1,32]{1,0:T(1,128)} %bitcast.18, f32[1,32]{1,0:T(1,128)} %bitcast.20, ...), custom_call_target="tpu_custom_call" | custom-call | flops 4194304 | bytes 8388608 | tf_op jit(solution)/shard_map/edges/pallas_call | solution.py:504
  3.9 0.0 copy-start
  3.9 0.0 copy-start.2
  3.9 0.0 copy-start.3
  3.9 0.0 copy-start.4
  3.9 0.0 copy-start.5
  4.0 0.0 copy-start.6
  4.0 0.0 copy-start.7
  4.0 0.8 %collective-permute-start.1 = (f32[2,552,128]{2,1,0:T(8,128)S(1)}, f32[2,552,128]{2,1,0:T(8,128)S(1)}, u32[]{:S(2)}, u32[]{:S(2)}) collective-permute-start(f32[2,552,128]{2,1,0:T(8,128)S(1)} %get-tuple-element.35), channel_id=1, source_target_pairs={{16,32},{32,16},{48,64},{64,48},{80,96},{96,80},{17,33},{33,17},{4... | collective-permute-start | bytes 1695752 | tf_op jit(solution)/shard_map/ppermute | solution.py:530
  4.8 3.1 %collective-permute-start = (f32[2,552,128]{2,1,0:T(8,128)S(1)}, f32[2,552,128]{2,1,0:T(8,128)S(1)}, u32[]{:S(2)}, u32[]{:S(2)}) collective-permute-start(f32[2,552,128]{2,1,0:T(8,128)S(1)} %get-tuple-element.35), channel_id=1, source_target_pairs={{0,16},{16,0},{32,48},{48,32},{64,80},{80,64},{96,112},{112,96},{1... | collective-permute-start | bytes 1695752 | tf_op jit(solution)/shard_map/ppermute | solution.py:530
  8.5 0.0 copy-done.1
  8.5 5.2 %sweep.1 = (f32[2,32,128,256]{3,2,1,0:T(8,128)S(1)}, f32[2,128,128]{2,1,0:T(8,128)S(1)}, f32[2,128,128]{2,1,0:T(8,128)S(1)}, f32[2,512,128]{2,1,0:T(8,128)S(1)}) custom-call(f32[5]{0:T(128)S(4)} %get-tuple-element.23.flags, f32[6,32,128]{2,1,0:T(8,128)S(1)} %get-tuple-element.24.tab, f32[512,2,8,256]{3,2,1,0:T(8,128)} %bitcast.25, ...), custom_call_target="tpu_custom_call" | custom-call | flops 31457280 | bytes 16777216 | tf_op jit(solution)/shard_map/sweep/pallas_call | solution.py:532
  13.8 0.0 copy-done
  13.8 0.0 copy-done.2
  13.8 0.0 copy-done.3
  13.8 0.0 copy-done.4
  13.8 0.0 copy-done.5
  13.8 0.0 copy-done.6
  13.9 0.0 copy-done.7
  13.9 1.7 %slots.1 = (bf16[256,1024]{1,0:T(8,128)(2,1)S(1)}, f32[16,1024]{1,0:T(8,128)S(1)}, f32[3,32,128]{2,1,0:T(8,128)S(1)}, f32[16,256]{1,0:T(8,128)S(1)}, f32[8,128]{...) custom-call(s32[1]{0:T(128)S(6)} %copy.12.cnt, ...), custom_call_target="tpu_custom_call" | custom-call | flops 31457280 | bytes 8388608 | tf_op jit(solution)/shard_map/slots/pallas_call | solution.py:553
  15.6 0.0 collective-permute-done.1.next_chip
  15.6 0.0 collective-permute-done.chip
  15.6 0.3 pack.1
  15.9 17.7 %all_to_all.10.got = f32[16,24,256]{2,1,0:T(8,128)S(1)} all-to-all(f32[16,24,256]{2,1,0:T(8,128)S(1)} %bitcast.13), channel_id=1, replica_groups=mesh['space'=8,'mode'=16] {'mode'}, dimensions={0} | all-to-all | bytes 786432 | tf_op jit(solution)/shard_map/all_to_all | solution.py:572
  33.5 1.3 %middle.1 = f32[16,32,256]{2,1,0:T(8,128)S(1)} custom-call(f32[16,24,256]{2,1,0:T(8,128)S(1)} %all_to_all.10.got, f32[3,32,128]{2,1,0:T(8,128)S(1)} %get-tuple-element.36.par, f32[16,256]{1,0:T(8,128)S(1)} %get-tuple-element.37.jm_ref, f32[8,128]{1,0:T(8,128)S(1)} %get-tuple-element.38.k0_ref, f32[16,128]{1,0:T(8,128)S(1)} %get-tuple-element.39.mt_ref), custom_call_target="tpu_custom_call" | custom-call | tf_op jit(solution)/shard_map/middle/pallas_call | solution.py:574
  34.9 14.0 %all_to_all.11 = f32[16,32,256]{2,1,0:T(8,128)S(1)} all-to-all(f32[16,32,256]{2,1,0:T(8,128)S(1)} %middle.1), channel_id=1, replica_groups=mesh['space'=8,'mode'=16] {'mode'}, dimensions={0} | all-to-all | bytes 1048576 | tf_op jit(solution)/shard_map/all_to_all | solution.py:583
  48.9 5.9 %finish.1 = (f32[2,32,128,256]{3,2,1,0:T(8,128)}, f32[128,256]{1,0:T(8,128)}) custom-call(f32[5]{0:T(128)S(4)} %get-tuple-element.23.flags, f32[6,32,128]{2,1,0:T(8,128)S(1)} %get-tuple-element.24.tab, f32[2,32,128,256]{3,2,1,0:T(8,128)S(1)} %get-tuple-element.26.l0_ref, f32[512,256]{1,0:T(8,128)S(1)} %bitcast.11, f32[512,256]{1,0:T(8,128)S(1)} %bitcast.12, ...), custom_call_target="tpu_custom_call" | custom-call | tf_op jit(solution)/shard_map/finish/pallas_call | solution.py:585
Async XLA Ops:
  0.6 7.9 %copy-start.1 = (f32[16,256]{1,0:T(8,128)S(1)}, f32[16,256]{1,0:T(8,128)}, u32[]{:S(2)}) copy-start(f32[16,256]{1,0:T(8,128)} %heat.1) | copy-start | bytes 49156
  3.9 9.9 %copy-start = (s32[1024,16]{0,1:T(8,128)S(1)}, s32[1024,16]{0,1:T(8,128)}, u32[]{:S(2)}) copy-start(s32[1024,16]{0,1:T(8,128)} %param.19) | copy-start | bytes 196612
  3.9 9.9 %copy-start.2 = (f32[3,32]{1,0:T(4,128)S(1)}, f32[3,32]{1,0:T(4,128)}, u32[]{:S(2)}) copy-start(f32[3,32]{1,0:T(4,128)} %dcv.1) | copy-start | bytes 1156
  3.9 9.9 %copy-start.3 = (s32[1024]{0:T(1024)S(1)}, s32[1024]{0:T(1024)}, u32[]{:S(2)}) copy-start(s32[1024]{0:T(1024)} %param.17) | copy-start | bytes 12292
  3.9 9.9 %copy-start.4 = (f32[32]{0:T(128)S(1)}, f32[32]{0:T(128)}, u32[]{:S(2)}) copy-start(f32[32]{0:T(128)} %param.12) | copy-start | bytes 388
  3.9 9.9 %copy-start.5 = (f32[32]{0:T(128)S(1)}, f32[32]{0:T(128)}, u32[]{:S(2)}) copy-start(f32[32]{0:T(128)} %param.13) | copy-start | bytes 388
  4.0 9.9 %copy-start.6 = (f32[32]{0:T(128)S(1)}, f32[32]{0:T(128)}, u32[]{:S(2)}) copy-start(f32[32]{0:T(128)} %param.14) | copy-start | bytes 388
  4.0 9.9 %copy-start.7 = (f32[32]{0:T(128)S(1)}, f32[32]{0:T(128)}, u32[]{:S(2)}) copy-start(f32[32]{0:T(128)} %param.15) | copy-start | bytes 388
  4.0 11.6 %collective-permute-start.1 = (f32[2,552,128]{2,1,0:T(8,128)S(1)}, f32[2,552,128]{2,1,0:T(8,128)S(1)}, u32[]{:S(2)}, u32[]{:S(2)}) collective-permute-start(f32[2,552,128]{2,1,0:T(8,128)S(1)} %get-tuple-element.35), channel_id=1, source_target_pairs={{16,32},{32,16},{48,64},{64,48},{80,96},{96,80},{17,33},{33,17},{4... | collective-permute-start | bytes 1695752 | tf_op jit(solution)/shard_map/ppermute | solution.py:530
  4.8 10.8 %collective-permute-start = (f32[2,552,128]{2,1,0:T(8,128)S(1)}, f32[2,552,128]{2,1,0:T(8,128)S(1)}, u32[]{:S(2)}, u32[]{:S(2)}) collective-permute-start(f32[2,552,128]{2,1,0:T(8,128)S(1)} %get-tuple-element.35), channel_id=1, source_target_pairs={{0,16},{16,0},{32,48},{48,32},{64,80},{80,64},{96,112},{112,96},{1... | collective-permute-start | bytes 1695752 | tf_op jit(solution)/shard_map/ppermute | solution.py:530

commit v5 on v4

--- a/solution.py
+++ b/solution.py
@@ -320,23 +320,25 @@
     for r in range(ROWS):
         tile, low_mode = (r % 8) * 128, 16 * (r // 8)
         for h in range(2):
-            at = pl.ds(h * 128, 128)
             part = e0_ref[h, pl.ds(r, 8, stride=ROWS), :]
             if r == 0:
                 part += jnp.where(up_x, extra[h], 0.0)
             if r == ROWS - 1:
                 part += jnp.where(up_x, 0.0, extra[h])
-            out[pl.ds(r * SEND, 8), at] = e_ref[h, pl.ds(r, 8, stride=ROWS), :]
-            out[pl.ds(r * SEND + 8, 8), at] = part
-            out[pl.ds(r * SEND + 16, 8), at] = slots[low_mode + 8 * h : low_mode + 8 * h + 8, tile : tile + 128]
+            out[r, h, 0:8, :] = e_ref[h, pl.ds(r, 8, stride=ROWS), :]
+            out[r, h, 8:16, :] = part
+            out[r, h, 16:24, :] = slots[low_mode + 8 * h : low_mode + 8 * h + 8, tile : tile + 128]
 
 
 def middle_kernel(got, par, jm_ref, k0_ref, mt_ref, out, q_ref):
-    energy = got[0, 0:8, :]
-    rest = got[0, 8:16, :]
+    def take(s, at):
+        return jnp.concatenate([got[s, h, at : at + 8, :] for h in range(2)], axis=1)
+
+    energy = take(0, 0)
+    rest = take(0, 8)
     for s in range(1, GROUP):
-        energy += got[s, 0:8, :]
-        rest += got[s, 8:16, :]
+        energy += take(s, 0)
+        rest += take(s, 8)
     energy = energy * (1.0 / PAIRS)
     equil = energy / (1.0 + 0.3 * jnp.abs(energy))
     eq = [jnp.broadcast_to(equil[z : z + 1, :], (8, COLS)) for z in range(Z)]
@@ -370,11 +372,12 @@
     acc = [jnp.zeros((8, COLS), F32) for _ in range(Z)]
     for k in range(GROUP):
         index = jnp.concatenate([jnp.broadcast_to(mt_ref[k : k + 1, :], (8, 128))] * 2, axis=1)
-        pick = got[0, 16:24, :]
+        pick = take(0, 16)
         for j in range(1, GROUP):
-            pick = jnp.where(index > j - 0.5, got[j, 16:24, :], pick)
+            pick = jnp.where(index > j - 0.5, take(j, 16), pick)
         pick = 0.9 * pick
-        out[k, 0:8, :] = pick
+        for h in range(2):
+            out[k, h, 0:8, :] = pick[:, h * 128 : h * 128 + 128]
         kp = jnp.concatenate(
             [jnp.broadcast_to(par[0, pl.ds(first + 8 * u, 8), pl.ds(0, 128)][:, 2 * k : 2 * k + 1], (8, 128)) for u in range(2)],
             axis=1,
@@ -385,26 +388,28 @@
             acc[z] += pick
     sums = [jnp.sum(t, axis=0, keepdims=True) for t in acc]
     at_slots = jnp.concatenate([t[:, 0:128] + t[:, 128:256] for t in sums], axis=0) * (1.0 / PAIRS)
-    at_slots = jnp.concatenate([at_slots, jnp.zeros((Z, 128), F32)], axis=1)
+    empty = jnp.zeros((Z, 128), F32)
     fresh = rest + bounce
     for z in range(Z):
         fresh += jnp.broadcast_to(k0_ref[:, z : z + 1], (8, COLS)) * eq[z]
     fresh = fresh * (1.0 / PAIRS)
     for k in range(GROUP):
-        out[k, 8:16, :] = equil
-        out[k, 16:24, :] = fresh
-        out[k, 24:32, :] = at_slots
+        for h in range(2):
+            out[k, h, 8:16, :] = equil[:, h * 128 : h * 128 + 128]
+            out[k, h, 16:24, :] = fresh[:, h * 128 : h * 128 + 128]
+            out[k, h, 24:32, :] = empty if h else at_slots
 
 
 def finish_kernel(
-    flags, tab, l0_ref, left, right, hot_ref, rm_ref, cz_ref, ksel, nsel, chip, next_chip,
-    out_hbm, en_ref, eq, res, cell, grid_en, sems,
+    flags, tab, l0_ref, back, hot_ref, rm_ref, cz_ref, ksel, nsel, chip, next_chip,
+    out_hbm, en_hbm, eq, res, cell, grid_en, en_ref, sems, en_sem,
 ):
     up_x, on_chip = flags[0] > 0.0, flags[4] > 0.5
     for z in range(Z):
-        for h, back in enumerate((left, right)):
+        for h in range(2):
             for b in range(2):
-                eq[pl.ds(z * ROWS + 8 * b, 8), pl.ds(h * 128, 128)] = back[pl.ds(8 * b * BACK + 8 + z, 8, stride=BACK), :]
+                got = back[pl.ds((16 * b + h) * BACK + 8 + z, 8, stride=2 * BACK), :]
+                eq[pl.ds(z * ROWS + 8 * b, 8), pl.ds(h * 128, 128)] = got
 
     def leave(g, d):
         part = pl.ds(g * STEP, STEP)
@@ -414,8 +419,8 @@
         first = 0 if pos_x else 8
         sub = lax.broadcasted_iota(jnp.int32, (8, 128), 0) == (0 if pos_x else 7)
 
-        def pair(i, carry):
-            modes = [2 * i, 2 * i + 1]
+        def some(g, carry):
+            modes = [STEP * g + n for n in range(STEP)]
             eta, beta, kappa = [
                 [jnp.broadcast_to(tab[n, pl.ds(m, 1), :], (8, 128)) for m in modes] for n in (ETA, BETA, KAPPA)
             ]
@@ -431,12 +436,12 @@
                             s += jnp.where(sub, beta[n] * jnp.broadcast_to(row, (8, 128)), 0.0)
                         return s
 
-                    t = [None, None]
+                    t = [None] * STEP
                     if d == 0:
                         rough = cz_ref[pl.ds(r, 8), pl.ds(h * 128, 128)] > 0.1
                         here = [pl.ds(pl.multiple_of(m * ROWS, ROWS) + r, 8) for m in modes]
                         kp = [ksel[h, to, :] for to in here]
-                        far = [e[Z - 1]] * 2
+                        far = [e[Z - 1]] * STEP
                         for z in reversed(range(Z - 1)):
                             far = [a * b + e[z] for a, b in zip(kp, far)]
                         for n, m in enumerate(modes):
@@ -446,10 +451,6 @@
                         for n, m in enumerate(modes):
                             t[n] = source(n, z) if t[n] is None else kappa[n] * t[n] + source(n, z)
                             res[(d, m) + at[z]] = l0_ref[(d, m) + at[z]] + t[n]
-            return carry
-
-        def some(g, carry):
-            lax.fori_loop(g * STEP // 2, g * STEP // 2 + STEP // 2, pair, 0)
             leave(g, d).start()
             return carry
 
@@ -462,27 +463,31 @@
 
     all_modes(1)
     hot = hot_ref[...]
-    picked = [
-        jnp.concatenate([back[pl.ds((8 * half + t) * BACK, 8), :] for t in range(8)], axis=1)
-        for half in range(2) for back in (left, right)
-    ]
-    heard = jnp.concatenate(
-        [left[pl.ds(t * BACK + 24, 8), :] + left[pl.ds((8 + t) * BACK + 24, 8), :] for t in range(8)], axis=1
-    )
+    def tiles_of(half, h, at):
+        return [back[pl.ds(((8 * half + t) * 2 + h) * BACK + at, 8), :] for t in range(8)]
+
+    picked = [jnp.concatenate(tiles_of(half, h, 0), axis=1) for half in range(2) for h in range(2)]
+    heard = jnp.concatenate(tiles_of(0, 0, 24), axis=1) + jnp.concatenate(tiles_of(1, 0, 24), axis=1)
+    high, low = split(jnp.concatenate(picked + [heard, jnp.zeros((8, SLOTS), F32)], axis=0))
+    mask = rm_ref[...].astype(jnp.bfloat16)
+    dims = (((1,), (1,)), ((), ()))
     for part in range(4):
-        lhs = []
-        for r in range(4 * part, 4 * part + 4):
-            lhs += [rm_ref[r : r + 1, :] * t for t in picked + [heard]]
-        got = spread(jnp.concatenate(lhs, axis=0), hot)
+        got = 0.0
+        for value in (high, low):
+            lhs = jnp.concatenate([mask[r : r + 1, :] * value for r in range(4 * part, 4 * part + 4)], axis=0)
+            got += lax.dot_general(lhs, hot, dims, preferred_element_type=F32)
         for n, r in enumerate(range(4 * part, 4 * part + 4)):
-            for h, back in enumerate((left, right)):
-                cell[h, pl.ds(r * MODES, MODES), :] = got[40 * n : 40 * n + 32, h * 128 : h * 128 + 128]
-                grid_en[h, pl.ds(r * 8, 8), :] = got[40 * n + 32 : 40 * n + 40, h * 128 : h * 128 + 128] + back[pl.ds(r * BACK + 16, 8), :]
-    all_modes(0)
+            for h in range(2):
+                cell[h, pl.ds(r * MODES, MODES), :] = got[48 * n : 48 * n + 32, h * 128 : h * 128 + 128]
+                grid_en[h, pl.ds(r * 8, 8), :] = got[48 * n + 32 : 48 * n + 40, h * 128 : h * 128 + 128] + back[pl.ds((2 * r + h) * BACK + 16, 8), :]
     for z in range(Z):
         for h in range(2):
             for b in range(2):
                 en_ref[pl.ds(z * ROWS + 8 * b, 8), pl.ds(h * 128, 128)] = grid_en[h, pl.ds(8 * b * 8 + z, 8, stride=8), :]
+    energy_copy = pltpu.make_async_copy(en_ref, en_hbm, en_sem)
+    energy_copy.start()
+    all_modes(0)
+    energy_copy.wait()
     for g in range(MODES // STEP):
         for d in range(2):
             leave(g, d).wait()
@@ -565,41 +570,40 @@
         pack_kernel,
         in_specs=[smem] + [vmem] * 9,
         out_specs=vmem,
-        out_shape=pltpu.VMEM((ROWS * SEND, COLS), F32),
+        out_shape=pltpu.VMEM((GROUP, 2, SEND, 128), F32),
         compiler_params=pltpu.CompilerParams(vmem_limit_bytes=8 << 20),
         name="pack",
     )(flags, tab, energy, e0, at_slots, hot, rm, cz, edge_chip, edge_next)
-    got = lax.all_to_all(pack.reshape(GROUP, SEND, COLS), "mode", 0, 0, tiled=True)
+    got = lax.all_to_all(pack, "mode", 0, 0, tiled=True)
 
     reply = pl.pallas_call(
         middle_kernel,
         in_specs=[vmem] * 5,
         out_specs=vmem,
-        out_shape=pltpu.VMEM((GROUP, BACK, COLS), F32),
+        out_shape=pltpu.VMEM((GROUP, 2, BACK, 128), F32),
         scratch_shapes=[pltpu.VMEM((GROUP, MODES, COLS), F32)],
         compiler_params=pltpu.CompilerParams(vmem_limit_bytes=8 << 20),
         name="middle",
     )(got, par, jm, k0, mt)
-    back = lax.all_to_all(reply, "mode", 0, 0, tiled=True).reshape(GROUP * BACK, COLS)
+    back = lax.all_to_all(reply, "mode", 0, 0, tiled=True).reshape(GROUP * 2 * BACK, 128)
 
     fresh, energy_new = pl.pallas_call(
         finish_kernel,
-        grid=(1,),
-        in_specs=[smem, vmem, vmem]
-        + [pl.BlockSpec((GROUP * BACK, 128), lambda i, h=h: (0, h)) for h in range(2)]
-        + [vmem] * 7,
-        out_specs=[anywhere, vmem],
-        out_shape=[pltpu.HBM(field, F32), jax.ShapeDtypeStruct((PLANE, COLS), F32)],
+        in_specs=[smem] + [vmem] * 10,
+        out_specs=[anywhere, anywhere],
+        out_shape=[pltpu.HBM(field, F32), pltpu.HBM((PLANE, COLS), F32)],
         scratch_shapes=[
             pltpu.VMEM((PLANE, COLS), F32),
             pltpu.VMEM(field, F32),
             pltpu.VMEM((2, MODES * ROWS, 128), F32),
             pltpu.VMEM((2, PLANE, 128), F32),
+            pltpu.VMEM((PLANE, COLS), F32),
             pltpu.SemaphoreType.DMA((2, MODES // STEP)),
+            pltpu.SemaphoreType.DMA,
         ],
         compiler_params=pltpu.CompilerParams(vmem_limit_bytes=24 << 20),
         name="finish",
-    )(flags, tab, base, back, back, hot, rm, cz, ksel, nsel, edge_chip, edge_next)
+    )(flags, tab, base, back, hot, rm, cz, ksel, nsel, edge_chip, edge_next)
     return fresh.reshape(intensity.shape), energy_new.reshape(Z, ROWS, COLS)
 
 

time: 55.1 us -> 54.1 us (0.982)
  Pallas kernels: 17.7 us -> 16.7 us
    pallas_call x1, Pallas kernels: 5.9 us -> 4.92 us  [per_device(): pl.pallas_call(finish_kernel, in_specs=[smem] + [vmem] * 10, out_specs=[a...]
where the time goes in v5:
time: 54.1 us; the launch traced here: 53.9 us
  blocking collectives  31.7 us (59%)
  Pallas kernels  16.7 us (31%)
  starting transfers between devices  3.89 us (7%)
  between operations  1.46 us (3%)
    all_to_all x1, blocking collectives, per_device(): got = lax.all_to_all(pack, 'mode', 0, 0, tiled=True)  17.7 us
    all_to_all x1, blocking collectives, per_device(): lax.all_to_all(reply, 'mode', 0, 0, tiled=True)  14 us
    pallas_call x1, Pallas kernels, per_device(): pl.pallas_call(sweep_kernel, in_specs=[smem, vmem, anywhere, vmem, vmem],...  5.23 us
    pallas_call x1, Pallas kernels, per_device(): pl.pallas_call(finish_kernel, in_specs=[smem] + [vmem] * 10, out_specs=[a...  4.92 us
    ppermute x2, starting transfers between devices, per_device(): lax.ppermute(edge, 'space', p)  3.89 us
    pallas_call x1, Pallas kernels, per_device(): pl.pallas_call(edge_kernel, in_specs=[anywhere] * 6, out_specs=[vmem] * 3...  3.24 us
    pallas_call x1, Pallas kernels, per_device(): pl.pallas_call(slot_kernel, in_specs=[smem] * 2 + [vmem] * 10, out_specs=...  1.72 us
    pallas_call x1, Pallas kernels, per_device(): pl.pallas_call(middle_kernel, in_specs=[vmem] * 5, out_specs=vmem, out_sh...  1.35 us
  transfers between devices with their start and end apart: 2, of which 0 were waited for; matrix products, arithmetic and copies ran while one was open for 0% of the time, Pallas kernels for 13%

profile of v5, /device:TPU:0, one launch (start us, length us, event | category | flops | bytes accessed | tf_op | source)
XLA Modules:
  0.0 53.9 jit_solution(1789405127745410843)
XLA Ops:
  0.6 0.0 copy-start.1
  0.6 3.2 %edges.1 = (f32[2,512,8,128]{3,2,1,0:T(8,128)S(1)}, f32[2,552,128]{2,1,0:T(8,128)S(1)}, f32[6,32,128]{2,1,0:T(8,128)S(1)}, f32[5]{0:T(128)S(4)}) custom-call(f32[512,2,8,256]{3,2,1,0:T(8,128)} %bitcast.21, f32[3,32]{1,0:T(4,128)} %dcv.1, f32[1,32]{1,0:T(1,128)} %bitcast.13, f32[1,32]{1,0:T(1,128)} %bitcast.15, f32[1,32]{1,0:T(1,128)} %bitcast.17, ...), custom_call_target="tpu_custom_call" | custom-call | flops 4194304 | bytes 8388608 | tf_op jit(solution)/shard_map/edges/pallas_call | solution.py:509
  3.9 0.0 copy-start
  3.9 0.0 copy-start.2
  3.9 0.0 copy-start.3
  3.9 0.0 copy-start.4
  3.9 0.0 copy-start.5
  4.0 0.0 copy-start.6
  4.0 0.0 copy-start.7
  4.0 0.8 %collective-permute-start.1 = (f32[2,552,128]{2,1,0:T(8,128)S(1)}, f32[2,552,128]{2,1,0:T(8,128)S(1)}, u32[]{:S(2)}, u32[]{:S(2)}) collective-permute-start(f32[2,552,128]{2,1,0:T(8,128)S(1)} %get-tuple-element.35), channel_id=1, source_target_pairs={{16,32},{32,16},{48,64},{64,48},{80,96},{96,80},{17,33},{33,17},{4... | collective-permute-start | bytes 1695752 | tf_op jit(solution)/shard_map/ppermute | solution.py:535
  4.8 3.1 %collective-permute-start = (f32[2,552,128]{2,1,0:T(8,128)S(1)}, f32[2,552,128]{2,1,0:T(8,128)S(1)}, u32[]{:S(2)}, u32[]{:S(2)}) collective-permute-start(f32[2,552,128]{2,1,0:T(8,128)S(1)} %get-tuple-element.35), channel_id=1, source_target_pairs={{0,16},{16,0},{32,48},{48,32},{64,80},{80,64},{96,112},{112,96},{1... | collective-permute-start | bytes 1695752 | tf_op jit(solution)/shard_map/ppermute | solution.py:535
  8.5 0.0 copy-done.1
  8.5 5.2 %sweep.1 = (f32[2,32,128,256]{3,2,1,0:T(8,128)S(1)}, f32[2,128,128]{2,1,0:T(8,128)S(1)}, f32[2,128,128]{2,1,0:T(8,128)S(1)}, f32[2,512,128]{2,1,0:T(8,128)S(1)}) custom-call(f32[5]{0:T(128)S(4)} %get-tuple-element.23.flags, f32[6,32,128]{2,1,0:T(8,128)S(1)} %get-tuple-element.24.tab, f32[512,2,8,256]{3,2,1,0:T(8,128)} %bitcast.22, ...), custom_call_target="tpu_custom_call" | custom-call | flops 31457280 | bytes 16777216 | tf_op jit(solution)/shard_map/sweep/pallas_call | solution.py:537
  13.8 0.0 copy-done
  13.8 0.0 copy-done.2
  13.8 0.0 copy-done.3
  13.8 0.0 copy-done.4
  13.8 0.0 copy-done.5
  13.8 0.0 copy-done.6
  13.8 0.0 copy-done.7
  13.8 1.7 %slots.1 = (bf16[256,1024]{1,0:T(8,128)(2,1)S(1)}, f32[16,1024]{1,0:T(8,128)S(1)}, f32[3,32,128]{2,1,0:T(8,128)S(1)}, f32[16,256]{1,0:T(8,128)S(1)}, f32[8,128]{...) custom-call(s32[1]{0:T(128)S(6)} %copy.12.cnt, ...), custom_call_target="tpu_custom_call" | custom-call | flops 31457280 | bytes 8388608 | tf_op jit(solution)/shard_map/slots/pallas_call | solution.py:558
  15.6 0.0 collective-permute-done.1.next_chip
  15.6 0.0 collective-permute-done.chip
  15.6 0.3 pack.1
  15.9 17.7 %all_to_all.10.got = f32[16,2,24,128]{3,2,1,0:T(8,128)S(1)} all-to-all(f32[16,2,24,128]{3,2,1,0:T(8,128)S(1)} %pack.1), channel_id=1, replica_groups=mesh['space'=8,'mode'=16] {'mode'}, dimensions={0} | all-to-all | bytes 786432 | tf_op jit(solution)/shard_map/all_to_all | solution.py:577
  33.6 1.3 %middle.1 = f32[16,2,32,128]{3,2,1,0:T(8,128)S(1)} custom-call(f32[16,2,24,128]{3,2,1,0:T(8,128)S(1)} %all_to_all.10.got, f32[3,32,128]{2,1,0:T(8,128)S(1)} %get-tuple-element.36.par, f32[16,256]{1,0:T(8,128)S(1)} %get-tuple-element.37.jm_ref, f32[8,128]{1,0:T(8,128)S(1)} %get-tuple-element.38.k0_ref, f32[16,128]{1,0:T(8,128)S(1)} %get-tuple-element.39.mt_ref), custom_call_target="tpu_custom_call" | custom-call | tf_op jit(solution)/shard_map/middle/pallas_call | solution.py:579
  34.9 14.0 %all_to_all.11 = f32[16,2,32,128]{3,2,1,0:T(8,128)S(1)} all-to-all(f32[16,2,32,128]{3,2,1,0:T(8,128)S(1)} %middle.1), channel_id=1, replica_groups=mesh['space'=8,'mode'=16] {'mode'}, dimensions={0} | all-to-all | bytes 1048576 | tf_op jit(solution)/shard_map/all_to_all | solution.py:588
  48.9 4.9 %finish.1 = (f32[2,32,128,256]{3,2,1,0:T(8,128)}, f32[128,256]{1,0:T(8,128)}) custom-call(f32[5]{0:T(128)S(4)} %get-tuple-element.23.flags, f32[6,32,128]{2,1,0:T(8,128)S(1)} %get-tuple-element.24.tab, f32[2,32,128,256]{3,2,1,0:T(8,128)S(1)} %get-tuple-element.26.l0_ref, f32[1024,128]{1,0:T(8,128)S(1)} %bitcast.10, ...), custom_call_target="tpu_custom_call" | custom-call | tf_op jit(solution)/shard_map/finish/pallas_call | solution.py:590
Async XLA Ops:
  0.6 7.9 %copy-start.1 = (f32[16,256]{1,0:T(8,128)S(1)}, f32[16,256]{1,0:T(8,128)}, u32[]{:S(2)}) copy-start(f32[16,256]{1,0:T(8,128)} %heat.1) | copy-start | bytes 49156
  3.9 9.9 %copy-start = (s32[1024,16]{0,1:T(8,128)S(1)}, s32[1024,16]{0,1:T(8,128)}, u32[]{:S(2)}) copy-start(s32[1024,16]{0,1:T(8,128)} %param.19) | copy-start | bytes 196612
  3.9 9.9 %copy-start.2 = (f32[3,32]{1,0:T(4,128)S(1)}, f32[3,32]{1,0:T(4,128)}, u32[]{:S(2)}) copy-start(f32[3,32]{1,0:T(4,128)} %dcv.1) | copy-start | bytes 1156
  3.9 9.9 %copy-start.3 = (s32[1024]{0:T(1024)S(1)}, s32[1024]{0:T(1024)}, u32[]{:S(2)}) copy-start(s32[1024]{0:T(1024)} %param.17) | copy-start | bytes 12292
  3.9 9.9 %copy-start.4 = (f32[32]{0:T(128)S(1)}, f32[32]{0:T(128)}, u32[]{:S(2)}) copy-start(f32[32]{0:T(128)} %param.12) | copy-start | bytes 388
  3.9 9.9 %copy-start.5 = (f32[32]{0:T(128)S(1)}, f32[32]{0:T(128)}, u32[]{:S(2)}) copy-start(f32[32]{0:T(128)} %param.13) | copy-start | bytes 388
  4.0 9.9 %copy-start.6 = (f32[32]{0:T(128)S(1)}, f32[32]{0:T(128)}, u32[]{:S(2)}) copy-start(f32[32]{0:T(128)} %param.14) | copy-start | bytes 388
  4.0 9.9 %copy-start.7 = (f32[32]{0:T(128)S(1)}, f32[32]{0:T(128)}, u32[]{:S(2)}) copy-start(f32[32]{0:T(128)} %param.15) | copy-start | bytes 388
  4.0 11.6 %collective-permute-start.1 = (f32[2,552,128]{2,1,0:T(8,128)S(1)}, f32[2,552,128]{2,1,0:T(8,128)S(1)}, u32[]{:S(2)}, u32[]{:S(2)}) collective-permute-start(f32[2,552,128]{2,1,0:T(8,128)S(1)} %get-tuple-element.35), channel_id=1, source_target_pairs={{16,32},{32,16},{48,64},{64,48},{80,96},{96,80},{17,33},{33,17},{4... | collective-permute-start | bytes 1695752 | tf_op jit(solution)/shard_map/ppermute | solution.py:535
  4.8 10.8 %collective-permute-start = (f32[2,552,128]{2,1,0:T(8,128)S(1)}, f32[2,552,128]{2,1,0:T(8,128)S(1)}, u32[]{:S(2)}, u32[]{:S(2)}) collective-permute-start(f32[2,552,128]{2,1,0:T(8,128)S(1)} %get-tuple-element.35), channel_id=1, source_target_pairs={{0,16},{16,0},{32,48},{48,32},{64,80},{80,64},{96,112},{112,96},{1... | collective-permute-start | bytes 1695752 | tf_op jit(solution)/shard_map/ppermute | solution.py:535

commit v6 on v5

--- a/solution.py
+++ b/solution.py
@@ -122,8 +122,14 @@
             edge_ref[h, pl.ds(EDGE + z, 1), :] = jnp.sum(acc[h, pl.ds(8 * z, 8), :], axis=0, keepdims=True)
 
 
+def total(values):
+    while len(values) > 1:
+        values = [a + b for a, b in zip(values[::2], values[1::2])]
+    return values[0]
+
+
 def sweep_kernel(
-    flags, tab, x_hbm, far_ref, heat, l0_ref, e_ref, e0_ref, d0, near_ref, accd, accu, xsems,
+    flags, tab, x_hbm, far_ref, heat, l0_ref, e_ref, e0_ref, d0, near_ref, accd, accu, rawd, rawu, xsems,
 ):
     up_x, up_y = flags[0] > 0.0, flags[1] > 0.0
     half = jnp.where(up_x, 0, 1)
@@ -133,7 +139,8 @@
                 half_tiles(x_hbm, near_ref, xsems, half, c, h).start()
     accd[...] = jnp.zeros_like(accd)
     accu[...] = jnp.zeros_like(accu)
-    e_ref[...] = jnp.zeros_like(e_ref)
+    rawd[...] = jnp.zeros_like(rawd)
+    rawu[...] = jnp.zeros_like(rawu)
 
     def run(pos_x, pos_y):
         rows = (0, 8) if pos_x else (8, 0)
@@ -142,8 +149,8 @@
         sub = lax.broadcasted_iota(jnp.int32, (8, 128), 0) == (0 if pos_x else 7)
         lane = lax.broadcasted_iota(jnp.int32, (8, 128), 1) == (0 if pos_y else 127)
 
-        def pair(i, carry):
-            modes = [2 * i, 2 * i + 1]
+        def some(i, carry):
+            modes = [STEP * i + n for n in range(STEP)]
             coef = [[jnp.broadcast_to(tab[n, pl.ds(m, 1), :], (8, 128)) for n in range(4)] for m in modes]
 
             def rhs(d, t, z):
@@ -160,28 +167,27 @@
                         out.append(alpha * f[r][c] + beta * x + gamma * y)
                 return out, f[0] + f[1]
 
-            for d, acc, order in ((1, accd, range(Z - 1, -1, -1)), (0, accu, range(Z))):
+            for d, acc, raw, order in ((1, accd, rawd, range(Z - 1, -1, -1)), (0, accu, rawu, range(Z))):
                 if d == 1:
                     state = [
                         [jnp.broadcast_to(tab[4, pl.ds(m, 1), :], (8, 128)) * heat[pl.ds(r, 8), pl.ds(c * 128, 128)] for r, c in tiles]
                         for m in modes
                     ]
                 else:
-                    state = [None, None]
-                weight = flags[2 + d]
+                    state = [None] * STEP
                 for z in order:
                     sums = []
-                    for t in range(2):
-                        f, raw = rhs(d, t, z)
-                        sums.append(raw)
+                    for t in range(STEP):
+                        f, taken = rhs(d, t, z)
+                        sums.append(taken)
                         state[t] = f if state[t] is None else [a + coef[t][3] * b for a, b in zip(f, state[t])]
                         for v, (r, c) in zip(state[t], tiles):
                             l0_ref[d, modes[t], pl.ds(z * ROWS + r, 8), pl.ds(c * 128, 128)] = v
                     for n, (r, c) in enumerate(tiles):
-                        acc[c, pl.ds(z * ROWS + r, 8), :] += state[0][n] + state[1][n]
-                        e_ref[c, pl.ds(z * ROWS + r, 8), :] += weight * (sums[0][n] + sums[1][n])
+                        acc[c, pl.ds(z * ROWS + r, 8), :] += total([t[n] for t in state])
+                        raw[c, pl.ds(z * ROWS + r, 8), :] += total([t[n] for t in sums])
                 if d == 1:
-                    for t in range(2):
+                    for t in range(STEP):
                         for v, (r, c) in zip(state[t], tiles):
                             d0[c, pl.ds(pl.multiple_of(modes[t] * ROWS, ROWS) + r, 8), :] = v
             return carry
@@ -190,7 +196,7 @@
             for c in (4 + g, g):
                 for h in range(2):
                     half_tiles(x_hbm, near_ref, xsems, half, c, h).wait()
-            return lax.fori_loop(4 * g, 4 * g + 4, pair, carry)
+            return lax.fori_loop(2 * g, 2 * g + 2, some, carry)
 
         lax.fori_loop(0, 4, eight, 0)
 
@@ -199,6 +205,7 @@
             pl.when((up_x == pos_x) & (up_y == pos_y))(lambda px=pos_x, py=pos_y: run(px, py))
 
     e0_ref[...] = flags[3] * accd[...] + flags[2] * accu[...]
+    e_ref[...] = flags[3] * rawd[...] + flags[2] * rawu[...]
 
 
 def split(x):
@@ -285,17 +292,14 @@
                 ],
                 axis=0,
             )
-            high, low = split(x)
-            parts[0, pl.ds(r * MODES + 16 * t, 16), :] = high
-            parts[1, pl.ds(r * MODES + 16 * t, 16), :] = low
+            parts[pl.ds(r * MODES + 16 * t, 16), :] = x.astype(jnp.bfloat16)
     for n in range(SLOTS // 256):
         at = pl.ds(n * 256, 256)
-        got = jnp.dot(parts[0], hot_ref[:, at], preferred_element_type=F32)
-        got += jnp.dot(parts[1], hot_ref[:, at], preferred_element_type=F32)
-        total = rm[0:1, n * 256 : n * 256 + 256] * got[0:MODES]
+        got = jnp.dot(parts[...], hot_ref[:, at], preferred_element_type=F32)
+        mine = rm[0:1, n * 256 : n * 256 + 256] * got[0:MODES]
         for r in range(1, ROWS):
-            total += rm[r : r + 1, n * 256 : n * 256 + 256] * got[r * MODES : (r + 1) * MODES]
-        slot_ref[:, at] = total
+            mine += rm[r : r + 1, n * 256 : n * 256 + 256] * got[r * MODES : (r + 1) * MODES]
+        slot_ref[:, at] = mine
 
 
 def pack_kernel(flags, tab, e_ref, e0_ref, slot_ref, hot, rm, cz_ref, chip, next_chip, out):
@@ -468,18 +472,18 @@
 
     picked = [jnp.concatenate(tiles_of(half, h, 0), axis=1) for half in range(2) for h in range(2)]
     heard = jnp.concatenate(tiles_of(0, 0, 24), axis=1) + jnp.concatenate(tiles_of(1, 0, 24), axis=1)
-    high, low = split(jnp.concatenate(picked + [heard, jnp.zeros((8, SLOTS), F32)], axis=0))
+    heard_high = heard.astype(jnp.bfloat16).astype(F32)
+    value = jnp.concatenate(picked + [heard_high, heard - heard_high], axis=0).astype(jnp.bfloat16)
     mask = rm_ref[...].astype(jnp.bfloat16)
     dims = (((1,), (1,)), ((), ()))
     for part in range(4):
-        got = 0.0
-        for value in (high, low):
-            lhs = jnp.concatenate([mask[r : r + 1, :] * value for r in range(4 * part, 4 * part + 4)], axis=0)
-            got += lax.dot_general(lhs, hot, dims, preferred_element_type=F32)
+        lhs = jnp.concatenate([mask[r : r + 1, :] * value for r in range(4 * part, 4 * part + 4)], axis=0)
+        got = lax.dot_general(lhs, hot, dims, preferred_element_type=F32)
         for n, r in enumerate(range(4 * part, 4 * part + 4)):
             for h in range(2):
                 cell[h, pl.ds(r * MODES, MODES), :] = got[48 * n : 48 * n + 32, h * 128 : h * 128 + 128]
-                grid_en[h, pl.ds(r * 8, 8), :] = got[48 * n + 32 : 48 * n + 40, h * 128 : h * 128 + 128] + back[pl.ds((2 * r + h) * BACK + 16, 8), :]
+                both = got[48 * n + 32 : 48 * n + 40, h * 128 : h * 128 + 128] + got[48 * n + 40 : 48 * n + 48, h * 128 : h * 128 + 128]
+                grid_en[h, pl.ds(r * 8, 8), :] = both + back[pl.ds((2 * r + h) * BACK + 16, 8), :]
     for z in range(Z):
         for h in range(2):
             for b in range(2):
@@ -543,6 +547,8 @@
             pltpu.VMEM((2, 512, 8, 128), F32),
             pltpu.VMEM((2, PLANE, 128), F32),
             pltpu.VMEM((2, PLANE, 128), F32),
+            pltpu.VMEM((2, PLANE, 128), F32),
+            pltpu.VMEM((2, PLANE, 128), F32),
             pltpu.SemaphoreType.DMA((2, 8)),
         ],
         compiler_params=pltpu.CompilerParams(vmem_limit_bytes=12 << 20),
@@ -560,7 +566,7 @@
         in_specs=[smem] * 2 + [vmem] * 10,
         out_specs=[vmem] * len(tables),
         out_shape=[pltpu.VMEM(*t) for t in tables],
-        scratch_shapes=[pltpu.VMEM((2, MODES * ROWS, COLS), jnp.bfloat16)],
+        scratch_shapes=[pltpu.VMEM((MODES * ROWS, COLS), jnp.bfloat16)],
         compiler_params=pltpu.CompilerParams(vmem_limit_bytes=12 << 20),
         cost_estimate=pl.CostEstimate(flops=30 << 20, bytes_accessed=8 << 20, transcendentals=0),
         name="slots",

time: 54.1 us -> 53.1 us (0.982)
  Pallas kernels: 16.7 us -> 15.6 us
    pallas_call x1, Pallas kernels: 4.92 us -> 4.21 us  [per_device(): pl.pallas_call(finish_kernel, in_specs=[smem] + [vmem] * 10, out_specs=[a...]
  transfers between devices with their start and end apart: 2 -> 2, of which waited for: 0 -> 0; matrix products, arithmetic and copies ran while one was open for 0% -> 0% of each run, Pallas kernels for 13% -> 12%
where the time goes in v6:
time: 53.1 us; the launch traced here: 52.7 us
  blocking collectives  31.7 us (60%)
  Pallas kernels  15.6 us (29%)
  starting transfers between devices  3.89 us (7%)
  between operations  1.46 us (3%)
    all_to_all x1, blocking collectives, per_device(): got = lax.all_to_all(pack, 'mode', 0, 0, tiled=True)  17.7 us
    all_to_all x1, blocking collectives, per_device(): lax.all_to_all(reply, 'mode', 0, 0, tiled=True)  14 us
    pallas_call x1, Pallas kernels, per_device(): pl.pallas_call(sweep_kernel, in_specs=[smem, vmem, anywhere, vmem, vmem],...  5.18 us
    pallas_call x1, Pallas kernels, per_device(): pl.pallas_call(finish_kernel, in_specs=[smem] + [vmem] * 10, out_specs=[a...  4.21 us
    ppermute x2, starting transfers between devices, per_device(): lax.ppermute(edge, 'space', p)  3.89 us
    pallas_call x1, Pallas kernels, per_device(): pl.pallas_call(edge_kernel, in_specs=[anywhere] * 6, out_specs=[vmem] * 3...  3.24 us
    pallas_call x1, Pallas kernels, per_device(): pl.pallas_call(slot_kernel, in_specs=[smem] * 2 + [vmem] * 10, out_specs=...  1.35 us
    pallas_call x1, Pallas kernels, per_device(): pl.pallas_call(middle_kernel, in_specs=[vmem] * 5, out_specs=vmem, out_sh...  1.35 us
  transfers between devices with their start and end apart: 2, of which 0 were waited for; matrix products, arithmetic and copies ran while one was open for 0% of the time, Pallas kernels for 12%

profile of v6, /device:TPU:0, one launch (start us, length us, event | category | flops | bytes accessed | tf_op | source)
XLA Modules:
  0.0 52.7 jit_solution(10252102554064581638)
XLA Ops:
  0.6 0.0 copy-start.1
  0.6 3.2 %edges.1 = (f32[2,512,8,128]{3,2,1,0:T(8,128)S(1)}, f32[2,552,128]{2,1,0:T(8,128)S(1)}, f32[6,32,128]{2,1,0:T(8,128)S(1)}, f32[5]{0:T(128)S(4)}) custom-call(f32[512,2,8,256]{3,2,1,0:T(8,128)} %bitcast.21, f32[3,32]{1,0:T(4,128)} %dcv.1, f32[1,32]{1,0:T(1,128)} %bitcast.13, f32[1,32]{1,0:T(1,128)} %bitcast.15, f32[1,32]{1,0:T(1,128)} %bitcast.17, ...), custom_call_target="tpu_custom_call" | custom-call | flops 4194304 | bytes 8388608 | tf_op jit(solution)/shard_map/edges/pallas_call | solution.py:513
  3.9 0.0 copy-start
  3.9 0.0 copy-start.2
  3.9 0.0 copy-start.3
  3.9 0.0 copy-start.4
  3.9 0.0 copy-start.5
  4.0 0.0 copy-start.6
  4.0 0.0 copy-start.7
  4.0 0.8 %collective-permute-start.1 = (f32[2,552,128]{2,1,0:T(8,128)S(1)}, f32[2,552,128]{2,1,0:T(8,128)S(1)}, u32[]{:S(2)}, u32[]{:S(2)}) collective-permute-start(f32[2,552,128]{2,1,0:T(8,128)S(1)} %get-tuple-element.35), channel_id=1, source_target_pairs={{16,32},{32,16},{48,64},{64,48},{80,96},{96,80},{17,33},{33,17},{4... | collective-permute-start | bytes 1695752 | tf_op jit(solution)/shard_map/ppermute | solution.py:539
  4.8 3.1 %collective-permute-start = (f32[2,552,128]{2,1,0:T(8,128)S(1)}, f32[2,552,128]{2,1,0:T(8,128)S(1)}, u32[]{:S(2)}, u32[]{:S(2)}) collective-permute-start(f32[2,552,128]{2,1,0:T(8,128)S(1)} %get-tuple-element.35), channel_id=1, source_target_pairs={{0,16},{16,0},{32,48},{48,32},{64,80},{80,64},{96,112},{112,96},{1... | collective-permute-start | bytes 1695752 | tf_op jit(solution)/shard_map/ppermute | solution.py:539
  8.5 0.0 copy-done.1
  8.5 5.2 %sweep.1 = (f32[2,32,128,256]{3,2,1,0:T(8,128)S(1)}, f32[2,128,128]{2,1,0:T(8,128)S(1)}, f32[2,128,128]{2,1,0:T(8,128)S(1)}, f32[2,512,128]{2,1,0:T(8,128)S(1)}) custom-call(f32[5]{0:T(128)S(4)} %get-tuple-element.23.flags, f32[6,32,128]{2,1,0:T(8,128)S(1)} %get-tuple-element.24.tab, f32[512,2,8,256]{3,2,1,0:T(8,128)} %bitcast.22, ...), custom_call_target="tpu_custom_call" | custom-call | flops 31457280 | bytes 16777216 | tf_op jit(solution)/shard_map/sweep/pallas_call | solution.py:541
  13.7 0.0 copy-done
  13.7 0.0 copy-done.2
  13.7 0.0 copy-done.3
  13.8 0.0 copy-done.4
  13.8 0.0 copy-done.5
  13.8 0.0 copy-done.6
  13.8 0.0 copy-done.7
  13.8 1.4 %slots.1 = (bf16[256,1024]{1,0:T(8,128)(2,1)S(1)}, f32[16,1024]{1,0:T(8,128)S(1)}, f32[3,32,128]{2,1,0:T(8,128)S(1)}, f32[16,256]{1,0:T(8,128)S(1)}, f32[8,128]{...) custom-call(s32[1]{0:T(128)S(6)} %copy.12.cnt, ...), custom_call_target="tpu_custom_call" | custom-call | flops 31457280 | bytes 8388608 | tf_op jit(solution)/shard_map/slots/pallas_call | solution.py:564
  15.2 0.0 collective-permute-done.1.next_chip
  15.2 0.0 collective-permute-done.chip
  15.2 0.3 pack.1
  15.4 17.7 %all_to_all.10.got = f32[16,2,24,128]{3,2,1,0:T(8,128)S(1)} all-to-all(f32[16,2,24,128]{3,2,1,0:T(8,128)S(1)} %pack.1), channel_id=1, replica_groups=mesh['space'=8,'mode'=16] {'mode'}, dimensions={0} | all-to-all | bytes 786432 | tf_op jit(solution)/shard_map/all_to_all | solution.py:583
  33.1 1.3 %middle.1 = f32[16,2,32,128]{3,2,1,0:T(8,128)S(1)} custom-call(f32[16,2,24,128]{3,2,1,0:T(8,128)S(1)} %all_to_all.10.got, f32[3,32,128]{2,1,0:T(8,128)S(1)} %get-tuple-element.36.par, f32[16,256]{1,0:T(8,128)S(1)} %get-tuple-element.37.jm_ref, f32[8,128]{1,0:T(8,128)S(1)} %get-tuple-element.38.k0_ref, f32[16,128]{1,0:T(8,128)S(1)} %get-tuple-element.39.mt_ref), custom_call_target="tpu_custom_call" | custom-call | tf_op jit(solution)/shard_map/middle/pallas_call | solution.py:585
  34.5 14.0 %all_to_all.11 = f32[16,2,32,128]{3,2,1,0:T(8,128)S(1)} all-to-all(f32[16,2,32,128]{3,2,1,0:T(8,128)S(1)} %middle.1), channel_id=1, replica_groups=mesh['space'=8,'mode'=16] {'mode'}, dimensions={0} | all-to-all | bytes 1048576 | tf_op jit(solution)/shard_map/all_to_all | solution.py:594
  48.5 4.2 %finish.1 = (f32[2,32,128,256]{3,2,1,0:T(8,128)}, f32[128,256]{1,0:T(8,128)}) custom-call(f32[5]{0:T(128)S(4)} %get-tuple-element.23.flags, f32[6,32,128]{2,1,0:T(8,128)S(1)} %get-tuple-element.24.tab, f32[2,32,128,256]{3,2,1,0:T(8,128)S(1)} %get-tuple-element.26.l0_ref, f32[1024,128]{1,0:T(8,128)S(1)} %bitcast.10, ...), custom_call_target="tpu_custom_call" | custom-call | tf_op jit(solution)/shard_map/finish/pallas_call | solution.py:596
Async XLA Ops:
  0.6 7.9 %copy-start.1 = (f32[16,256]{1,0:T(8,128)S(1)}, f32[16,256]{1,0:T(8,128)}, u32[]{:S(2)}) copy-start(f32[16,256]{1,0:T(8,128)} %heat.1) | copy-start | bytes 49156
  3.9 9.8 %copy-start = (s32[1024,16]{0,1:T(8,128)S(1)}, s32[1024,16]{0,1:T(8,128)}, u32[]{:S(2)}) copy-start(s32[1024,16]{0,1:T(8,128)} %param.19) | copy-start | bytes 196612
  3.9 9.8 %copy-start.2 = (f32[3,32]{1,0:T(4,128)S(1)}, f32[3,32]{1,0:T(4,128)}, u32[]{:S(2)}) copy-start(f32[3,32]{1,0:T(4,128)} %dcv.1) | copy-start | bytes 1156
  3.9 9.8 %copy-start.3 = (s32[1024]{0:T(1024)S(1)}, s32[1024]{0:T(1024)}, u32[]{:S(2)}) copy-start(s32[1024]{0:T(1024)} %param.17) | copy-start | bytes 12292
  3.9 9.8 %copy-start.4 = (f32[32]{0:T(128)S(1)}, f32[32]{0:T(128)}, u32[]{:S(2)}) copy-start(f32[32]{0:T(128)} %param.12) | copy-start | bytes 388
  3.9 9.8 %copy-start.5 = (f32[32]{0:T(128)S(1)}, f32[32]{0:T(128)}, u32[]{:S(2)}) copy-start(f32[32]{0:T(128)} %param.13) | copy-start | bytes 388
  4.0 9.8 %copy-start.6 = (f32[32]{0:T(128)S(1)}, f32[32]{0:T(128)}, u32[]{:S(2)}) copy-start(f32[32]{0:T(128)} %param.14) | copy-start | bytes 388
  4.0 9.8 %copy-start.7 = (f32[32]{0:T(128)S(1)}, f32[32]{0:T(128)}, u32[]{:S(2)}) copy-start(f32[32]{0:T(128)} %param.15) | copy-start | bytes 388
  4.0 11.2 %collective-permute-start.1 = (f32[2,552,128]{2,1,0:T(8,128)S(1)}, f32[2,552,128]{2,1,0:T(8,128)S(1)}, u32[]{:S(2)}, u32[]{:S(2)}) collective-permute-start(f32[2,552,128]{2,1,0:T(8,128)S(1)} %get-tuple-element.35), channel_id=1, source_target_pairs={{16,32},{32,16},{48,64},{64,48},{80,96},{96,80},{17,33},{33,17},{4... | collective-permute-start | bytes 1695752 | tf_op jit(solution)/shard_map/ppermute | solution.py:539
  4.8 10.4 %collective-permute-start = (f32[2,552,128]{2,1,0:T(8,128)S(1)}, f32[2,552,128]{2,1,0:T(8,128)S(1)}, u32[]{:S(2)}, u32[]{:S(2)}) collective-permute-start(f32[2,552,128]{2,1,0:T(8,128)S(1)} %get-tuple-element.35), channel_id=1, source_target_pairs={{0,16},{16,0},{32,48},{48,32},{64,80},{80,64},{96,112},{112,96},{1... | collective-permute-start | bytes 1695752 | tf_op jit(solution)/shard_map/ppermute | solution.py:539

commit v7 on v6

--- a/solution.py
+++ b/solution.py
@@ -14,7 +14,7 @@
 GROUP = 16
 PLANE = Z * ROWS
 SEND = 24
-BACK = 32
+BACK = 7
 SLOTS = 1024
 STEP = 4
 F32 = jnp.float32
@@ -381,7 +381,7 @@
             pick = jnp.where(index > j - 0.5, take(j, 16), pick)
         pick = 0.9 * pick
         for h in range(2):
-            out[k, h, 0:8, :] = pick[:, h * 128 : h * 128 + 128]
+            out[k, h] = pick[:, h * 128 : h * 128 + 128]
         kp = jnp.concatenate(
             [jnp.broadcast_to(par[0, pl.ds(first + 8 * u, 8), pl.ds(0, 128)][:, 2 * k : 2 * k + 1], (8, 128)) for u in range(2)],
             axis=1,
@@ -392,16 +392,15 @@
             acc[z] += pick
     sums = [jnp.sum(t, axis=0, keepdims=True) for t in acc]
     at_slots = jnp.concatenate([t[:, 0:128] + t[:, 128:256] for t in sums], axis=0) * (1.0 / PAIRS)
-    empty = jnp.zeros((Z, 128), F32)
     fresh = rest + bounce
     for z in range(Z):
         fresh += jnp.broadcast_to(k0_ref[:, z : z + 1], (8, COLS)) * eq[z]
     fresh = fresh * (1.0 / PAIRS)
     for k in range(GROUP):
         for h in range(2):
-            out[k, h, 8:16, :] = equil[:, h * 128 : h * 128 + 128]
-            out[k, h, 16:24, :] = fresh[:, h * 128 : h * 128 + 128]
-            out[k, h, 24:32, :] = empty if h else at_slots
+            out[k, 2 + h] = equil[:, h * 128 : h * 128 + 128]
+            out[k, 4 + h] = fresh[:, h * 128 : h * 128 + 128]
+        out[k, 6] = at_slots
 
 
 def finish_kernel(
@@ -412,7 +411,7 @@
     for z in range(Z):
         for h in range(2):
             for b in range(2):
-                got = back[pl.ds((16 * b + h) * BACK + 8 + z, 8, stride=2 * BACK), :]
+                got = back[pl.ds((8 * b * BACK + 2 + h) * 8 + z, 8, stride=8 * BACK), :]
                 eq[pl.ds(z * ROWS + 8 * b, 8), pl.ds(h * 128, 128)] = got
 
     def leave(g, d):
@@ -467,11 +466,11 @@
 
     all_modes(1)
     hot = hot_ref[...]
-    def tiles_of(half, h, at):
-        return [back[pl.ds(((8 * half + t) * 2 + h) * BACK + at, 8), :] for t in range(8)]
-
-    picked = [jnp.concatenate(tiles_of(half, h, 0), axis=1) for half in range(2) for h in range(2)]
-    heard = jnp.concatenate(tiles_of(0, 0, 24), axis=1) + jnp.concatenate(tiles_of(1, 0, 24), axis=1)
+    def tiles_of(half, n):
+        return [back[pl.ds(((8 * half + t) * BACK + n) * 8, 8), :] for t in range(8)]
+
+    picked = [jnp.concatenate(tiles_of(half, h), axis=1) for half in range(2) for h in range(2)]
+    heard = jnp.concatenate(tiles_of(0, 6), axis=1) + jnp.concatenate(tiles_of(1, 6), axis=1)
     heard_high = heard.astype(jnp.bfloat16).astype(F32)
     value = jnp.concatenate(picked + [heard_high, heard - heard_high], axis=0).astype(jnp.bfloat16)
     mask = rm_ref[...].astype(jnp.bfloat16)
@@ -483,7 +482,7 @@
             for h in range(2):
                 cell[h, pl.ds(r * MODES, MODES), :] = got[48 * n : 48 * n + 32, h * 128 : h * 128 + 128]
                 both = got[48 * n + 32 : 48 * n + 40, h * 128 : h * 128 + 128] + got[48 * n + 40 : 48 * n + 48, h * 128 : h * 128 + 128]
-                grid_en[h, pl.ds(r * 8, 8), :] = both + back[pl.ds((2 * r + h) * BACK + 16, 8), :]
+                grid_en[h, pl.ds(r * 8, 8), :] = both + back[pl.ds((r * BACK + 4 + h) * 8, 8), :]
     for z in range(Z):
         for h in range(2):
             for b in range(2):
@@ -586,12 +585,12 @@
         middle_kernel,
         in_specs=[vmem] * 5,
         out_specs=vmem,
-        out_shape=pltpu.VMEM((GROUP, 2, BACK, 128), F32),
+        out_shape=pltpu.VMEM((GROUP, BACK, 8, 128), F32),
         scratch_shapes=[pltpu.VMEM((GROUP, MODES, COLS), F32)],
         compiler_params=pltpu.CompilerParams(vmem_limit_bytes=8 << 20),
         name="middle",
     )(got, par, jm, k0, mt)
-    back = lax.all_to_all(reply, "mode", 0, 0, tiled=True).reshape(GROUP * 2 * BACK, 128)
+    back = lax.all_to_all(reply, "mode", 0, 0, tiled=True).reshape(GROUP * BACK * 8, 128)
 
     fresh, energy_new = pl.pallas_call(
         finish_kernel,

time: 53.1 us -> 52.4 us (0.987)
  blocking collectives: 31.7 us -> 31 us
    all_to_all x1, blocking collectives: 14 us -> 13.3 us  [per_device(): lax.all_to_all(reply, 'mode', 0, 0, tiled=True)]
  transfers between devices with their start and end apart: 2 -> 2, of which waited for: 0 -> 0; matrix products, arithmetic and copies ran while one was open for 0% -> 0% of each run, Pallas kernels for 12% -> 13%
where the time goes in v7:
time: 52.4 us; the launch traced here: 52 us
  blocking collectives  31 us (59%)
  Pallas kernels  15.6 us (30%)
  starting transfers between devices  3.89 us (7%)
  between operations  1.46 us (3%)
    all_to_all x1, blocking collectives, per_device(): got = lax.all_to_all(pack, 'mode', 0, 0, tiled=True)  17.7 us
    all_to_all x1, blocking collectives, per_device(): lax.all_to_all(reply, 'mode', 0, 0, tiled=True)  13.3 us
    pallas_call x1, Pallas kernels, per_device(): pl.pallas_call(sweep_kernel, in_specs=[smem, vmem, anywhere, vmem, vmem],...  5.17 us
    pallas_call x1, Pallas kernels, per_device(): pl.pallas_call(finish_kernel, in_specs=[smem] + [vmem] * 10, out_specs=[a...  4.15 us
    ppermute x2, starting transfers between devices, per_device(): lax.ppermute(edge, 'space', p)  3.89 us
    pallas_call x1, Pallas kernels, per_device(): pl.pallas_call(edge_kernel, in_specs=[anywhere] * 6, out_specs=[vmem] * 3...  3.24 us
    pallas_call x1, Pallas kernels, per_device(): pl.pallas_call(middle_kernel, in_specs=[vmem] * 5, out_specs=vmem, out_sh...  1.37 us
    pallas_call x1, Pallas kernels, per_device(): pl.pallas_call(slot_kernel, in_specs=[smem] * 2 + [vmem] * 10, out_specs=...  1.35 us
  transfers between devices with their start and end apart: 2, of which 0 were waited for; matrix products, arithmetic and copies ran while one was open for 0% of the time, Pallas kernels for 13%

profile of v7, /device:TPU:0, one launch (start us, length us, event | category | flops | bytes accessed | tf_op | source)
XLA Modules:
  0.0 52.0 jit_solution(14521526429885916567)
XLA Ops:
  0.6 0.0 copy-start.1
  0.6 3.2 %edges.1 = (f32[2,512,8,128]{3,2,1,0:T(8,128)S(1)}, f32[2,552,128]{2,1,0:T(8,128)S(1)}, f32[6,32,128]{2,1,0:T(8,128)S(1)}, f32[5]{0:T(128)S(4)}) custom-call(f32[512,2,8,256]{3,2,1,0:T(8,128)} %bitcast.21, f32[3,32]{1,0:T(4,128)} %dcv.1, f32[1,32]{1,0:T(1,128)} %bitcast.13, f32[1,32]{1,0:T(1,128)} %bitcast.15, f32[1,32]{1,0:T(1,128)} %bitcast.17, ...), custom_call_target="tpu_custom_call" | custom-call | flops 4194304 | bytes 8388608 | tf_op jit(solution)/shard_map/edges/pallas_call | solution.py:512
  3.9 0.0 copy-start
  3.9 0.0 copy-start.2
  3.9 0.0 copy-start.3
  3.9 0.0 copy-start.4
  3.9 0.0 copy-start.5
  4.0 0.0 copy-start.6
  4.0 0.0 copy-start.7
  4.0 0.8 %collective-permute-start.1 = (f32[2,552,128]{2,1,0:T(8,128)S(1)}, f32[2,552,128]{2,1,0:T(8,128)S(1)}, u32[]{:S(2)}, u32[]{:S(2)}) collective-permute-start(f32[2,552,128]{2,1,0:T(8,128)S(1)} %get-tuple-element.35), channel_id=1, source_target_pairs={{16,32},{32,16},{48,64},{64,48},{80,96},{96,80},{17,33},{33,17},{4... | collective-permute-start | bytes 1695752 | tf_op jit(solution)/shard_map/ppermute | solution.py:538
  4.8 3.1 %collective-permute-start = (f32[2,552,128]{2,1,0:T(8,128)S(1)}, f32[2,552,128]{2,1,0:T(8,128)S(1)}, u32[]{:S(2)}, u32[]{:S(2)}) collective-permute-start(f32[2,552,128]{2,1,0:T(8,128)S(1)} %get-tuple-element.35), channel_id=1, source_target_pairs={{0,16},{16,0},{32,48},{48,32},{64,80},{80,64},{96,112},{112,96},{1... | collective-permute-start | bytes 1695752 | tf_op jit(solution)/shard_map/ppermute | solution.py:538
  8.5 0.0 copy-done.1
  8.5 5.2 %sweep.1 = (f32[2,32,128,256]{3,2,1,0:T(8,128)S(1)}, f32[2,128,128]{2,1,0:T(8,128)S(1)}, f32[2,128,128]{2,1,0:T(8,128)S(1)}, f32[2,512,128]{2,1,0:T(8,128)S(1)}) custom-call(f32[5]{0:T(128)S(4)} %get-tuple-element.23.flags, f32[6,32,128]{2,1,0:T(8,128)S(1)} %get-tuple-element.24.tab, f32[512,2,8,256]{3,2,1,0:T(8,128)} %bitcast.22, ...), custom_call_target="tpu_custom_call" | custom-call | flops 31457280 | bytes 16777216 | tf_op jit(solution)/shard_map/sweep/pallas_call | solution.py:540
  13.7 0.0 copy-done
  13.7 0.0 copy-done.2
  13.7 0.0 copy-done.3
  13.8 0.0 copy-done.4
  13.8 0.0 copy-done.5
  13.8 0.0 copy-done.6
  13.8 0.0 copy-done.7
  13.8 1.4 %slots.1 = (bf16[256,1024]{1,0:T(8,128)(2,1)S(1)}, f32[16,1024]{1,0:T(8,128)S(1)}, f32[3,32,128]{2,1,0:T(8,128)S(1)}, f32[16,256]{1,0:T(8,128)S(1)}, f32[8,128]{...) custom-call(s32[1]{0:T(128)S(6)} %copy.12.cnt, ...), custom_call_target="tpu_custom_call" | custom-call | flops 31457280 | bytes 8388608 | tf_op jit(solution)/shard_map/slots/pallas_call | solution.py:563
  15.2 0.0 collective-permute-done.1.next_chip
  15.2 0.0 collective-permute-done.chip
  15.2 0.3 pack.1
  15.4 17.7 %all_to_all.10.got = f32[16,2,24,128]{3,2,1,0:T(8,128)S(1)} all-to-all(f32[16,2,24,128]{3,2,1,0:T(8,128)S(1)} %pack.1), channel_id=1, replica_groups=mesh['space'=8,'mode'=16] {'mode'}, dimensions={0} | all-to-all | bytes 786432 | tf_op jit(solution)/shard_map/all_to_all | solution.py:582
  33.1 1.4 %middle.1 = f32[16,7,8,128]{3,2,1,0:T(8,128)S(1)} custom-call(f32[16,2,24,128]{3,2,1,0:T(8,128)S(1)} %all_to_all.10.got, f32[3,32,128]{2,1,0:T(8,128)S(1)} %get-tuple-element.36.par, f32[16,256]{1,0:T(8,128)S(1)} %get-tuple-element.37.jm_ref, f32[8,128]{1,0:T(8,128)S(1)} %get-tuple-element.38.k0_ref, f32[16,128]{1,0:T(8,128)S(1)} %get-tuple-element.39.mt_ref), custom_call_target="tpu_custom_call" | custom-call | tf_op jit(solution)/shard_map/middle/pallas_call | solution.py:584
  34.5 13.3 %all_to_all.11 = f32[16,7,8,128]{3,2,1,0:T(8,128)S(1)} all-to-all(f32[16,7,8,128]{3,2,1,0:T(8,128)S(1)} %middle.1), channel_id=1, replica_groups=mesh['space'=8,'mode'=16] {'mode'}, dimensions={0} | all-to-all | bytes 917504 | tf_op jit(solution)/shard_map/all_to_all | solution.py:593
  47.8 4.2 %finish.1 = (f32[2,32,128,256]{3,2,1,0:T(8,128)}, f32[128,256]{1,0:T(8,128)}) custom-call(f32[5]{0:T(128)S(4)} %get-tuple-element.23.flags, f32[6,32,128]{2,1,0:T(8,128)S(1)} %get-tuple-element.24.tab, f32[2,32,128,256]{3,2,1,0:T(8,128)S(1)} %get-tuple-element.26.l0_ref, f32[896,128]{1,0:T(8,128)S(1)} %bitcast.10, ...), custom_call_target="tpu_custom_call" | custom-call | tf_op jit(solution)/shard_map/finish/pallas_call | solution.py:595
Async XLA Ops:
  0.6 7.9 %copy-start.1 = (f32[16,256]{1,0:T(8,128)S(1)}, f32[16,256]{1,0:T(8,128)}, u32[]{:S(2)}) copy-start(f32[16,256]{1,0:T(8,128)} %heat.1) | copy-start | bytes 49156
  3.9 9.8 %copy-start = (s32[1024,16]{0,1:T(8,128)S(1)}, s32[1024,16]{0,1:T(8,128)}, u32[]{:S(2)}) copy-start(s32[1024,16]{0,1:T(8,128)} %param.19) | copy-start | bytes 196612
  3.9 9.8 %copy-start.2 = (f32[3,32]{1,0:T(4,128)S(1)}, f32[3,32]{1,0:T(4,128)}, u32[]{:S(2)}) copy-start(f32[3,32]{1,0:T(4,128)} %dcv.1) | copy-start | bytes 1156
  3.9 9.8 %copy-start.3 = (s32[1024]{0:T(1024)S(1)}, s32[1024]{0:T(1024)}, u32[]{:S(2)}) copy-start(s32[1024]{0:T(1024)} %param.17) | copy-start | bytes 12292
  3.9 9.8 %copy-start.4 = (f32[32]{0:T(128)S(1)}, f32[32]{0:T(128)}, u32[]{:S(2)}) copy-start(f32[32]{0:T(128)} %param.12) | copy-start | bytes 388
  3.9 9.8 %copy-start.5 = (f32[32]{0:T(128)S(1)}, f32[32]{0:T(128)}, u32[]{:S(2)}) copy-start(f32[32]{0:T(128)} %param.13) | copy-start | bytes 388
  4.0 9.8 %copy-start.6 = (f32[32]{0:T(128)S(1)}, f32[32]{0:T(128)}, u32[]{:S(2)}) copy-start(f32[32]{0:T(128)} %param.14) | copy-start | bytes 388
  4.0 9.8 %copy-start.7 = (f32[32]{0:T(128)S(1)}, f32[32]{0:T(128)}, u32[]{:S(2)}) copy-start(f32[32]{0:T(128)} %param.15) | copy-start | bytes 388
  4.0 11.2 %collective-permute-start.1 = (f32[2,552,128]{2,1,0:T(8,128)S(1)}, f32[2,552,128]{2,1,0:T(8,128)S(1)}, u32[]{:S(2)}, u32[]{:S(2)}) collective-permute-start(f32[2,552,128]{2,1,0:T(8,128)S(1)} %get-tuple-element.35), channel_id=1, source_target_pairs={{16,32},{32,16},{48,64},{64,48},{80,96},{96,80},{17,33},{33,17},{4... | collective-permute-start | bytes 1695752 | tf_op jit(solution)/shard_map/ppermute | solution.py:538
  4.8 10.4 %collective-permute-start = (f32[2,552,128]{2,1,0:T(8,128)S(1)}, f32[2,552,128]{2,1,0:T(8,128)S(1)}, u32[]{:S(2)}, u32[]{:S(2)}) collective-permute-start(f32[2,552,128]{2,1,0:T(8,128)S(1)} %get-tuple-element.35), channel_id=1, source_target_pairs={{0,16},{16,0},{32,48},{48,32},{64,80},{80,64},{96,112},{112,96},{1... | collective-permute-start | bytes 1695752 | tf_op jit(solution)/shard_map/ppermute | solution.py:538

commit v8 on v7

--- a/solution.py
+++ b/solution.py
@@ -168,6 +168,12 @@
                 return out, f[0] + f[1]
 
             for d, acc, raw, order in ((1, accd, rawd, range(Z - 1, -1, -1)), (0, accu, rawu, range(Z))):
+
+                @pl.when(i % 2 == 0)
+                def _(d=d):
+                    for h in range(2):
+                        half_tiles(x_hbm, near_ref, xsems, half, i // 2 + 4 * d, h).wait()
+
                 if d == 1:
                     state = [
                         [jnp.broadcast_to(tab[4, pl.ds(m, 1), :], (8, 128)) * heat[pl.ds(r, 8), pl.ds(c * 128, 128)] for r, c in tiles]
@@ -193,9 +199,6 @@
             return carry
 
         def eight(g, carry):
-            for c in (4 + g, g):
-                for h in range(2):
-                    half_tiles(x_hbm, near_ref, xsems, half, c, h).wait()
             return lax.fori_loop(2 * g, 2 * g + 2, some, carry)
 
         lax.fori_loop(0, 4, eight, 0)

time: 52.4 us -> 52.4 us (level)
  no operation moved by 1% of the time
where the time goes in v8:
time: 52.4 us; the launch traced here: 52.1 us
  blocking collectives  31 us (59%)
  Pallas kernels  15.7 us (30%)
  starting transfers between devices  3.89 us (7%)
  between operations  1.46 us (3%)
    all_to_all x1, blocking collectives, per_device(): got = lax.all_to_all(pack, 'mode', 0, 0, tiled=True)  17.6 us
    all_to_all x1, blocking collectives, per_device(): lax.all_to_all(reply, 'mode', 0, 0, tiled=True)  13.3 us
    pallas_call x1, Pallas kernels, per_device(): pl.pallas_call(sweep_kernel, in_specs=[smem, vmem, anywhere, vmem, vmem],...  5.3 us
    pallas_call x1, Pallas kernels, per_device(): pl.pallas_call(finish_kernel, in_specs=[smem] + [vmem] * 10, out_specs=[a...  4.21 us
    ppermute x2, starting transfers between devices, per_device(): lax.ppermute(edge, 'space', p)  3.89 us
    pallas_call x1, Pallas kernels, per_device(): pl.pallas_call(edge_kernel, in_specs=[anywhere] * 6, out_specs=[vmem] * 3...  3.24 us
    pallas_call x1, Pallas kernels, per_device(): pl.pallas_call(middle_kernel, in_specs=[vmem] * 5, out_specs=vmem, out_sh...  1.37 us
    pallas_call x1, Pallas kernels, per_device(): pl.pallas_call(slot_kernel, in_specs=[smem] * 2 + [vmem] * 10, out_specs=...  1.35 us
  transfers between devices with their start and end apart: 2, of which 0 were waited for; matrix products, arithmetic and copies ran while one was open for 0% of the time, Pallas kernels for 13%

profile of v8, /device:TPU:0, one launch (start us, length us, event | category | flops | bytes accessed | tf_op | source)
XLA Modules:
  0.0 52.1 jit_solution(3827248929803143296)
XLA Ops:
  0.6 0.0 copy-start.1
  0.6 3.2 %edges.1 = (f32[2,512,8,128]{3,2,1,0:T(8,128)S(1)}, f32[2,552,128]{2,1,0:T(8,128)S(1)}, f32[6,32,128]{2,1,0:T(8,128)S(1)}, f32[5]{0:T(128)S(4)}) custom-call(f32[512,2,8,256]{3,2,1,0:T(8,128)} %bitcast.21, f32[3,32]{1,0:T(4,128)} %dcv.1, f32[1,32]{1,0:T(1,128)} %bitcast.13, f32[1,32]{1,0:T(1,128)} %bitcast.15, f32[1,32]{1,0:T(1,128)} %bitcast.17, ...), custom_call_target="tpu_custom_call" | custom-call | flops 4194304 | bytes 8388608 | tf_op jit(solution)/shard_map/edges/pallas_call | solution.py:515
  3.9 0.0 copy-start
  3.9 0.0 copy-start.2
  3.9 0.0 copy-start.3
  3.9 0.0 copy-start.4
  3.9 0.0 copy-start.5
  4.0 0.0 copy-start.6
  4.0 0.0 copy-start.7
  4.0 0.8 %collective-permute-start.1 = (f32[2,552,128]{2,1,0:T(8,128)S(1)}, f32[2,552,128]{2,1,0:T(8,128)S(1)}, u32[]{:S(2)}, u32[]{:S(2)}) collective-permute-start(f32[2,552,128]{2,1,0:T(8,128)S(1)} %get-tuple-element.35), channel_id=1, source_target_pairs={{16,32},{32,16},{48,64},{64,48},{80,96},{96,80},{17,33},{33,17},{4... | collective-permute-start | bytes 1695752 | tf_op jit(solution)/shard_map/ppermute | solution.py:541
  4.8 3.1 %collective-permute-start = (f32[2,552,128]{2,1,0:T(8,128)S(1)}, f32[2,552,128]{2,1,0:T(8,128)S(1)}, u32[]{:S(2)}, u32[]{:S(2)}) collective-permute-start(f32[2,552,128]{2,1,0:T(8,128)S(1)} %get-tuple-element.35), channel_id=1, source_target_pairs={{0,16},{16,0},{32,48},{48,32},{64,80},{80,64},{96,112},{112,96},{1... | collective-permute-start | bytes 1695752 | tf_op jit(solution)/shard_map/ppermute | solution.py:541
  8.5 0.0 copy-done.1
  8.5 5.3 %sweep.1 = (f32[2,32,128,256]{3,2,1,0:T(8,128)S(1)}, f32[2,128,128]{2,1,0:T(8,128)S(1)}, f32[2,128,128]{2,1,0:T(8,128)S(1)}, f32[2,512,128]{2,1,0:T(8,128)S(1)}) custom-call(f32[5]{0:T(128)S(4)} %get-tuple-element.23.flags, f32[6,32,128]{2,1,0:T(8,128)S(1)} %get-tuple-element.24.tab, f32[512,2,8,256]{3,2,1,0:T(8,128)} %bitcast.22, ...), custom_call_target="tpu_custom_call" | custom-call | flops 31457280 | bytes 16777216 | tf_op jit(solution)/shard_map/sweep/pallas_call | solution.py:543
  13.8 0.0 copy-done
  13.9 0.0 copy-done.2
  13.9 0.0 copy-done.3
  13.9 0.0 copy-done.4
  13.9 0.0 copy-done.5
  13.9 0.0 copy-done.6
  13.9 0.0 copy-done.7
  13.9 1.4 %slots.1 = (bf16[256,1024]{1,0:T(8,128)(2,1)S(1)}, f32[16,1024]{1,0:T(8,128)S(1)}, f32[3,32,128]{2,1,0:T(8,128)S(1)}, f32[16,256]{1,0:T(8,128)S(1)}, f32[8,128]{...) custom-call(s32[1]{0:T(128)S(6)} %copy.12.cnt, ...), custom_call_target="tpu_custom_call" | custom-call | flops 31457280 | bytes 8388608 | tf_op jit(solution)/shard_map/slots/pallas_call | solution.py:566
  15.3 0.0 collective-permute-done.1.next_chip
  15.3 0.0 collective-permute-done.chip
  15.3 0.3 pack.1
  15.6 17.6 %all_to_all.10.got = f32[16,2,24,128]{3,2,1,0:T(8,128)S(1)} all-to-all(f32[16,2,24,128]{3,2,1,0:T(8,128)S(1)} %pack.1), channel_id=1, replica_groups=mesh['space'=8,'mode'=16] {'mode'}, dimensions={0} | all-to-all | bytes 786432 | tf_op jit(solution)/shard_map/all_to_all | solution.py:585
  33.2 1.4 %middle.1 = f32[16,7,8,128]{3,2,1,0:T(8,128)S(1)} custom-call(f32[16,2,24,128]{3,2,1,0:T(8,128)S(1)} %all_to_all.10.got, f32[3,32,128]{2,1,0:T(8,128)S(1)} %get-tuple-element.36.par, f32[16,256]{1,0:T(8,128)S(1)} %get-tuple-element.37.jm_ref, f32[8,128]{1,0:T(8,128)S(1)} %get-tuple-element.38.k0_ref, f32[16,128]{1,0:T(8,128)S(1)} %get-tuple-element.39.mt_ref), custom_call_target="tpu_custom_call" | custom-call | tf_op jit(solution)/shard_map/middle/pallas_call | solution.py:587
  34.6 13.3 %all_to_all.11 = f32[16,7,8,128]{3,2,1,0:T(8,128)S(1)} all-to-all(f32[16,7,8,128]{3,2,1,0:T(8,128)S(1)} %middle.1), channel_id=1, replica_groups=mesh['space'=8,'mode'=16] {'mode'}, dimensions={0} | all-to-all | bytes 917504 | tf_op jit(solution)/shard_map/all_to_all | solution.py:596
  47.9 4.2 %finish.1 = (f32[2,32,128,256]{3,2,1,0:T(8,128)}, f32[128,256]{1,0:T(8,128)}) custom-call(f32[5]{0:T(128)S(4)} %get-tuple-element.23.flags, f32[6,32,128]{2,1,0:T(8,128)S(1)} %get-tuple-element.24.tab, f32[2,32,128,256]{3,2,1,0:T(8,128)S(1)} %get-tuple-element.26.l0_ref, f32[896,128]{1,0:T(8,128)S(1)} %bitcast.10, ...), custom_call_target="tpu_custom_call" | custom-call | tf_op jit(solution)/shard_map/finish/pallas_call | solution.py:598
Async XLA Ops:
  0.6 7.9 %copy-start.1 = (f32[16,256]{1,0:T(8,128)S(1)}, f32[16,256]{1,0:T(8,128)}, u32[]{:S(2)}) copy-start(f32[16,256]{1,0:T(8,128)} %heat.1) | copy-start | bytes 49156
  3.9 10.0 %copy-start = (s32[1024,16]{0,1:T(8,128)S(1)}, s32[1024,16]{0,1:T(8,128)}, u32[]{:S(2)}) copy-start(s32[1024,16]{0,1:T(8,128)} %param.19) | copy-start | bytes 196612
  3.9 10.0 %copy-start.2 = (f32[3,32]{1,0:T(4,128)S(1)}, f32[3,32]{1,0:T(4,128)}, u32[]{:S(2)}) copy-start(f32[3,32]{1,0:T(4,128)} %dcv.1) | copy-start | bytes 1156
  3.9 10.0 %copy-start.3 = (s32[1024]{0:T(1024)S(1)}, s32[1024]{0:T(1024)}, u32[]{:S(2)}) copy-start(s32[1024]{0:T(1024)} %param.17) | copy-start | bytes 12292
  3.9 9.9 %copy-start.4 = (f32[32]{0:T(128)S(1)}, f32[32]{0:T(128)}, u32[]{:S(2)}) copy-start(f32[32]{0:T(128)} %param.12) | copy-start | bytes 388
  3.9 9.9 %copy-start.5 = (f32[32]{0:T(128)S(1)}, f32[32]{0:T(128)}, u32[]{:S(2)}) copy-start(f32[32]{0:T(128)} %param.13) | copy-start | bytes 388
  4.0 9.9 %copy-start.6 = (f32[32]{0:T(128)S(1)}, f32[32]{0:T(128)}, u32[]{:S(2)}) copy-start(f32[32]{0:T(128)} %param.14) | copy-start | bytes 388
  4.0 9.9 %copy-start.7 = (f32[32]{0:T(128)S(1)}, f32[32]{0:T(128)}, u32[]{:S(2)}) copy-start(f32[32]{0:T(128)} %param.15) | copy-start | bytes 388
  4.0 11.3 %collective-permute-start.1 = (f32[2,552,128]{2,1,0:T(8,128)S(1)}, f32[2,552,128]{2,1,0:T(8,128)S(1)}, u32[]{:S(2)}, u32[]{:S(2)}) collective-permute-start(f32[2,552,128]{2,1,0:T(8,128)S(1)} %get-tuple-element.35), channel_id=1, source_target_pairs={{16,32},{32,16},{48,64},{64,48},{80,96},{96,80},{17,33},{33,17},{4... | collective-permute-start | bytes 1695752 | tf_op jit(solution)/shard_map/ppermute | solution.py:541
  4.8 10.5 %collective-permute-start = (f32[2,552,128]{2,1,0:T(8,128)S(1)}, f32[2,552,128]{2,1,0:T(8,128)S(1)}, u32[]{:S(2)}, u32[]{:S(2)}) collective-permute-start(f32[2,552,128]{2,1,0:T(8,128)S(1)} %get-tuple-element.35), channel_id=1, source_target_pairs={{0,16},{16,0},{32,48},{48,32},{64,80},{80,64},{96,112},{112,96},{1... | collective-permute-start | bytes 1695752 | tf_op jit(solution)/shard_map/ppermute | solution.py:541
